TPU v7x, 32 devices: a whole 2x2x4 slice. The times are simulated.
32 devices in a mesh: groups: 2 (over y), dp: 16 (over z, x, core).
Axes of the slice: x: 2, y: 2, z: 4, core: 2. Of those that a mesh axis runs over, the one named last changes fastest.
Arguments:
- activations: bfloat16 [64, 2, 64, 4096], P(('groups', 'dp')), parts along dimension 0
- out_grads: bfloat16 [64, 2, 64, 4096], P(('groups', 'dp')), parts along dimension 0
- lengths: int32 [64, 2], P(('groups', 'dp')), parts along dimension 0, may hold values from 16 to 64, as said below
- proj_in: bfloat16 [8192, 64], P(('groups', 'dp')), parts along dimension 0, may hold values from -0.09375 to 0.09375
- proj_out: bfloat16 [8192, 64], P(('groups', 'dp')), parts along dimension 0, may hold values from -0.09375 to 0.09375
- eval_sketches: bfloat16 [128, 4096], P(('groups', 'dp')), parts along dimension 0, may hold values from -0.011962891 to 0.011962891
Outputs:
- scores: float32 [64, 64], P(('groups', 'dp')), parts along dimension 0
There are 2 independent parts, one for each index of `groups`. A program takes and returns all parts, laid end to end along the dimension named above; each array names one. Nothing has to cross between parts.
Inputs may be any that keep to these rules, and one draw needn't show every extreme that they name: `lengths`: some response has exactly 64 live tokens and some exactly 16.
All inputs are finite; a program needn't handle non-finite values.
Results may differ from a plain program's by a relative error of at most 0.0022.
The roundings to bfloat16 on the way count: a program that leaves them out, or rounds other values in their place, can miss the bound.
Values may be sent and summed in bfloat16 or wider, within the bound.
No kernel may reach another device: no remote copies, remote signals or barrier semaphores. Data moves between devices by JAX's collectives and lax.ppermute only.
A program may use at most 64 MiB of HBM per device.

v0:
```python
import jax
import jax.numpy as jnp
from jax import lax
from jax.sharding import PartitionSpec as P


def factor_solve(matrix_a, matrix_b, stack):
    width = matrix_a.shape[0]
    lower_a = jnp.linalg.cholesky(matrix_a)
    lower_b = jnp.linalg.cholesky(matrix_b)
    count_p = stack.shape[0]
    left = jax.scipy.linalg.cho_solve(
        (lower_a, True), stack.transpose(1, 0, 2).reshape(width, count_p * width)
    )
    left = left.reshape(width, count_p, width).transpose(2, 1, 0).reshape(width, count_p * width)
    right = jax.scipy.linalg.cho_solve((lower_b, True), left)
    return right.reshape(width, count_p, width).transpose(1, 2, 0)


def damped(cov):
    width = cov.shape[0]
    return cov + (0.1 * jnp.trace(cov) / width + 1e-06) * jnp.eye(width, dtype=jnp.float32)


def on_device(activations, out_grads, lengths, proj_in, proj_out, eval_sketches):
    local_pairs, _, seq_len, width_d = activations.shape
    rank = proj_in.shape[1]
    flat_in = activations.reshape(-1, width_d)
    flat_out = out_grads.reshape(-1, width_d)
    whole_in, whole_out = (
        lax.all_gather(proj_in, "dp", axis=0, tiled=True),
        lax.all_gather(proj_out, "dp", axis=0, tiled=True),
    )
    inner_acc = jnp.dot(flat_in, whole_in, preferred_element_type=jnp.float32)
    outer_acc = jnp.dot(flat_out, whole_out, preferred_element_type=jnp.float32)
    inner = inner_acc.astype(jnp.bfloat16).reshape(local_pairs, 2 * seq_len, rank)
    outer = outer_acc.astype(jnp.bfloat16).reshape(local_pairs, 2 * seq_len, rank)
    position = jnp.arange(seq_len, dtype=jnp.int32)
    live = (position[None, None, :] < lengths[:, :, None]).astype(jnp.float32)
    signs = jnp.array([1.0, -1.0], dtype=jnp.float32)
    weight = (live * signs[None, :, None]).reshape(local_pairs, 2 * seq_len).astype(jnp.bfloat16)
    live_mask = live.reshape(local_pairs, 2 * seq_len).astype(jnp.bfloat16)
    sketch = jnp.einsum(
        "pto,pti->poi", outer * weight[:, :, None], inner, preferred_element_type=jnp.float32
    )
    inner_rows = inner.reshape(-1, rank)
    outer_rows = outer.reshape(-1, rank)
    mask_rows = live_mask.reshape(-1, 1)
    contract = (((0,), (0,)), ((), ()))
    part_in = lax.dot_general(
        inner_rows * mask_rows, inner_rows, contract, preferred_element_type=jnp.float32
    )
    part_out = lax.dot_general(
        outer_rows * mask_rows, outer_rows, contract, preferred_element_type=jnp.float32
    )
    sum_in, sum_out, count = lax.psum((part_in, part_out, jnp.sum(live)), "dp")
    cov_in = sum_in / count
    cov_out = sum_out / count
    precond = (
        factor_solve(damped(cov_out), damped(cov_in), sketch)
        .astype(jnp.bfloat16)
        .reshape(local_pairs, rank * rank)
    )
    product_dims = (((1,), (1,)), ((), ()))
    every_eval = lax.all_gather(eval_sketches, "dp", axis=0, tiled=True)
    scores = lax.dot_general(precond, every_eval, product_dims, preferred_element_type=jnp.float32)
    return scores


def solution(mesh):
    in_specs = (
        P(("groups", "dp"), None, None, None),
        P(("groups", "dp"), None, None, None),
        P(("groups", "dp"), None),
        P(("groups", "dp"), None),
        P(("groups", "dp"), None),
        P(("groups", "dp"), None),
    )
    out_specs = P(("groups", "dp"), None)
    return jax.shard_map(
        on_device, mesh=mesh, in_specs=in_specs, out_specs=out_specs, check_vma=False
    )
```

profile of v0, /device:TPU:0, one launch (start us, length us, event | category | flops | bytes accessed | tf_op | source)
XLA Modules:
  0.0 160.4 jit_solution(7434856879744193846)
XLA Ops:
  0.0 0.0 copy-start
  0.0 0.0 copy-start.2
  0.0 1.5 fusion.21
  1.5 0.1 copy-done
  1.6 0.7 mul.55
  2.3 0.1 mul.56
  2.4 0.1 lt.46
  2.5 0.7 lt.49
  3.3 0.1 lt.54
  3.3 0.1 lt.50
  3.4 0.0 copy-start.1
  3.4 24.9 %all_gather.9 = bf16[4096,64]{0,1:T(8,128)(2,1)S(1)} all-gather(bf16[256,64]{0,1:T(8,128)(2,1)} %param.13), channel_id=1, replica_groups=mesh['groups'=2,'dp'=16] {'dp'}, dimensions={0}, use_global_device_ids=true | all-gather | bytes 557056 | tf_op jit(solution)/shard_map/all_gather | solution.py:31
  28.4 0.8 convolution_convert_fusion.1
  29.1 0.1 fusion.2
  29.3 0.0 copy-done.2
  29.3 18.9 %all_gather.10 = bf16[4096,64]{0,1:T(8,128)(2,1)S(1)} all-gather(bf16[256,64]{0,1:T(8,128)(2,1)S(1)} %copy-done.2), channel_id=1, replica_groups=mesh['groups'=2,'dp'=16] {'dp'}, dimensions={0}, use_global_device_ids=true | all-gather | bytes 557056 | tf_op jit(solution)/shard_map/all_gather | solution.py:32
  48.1 0.0 copy-done.1
  48.1 0.0 copy-start.3
  48.1 0.8 convolution_convert_fusion
  48.9 0.1 fusion
  49.0 0.1 convolution_bitcast_fusion
  49.2 0.1 copy.29
  49.2 0.1 reshape.96
  49.3 61.0 %all-reduce = (f32[64,64]{0,1:T(8,128)S(1)}, f32[]{:T(128)}, f32[64,64]{0,1:T(8,128)S(1)}) all-reduce(f32[64,64]{0,1:T(8,128)S(1)} %fusion, f32[]{:T(128)} %fusion.21, f32[64,64]{0,1:T(8,128)S(1)} %fusion.2), channel_id=1, replica_groups=mesh['groups'=2,'dp'=16] {'dp'}, use_global_device_ids=true, to_apply=%region_6.8 | all-reduce | flops 8193 | bytes 65544 | tf_op jit(solution)/shard_map/psum | solution.py:56
  110.3 1.3 select_reduce_fusion.3
  112.3 1.3 select_reduce_fusion.2
  114.4 0.7 select_add_fusion
  115.1 0.1 copy.26
  115.1 5.8 %cholesky.55 = f32[64,64]{1,0:T(8,128)S(1)} custom-call(f32[64,64]{1,0:T(8,128)S(1)} %fusion.13), custom_call_target="Cholesky" | custom-call | tf_op jit(solution)/shard_map/jit(cholesky)/cholesky | solution.py:9
  121.0 0.6 compare_reduce_fusion
  121.7 0.7 fusion.5
  122.3 4.9 %custom-call.8 = f32[1,64,64]{1,2,0:T(8,128)S(1)} custom-call(f32[1,64,64]{2,1,0:T(8,128)S(1)} %fusion.5), custom_call_target="InvertDiagBlocksLowerTriangular" | custom-call | tf_op jit(solution)/shard_map/jit(_cho_solve)/triangular_solve | solution.py:12
  127.2 0.3 fusion.11
  127.5 0.2 fusion.9
  127.7 0.1 reshape.97
  127.8 0.1 copy.30
  127.9 0.1 reshape.98
  128.0 0.1 copy.24
  128.1 5.8 %cholesky.44 = f32[64,64]{1,0:T(8,128)S(1)} custom-call(f32[64,64]{1,0:T(8,128)S(1)} %fusion.17), custom_call_target="Cholesky" | custom-call | tf_op jit(solution)/shard_map/jit(cholesky)/cholesky | solution.py:10
  133.9 0.6 compare_reduce_fusion.1
  134.6 0.7 fusion.4
  135.2 4.9 %custom-call.9 = f32[1,64,64]{1,2,0:T(8,128)S(1)} custom-call(f32[1,64,64]{2,1,0:T(8,128)S(1)} %fusion.4), custom_call_target="InvertDiagBlocksLowerTriangular" | custom-call | tf_op jit(solution)/shard_map/jit(_cho_solve)/triangular_solve | solution.py:16
  140.1 0.3 fusion.15
  140.4 0.2 convolution_convert_fusion.2
  140.6 0.1 copy.34
  140.7 0.1 reshape.99
  140.8 0.0 copy-done.3
  140.8 18.7 %all-gather = bf16[16,4,4096]{2,1,0:T(4,128)(2,1)S(1)} all-gather(bf16[1,4,4096]{2,1,0:T(4,128)(2,1)S(1)} %bitcast.63), channel_id=1, replica_groups=mesh['groups'=2,'dp'=16] {'dp'}, dimensions={0}, use_global_device_ids=true | all-gather | bytes 557056 | tf_op jit(solution)/shard_map/all_gather | solution.py:65
  159.5 0.1 reshape.101
  159.6 0.8 fusion.24
  (7 shorter events, 0.1 us)
Async XLA Ops:
  0.0 1.6 %copy-start = (bf16[2,2,64,4096]{3,2,1,0:T(8,128)(2,1)S(1)}, bf16[2,2,64,4096]{3,2,1,0:T(8,128)(2,1)}, u32[]{:S(2)}) copy-start(bf16[2,2,64,4096]{3,2,1,0:T(8,128)(2,1)} %param.10) | copy-start | bytes 6291460
  0.0 29.3 %copy-start.2 = (bf16[256,64]{0,1:T(8,128)(2,1)S(1)}, bf16[256,64]{0,1:T(8,128)(2,1)}, u32[]{:S(2)}) copy-start(bf16[256,64]{0,1:T(8,128)(2,1)} %param.14) | copy-start | bytes 98308
  3.4 44.7 %copy-start.1 = (bf16[2,2,64,4096]{3,2,1,0:T(8,128)(2,1)S(1)}, bf16[2,2,64,4096]{3,2,1,0:T(8,128)(2,1)}, u32[]{:S(2)}) copy-start(bf16[2,2,64,4096]{3,2,1,0:T(8,128)(2,1)} %param.11) | copy-start | bytes 6291460
  48.1 92.7 %copy-start.3 = (bf16[4,4096]{1,0:T(4,128)(2,1)S(1)}, bf16[4,4096]{1,0:T(4,128)(2,1)}, u32[]{:S(2)}) copy-start(bf16[4,4096]{1,0:T(4,128)(2,1)} %param.15) | copy-start | bytes 98308
where the time goes:
time: 161 us; the launch traced here: 160 us
  blocking collectives  123 us (76%)
  other arithmetic  29 us (18%)
  matrix products  3.56 us (2%)
  local copies, waits for them, and re-layouts  2.87 us (2%)
    psum x1, blocking collectives, on_device(): sum_in, sum_out, count = lax.psum((part_in, part_out, jnp.sum(live)), 'dp')  61 us
    all_gather x1, blocking collectives, on_device(): lax.all_gather(proj_in, 'dp', axis=0, tiled=True)  24.9 us
    all_gather x1, blocking collectives, on_device(): lax.all_gather(proj_out, 'dp', axis=0, tiled=True)  18.9 us
    all_gather x1, blocking collectives, on_device(): every_eval = lax.all_gather(eval_sketches, 'dp', axis=0, tiled=True)  18.7 us
    another operation x3, other arithmetic, factor_solve(): lower_b = jnp.linalg.cholesky(matrix_b)  6.52 us
    another operation x3, other arithmetic, factor_solve(): lower_a = jnp.linalg.cholesky(matrix_a)  6.52 us
    another operation x2, other arithmetic, factor_solve(): right = jax.scipy.linalg.cho_solve((lower_b, True), left)  5.55 us
    another operation x2, other arithmetic, factor_solve(): jax.scipy.linalg.cho_solve((lower_a, True), stack.transpose(1, 0, 2).resh...  5.55 us

commit v1 on v0

v1 whole, which is shorter than its diff:
```python
import functools

import jax
import jax.numpy as jnp
from jax import lax
from jax.experimental import pallas as pl
from jax.experimental.pallas import tpu as pltpu
from jax.sharding import PartitionSpec as P

F32 = jnp.float32
BF16 = jnp.bfloat16
LANES = 128
SUB = 8
VMEM = pltpu.VMEM
SMEM = pltpu.SMEM


def contract_last(a, b):
    return lax.dot_general(a, b, (((1,), (1,)), ((), ())), preferred_element_type=F32)


def contract_first(a, b):
    return lax.dot_general(a, b, (((0,), (0,)), ((), ())), preferred_element_type=F32)


def project_kernel(
    core_ref, lengths_ref, act_ref, grad_ref, own_ref, other_ref, keep_ref, send_ref, sketch_ref
):
    place, core = core_ref[0], core_ref[1]
    blocks, both_ranks, chunk = own_ref.shape
    rank = both_ranks // 2
    pairs, _ = lengths_ref.shape
    rows = act_ref.shape[0]
    seq = rows // (2 * pairs)

    def project(x_ref, first):
        total = jnp.zeros((rows, rank), F32)
        for g in range(blocks):
            for ref, at in ((own_ref, place), (other_ref, 1 - place)):
                start = pl.multiple_of((2 * g + at) * chunk, chunk)
                total += contract_last(
                    x_ref[:, pl.ds(start, chunk)], ref[g, first : first + rank, :]
                )
        return total

    token = lax.broadcasted_iota(jnp.int32, (seq, rank), 0)

    def masked(total):
        parts = []
        for s in range(2 * pairs):
            live = token < lengths_ref[s // 2, s % 2]
            parts.append(jnp.where(live, total[s * seq : (s + 1) * seq], 0.0))
        return parts

    inner_parts = masked(project(act_ref, 0))
    outer_parts = masked(project(grad_ref, rank))
    inner = jnp.concatenate(inner_parts, 0).astype(BF16)
    outer = jnp.concatenate(outer_parts, 0).astype(BF16)
    signed = jnp.concatenate(
        [-part if s % 2 else part for s, part in enumerate(outer_parts)], 0
    ).astype(BF16)
    sketches = []
    for p in range(pairs):
        own_rows = slice(2 * p * seq, 2 * (p + 1) * seq)
        sketches.append(contract_first(signed[own_rows], inner[own_rows]))
    sketch_ref[...] = jnp.concatenate(sketches, 1)

    count = lengths_ref[0, 0]
    for s in range(1, 2 * pairs):
        count += lengths_ref[s // 2, s % 2]
    half = rank // 2
    row = lax.broadcasted_iota(jnp.int32, (half, 2 * rank), 0)
    lane = lax.broadcasted_iota(jnp.int32, (half, 2 * rank), 1)
    slot = (row == 0) & (lane == rank)

    def packed(rows_of):
        cov = contract_first(rows_of, rows_of)
        wide = jnp.concatenate([cov[:half], cov[half:]], 1)
        return jnp.where(slot, count.astype(F32), wide)

    cov_in = packed(inner)
    cov_out = packed(outer)
    first_core = core == 0
    keep_ref[...] = jnp.where(first_core, cov_in, cov_out)
    send_ref[...] = jnp.where(first_core, cov_out, cov_in)


def gauss_jordan(tiles, width, group):
    count = len(tiles)
    sub = lax.broadcasted_iota(jnp.int32, tiles[0].shape, 0)
    shape = tiles[0].shape

    def spread_row(tile, j):
        return jnp.broadcast_to(tile[j : j + 1, :], shape)

    for start in range(0, width, group):
        columns = [
            [jnp.broadcast_to(tile[:, k : k + 1], shape) for tile in tiles]
            for k in range(start, start + group)
        ]
        for step in range(group):
            home, j = divmod(start + step, SUB)
            column = columns[step]
            inverse = 1.0 / spread_row(column[home], j)

            def eliminate(block):
                scaled = spread_row(block[home], j) * inverse
                result = [block[g] - column[g] * scaled for g in range(count)]
                result[home] = jnp.where(sub == j, scaled, result[home])
                return result

            for later in range(step + 1, group):
                columns[later] = eliminate(columns[later])
            tiles = eliminate(tiles)
    return tiles


def invert_kernel(blocks_ref, inverse_ref):
    _, half, wide = blocks_ref.shape
    rank = 2 * half
    total = jnp.sum(blocks_ref[...], axis=0)
    row = lax.broadcasted_iota(jnp.int32, (half, wide), 0)
    lane = lax.broadcasted_iota(jnp.int32, (half, wide), 1)
    slot = (row == 0) & (lane == rank)
    mirror = (row == 0) & (lane == half)
    diagonal = (lane == row) | (lane == row + rank + half)

    def pick(mask):
        return jnp.sum(jnp.where(mask, total, 0.0), axis=(0, 1), keepdims=True)

    count = pick(slot)
    damp = 0.1 * (pick(diagonal) / count) / rank + 1e-06
    total = jnp.where(slot, pick(mirror), total)
    matrix = total / count + jnp.where(diagonal, damp, 0.0)
    left = jnp.concatenate([matrix[:, :rank], matrix[:, rank:]], 0)
    row = lax.broadcasted_iota(jnp.int32, (rank, rank), 0)
    lane = lax.broadcasted_iota(jnp.int32, (rank, rank), 1)
    both = jnp.concatenate([left, jnp.where(row == lane, 1.0, 0.0)], 1)
    tiles = [both[g * SUB : (g + 1) * SUB] for g in range(rank // SUB)]
    tiles = gauss_jordan(tiles, rank, 4)
    inverse_ref[...] = jnp.concatenate([tile[:, rank:] for tile in tiles], 0)


def precond_kernel(core_ref, own_ref, other_ref, sketch_ref, precond_ref):
    first_core = core_ref[0] == 0
    own = own_ref[...]
    other = other_ref[...]
    inverse_in = jnp.where(first_core, own, other)
    inverse_out = jnp.where(first_core, other, own)
    rank = own.shape[0]
    left = jnp.dot(
        inverse_out, sketch_ref[...], precision=lax.Precision.HIGHEST, preferred_element_type=F32
    )
    for p in range(precond_ref.shape[0]):
        right = jnp.dot(
            left[:, p * rank : (p + 1) * rank],
            inverse_in,
            precision=lax.Precision.HIGHEST,
            preferred_element_type=F32,
        )
        precond_ref[p] = right.astype(BF16)


def whole(space=VMEM):
    return pl.BlockSpec(memory_space=space)


def on_device(devices, activations, out_grads, lengths, proj_in, proj_out, eval_sketches):
    pairs, _, seq, depth = activations.shape
    rank = proj_in.shape[1]
    chips = devices // 2
    same_core = [[2 * chip + core for chip in range(chips)] for core in range(2)]
    swap = [(d, d ^ 1) for d in range(devices)]
    place = lax.axis_index("dp")
    core = (place % 2).astype(jnp.int32).reshape(1)

    def to_all_chips(block):
        copies = jnp.broadcast_to(block[None], (chips,) + block.shape)
        return lax.all_to_all(copies, "dp", 0, 0, axis_index_groups=same_core)

    every_eval = lax.all_gather(eval_sketches, ("groups", "dp"), axis=0, tiled=True)
    evals = every_eval.shape[0] // lax.axis_size("groups")
    every_eval = lax.dynamic_slice_in_dim(every_eval, lax.axis_index("groups") * evals, evals, 0)

    mine = jnp.concatenate([proj_in, proj_out], 1).T
    own = to_all_chips(mine)
    other = lax.ppermute(own, "dp", swap)
    slot_core = core
    local = mine.shape[1]
    if local % LANES:
        stacked = jnp.where(place % 2 == 0, jnp.stack([own, other], 1), jnp.stack([other, own], 1))
        full = stacked.transpose(2, 0, 1, 3).reshape(2 * rank, depth)
        split = full.reshape(2 * rank, -1, 2, 2 * LANES).transpose(1, 2, 0, 3)
        own, other = split[:, 0], split[:, 1]
        slot_core = jnp.zeros((1,), jnp.int32)

    rows = 2 * pairs * seq
    half = rank // 2
    keep, send, sketch = pl.pallas_call(
        project_kernel,
        out_shape=(
            jax.ShapeDtypeStruct((half, 2 * rank), F32),
            jax.ShapeDtypeStruct((half, 2 * rank), F32),
            jax.ShapeDtypeStruct((rank, pairs * rank), F32),
        ),
        in_specs=[whole(SMEM), whole(SMEM)] + [whole()] * 4,
        out_specs=(whole(), whole(), whole()),
        name="project",
    )(
        jnp.concatenate([slot_core, core]),
        lengths,
        activations.reshape(rows, depth),
        out_grads.reshape(rows, depth),
        own,
        other,
    )
    chip_sum = keep + lax.ppermute(send, "dp", swap)
    blocks = to_all_chips(chip_sum)
    inverse = pl.pallas_call(
        invert_kernel,
        out_shape=jax.ShapeDtypeStruct((rank, rank), F32),
        in_specs=[whole()],
        out_specs=whole(),
        name="invert",
    )(blocks)
    other_inverse = lax.ppermute(inverse, "dp", swap)
    precond = pl.pallas_call(
        precond_kernel,
        out_shape=jax.ShapeDtypeStruct((pairs, rank, rank), BF16),
        in_specs=[whole(SMEM)] + [whole()] * 3,
        out_specs=whole(),
        name="precond",
    )(core, inverse, other_inverse, sketch)
    return contract_last(precond.reshape(pairs, rank * rank), every_eval)


def solution(mesh):
    in_specs = (
        P(("groups", "dp"), None, None, None),
        P(("groups", "dp"), None, None, None),
        P(("groups", "dp"), None),
        P(("groups", "dp"), None),
        P(("groups", "dp"), None),
        P(("groups", "dp"), None),
    )
    out_specs = P(("groups", "dp"), None)
    return jax.shard_map(
        functools.partial(on_device, mesh.shape["dp"]),
        mesh=mesh,
        in_specs=in_specs,
        out_specs=out_specs,
        check_vma=False,
    )
```

time: 161 us -> 76.9 us (0.48)
  blocking collectives: 123 us -> 33 us
  other arithmetic: 29 us -> 2.25 us
  between operations: 1.53 us -> 13.4 us
  waiting for transfers between devices: 0 us -> 11.8 us
  Pallas kernels: 0 us -> 11.3 us
  matrix products: 3.56 us -> 0.82 us
    all_gather x3 -> x0, blocking collectives: 62.5 us -> none  [the longest x1 24.9 us: on_device(): lax.all_gather(proj_in, 'dp', axis=0, tiled=True)]
    psum x1 -> x0, blocking collectives: 61 us -> none  [on_device(): sum_in, sum_out, count = lax.psum((part_in, part_out, jnp.sum(live)), 'dp')]
    all_to_all x0 -> x2, blocking collectives: none -> 33 us  [to_all_chips(): return lax.all_to_all(copies, 'dp', 0, 0, axis_index_groups=same_core)]
    another operation x10 -> x0, other arithmetic: 24.1 us -> none  [the longest x3 6.52 us: factor_solve(): lower_b = jnp.linalg.cholesky(matrix_b)]
    pallas_call x0 -> x3, Pallas kernels: none -> 11.3 us  [the longest x1 4.93 us: on_device(): pl.pallas_call(invert_kernel, out_shape=jax.ShapeDtypeStruct((rank, rank)...]
    all_gather x0 -> x1, waiting for transfers between devices: none -> 7.23 us  [on_device(): lax.all_gather(eval_sketches, ('groups', 'dp'), axis=0, tiled=True)]
    reduce_sum x3 -> x0, other arithmetic: 4.18 us -> none  [the longest x2 2.68 us: damped(): jnp.trace(cov)]
    ppermute x0 -> x3, waiting for transfers between devices: none -> 3.84 us  [the longest x1 1.42 us: on_device(): other_inverse = lax.ppermute(inverse, 'dp', swap)]
  transfers between devices with their start and end apart: 0 -> 4, of which waited for: 0 -> 4; matrix products, arithmetic and copies ran while one was open for 0% -> 4% of each run, Pallas kernels for 0% -> 15%
where the time goes in v1:
time: 76.9 us; the launch traced here: 76.4 us
  blocking collectives  33 us (43%)
  between operations  13.4 us (17%)
  waiting for transfers between devices  11.8 us (15%)
  Pallas kernels  11.3 us (15%)
  local copies, waits for them, and re-layouts  3.63 us (5%)
  other arithmetic  2.25 us (3%)
  matrix products  0.82 us (1%)
    all_to_all x2, blocking collectives, to_all_chips(): return lax.all_to_all(copies, 'dp', 0, 0, axis_index_groups=same_core)  33 us
    all_gather x1, waiting for transfers between devices, on_device(): lax.all_gather(eval_sketches, ('groups', 'dp'), axis=0, tiled=True)  7.23 us
    pallas_call x1, Pallas kernels, on_device(): pl.pallas_call(invert_kernel, out_shape=jax.ShapeDtypeStruct((rank, rank)...  4.93 us
    pallas_call x1, Pallas kernels, on_device(): pl.pallas_call(project_kernel, out_shape=(jax.ShapeDtypeStruct((half, 2 *...  4.61 us
    unnamed x7, local copies, waits for them, and re-layouts  2.73 us
    pallas_call x1, Pallas kernels, on_device(): pl.pallas_call(precond_kernel, out_shape=jax.ShapeDtypeStruct((pairs, ran...  1.78 us
  transfers between devices with their start and end apart: 4, of which 4 were waited for; matrix products, arithmetic and copies ran while one was open for 4% of the time, Pallas kernels for 15%

profile of v1, /device:TPU:0, one launch (start us, length us, event | category | flops | bytes accessed | tf_op | source)
XLA Modules:
  0.0 76.4 jit_solution(577714455623399379)
XLA Ops:
  6.5 0.0 all-gather.3.cloned.1.call-start
  6.5 0.7 all-gather.3.cloned.1.call-update
  7.3 0.8 %maximum_bitcast_fusion = bf16[128,256]{1,0:T(8,128)(2,1)S(1)} fusion(bf16[256,64]{0,1:T(8,128)(2,1)} %param.10, bf16[256,64]{0,1:T(8,128)(2,1)} %param.9), kind=kLoop, calls=%fused_computation.2 | loop fusion | flops 131072 | bytes 131072 | tf_op jit(solution)/shard_map/transpose | solution.py:185
  8.1 22.0 %all_to_all.10.own_ref = bf16[8,128,256]{2,1,0:T(8,128)(2,1)S(1)} all-to-all(bf16[8,128,256]{2,1,0:T(8,128)(2,1)S(1)} %broadcast_in_dim.4), channel_id=1, replica_groups={{0,2,4,6,8,10,12,14},{1,3,5,7,9,11,13,15},{16,18,20,22,24,26,28,30},{17..., dimensions={0} | all-to-all | bytes 1048576 | tf_op jit(solution)/shard_map/all_to_all | solution.py:179
  30.1 0.0 copy-start
  30.1 0.0 collective-permute-start
  30.1 0.7 pad_add_fusion.core_ref
  30.8 1.2 %collective-permute-done.other_ref = bf16[8,128,256]{2,1,0:T(8,128)(2,1)S(1)} collective-permute-done((bf16[8,128,256]{2,1,0:T(8,128)(2,1)S(1)}, bf16[8,128,256]{2,1,0:T(8,128)(2,1)S(1)}, u32[]{:S(2)}, u32[]{:S(2)}) %collective-permute-start) | collective-permute-done | bytes 524320 | tf_op jit(solution)/shard_map/ppermute | solution.py:187
  32.0 0.0 copy-start.1
  32.0 0.0 copy-done
  32.0 0.8 %copy-done.1 = bf16[8,128,256]{2,1,0:T(8,128)(2,1)} copy-done((bf16[8,128,256]{2,1,0:T(8,128)(2,1)}, bf16[8,128,256]{2,1,0:T(8,128)(2,1)S(1)}, u32[]{:S(2)}) %copy-start.1) | copy-done | bytes 524312
  32.8 4.6 %project.1 = (f32[32,128]{1,0:T(8,128)}, f32[32,128]{1,0:T(8,128)}, f32[64,128]{1,0:T(8,128)}) custom-call(s32[2]{0:T(128)} %pad_add_fusion.core_ref, s32[2,2]{1,0:T(2,128)} %lengths_ref.1, bf16[256,4096]{1,0:T(8,128)(2,1)} %bitcast.7, bf16[256,4096]{1,0:T(8,128)(2,1)} %bitcast.8, bf16[8,128,256]{2,1,0:T(8,128)(2,1)} %copy-done, bf16[8,128,256]{2,1,0:T(8,128)(2,1)} %copy-done.1), custom_call_target="tpu_custom_call" | custom-call | tf_op jit(solution)/shard_map/project/pallas_call | solution.py:199
  37.4 0.1 collective-permute-start.1
  37.5 1.3 %collective-permute-done.1 = f32[32,128]{1,0:T(8,128)S(1)} collective-permute-done((f32[32,128]{1,0:T(8,128)}, f32[32,128]{1,0:T(8,128)S(1)}, u32[]{:S(2)}, u32[]{:S(2)}) %collective-permute-start.1) | collective-permute-done | bytes 16416 | tf_op jit(solution)/shard_map/ppermute | solution.py:217
  38.8 0.7 add.11
  39.5 11.0 %all_to_all.11.blocks_ref = f32[8,32,128]{2,1,0:T(8,128)} all-to-all(f32[8,32,128]{2,1,0:T(8,128)S(1)} %broadcast_in_dim.5), channel_id=1, replica_groups={{0,2,4,6,8,10,12,14},{1,3,5,7,9,11,13,15},{16,18,20,22,24,26,28,30},{17..., dimensions={0} | all-to-all | bytes 262144 | tf_op jit(solution)/shard_map/all_to_all | solution.py:179
  50.5 4.9 %invert.1.own_ref = f32[64,64]{1,0:T(8,128)} custom-call(f32[8,32,128]{2,1,0:T(8,128)} %all_to_all.11.blocks_ref), custom_call_target="tpu_custom_call" | custom-call | tf_op jit(solution)/shard_map/invert/pallas_call | solution.py:219
  55.5 0.0 collective-permute-start.2
  55.5 1.4 %collective-permute-done.2.other_ref = f32[64,64]{1,0:T(8,128)S(1)} collective-permute-done((f32[64,64]{1,0:T(8,128)}, f32[64,64]{1,0:T(8,128)S(1)}, u32[]{:S(2)}, u32[]{:S(2)}) %collective-permute-start.2) | collective-permute-done | bytes 16416 | tf_op jit(solution)/shard_map/ppermute | solution.py:226
  56.9 0.0 copy-start.2
  56.9 0.6 copy-done.2
  57.5 1.8 %precond.1 = bf16[2,64,64]{2,1,0:T(8,128)(2,1)} custom-call(s32[1]{0:T(128)} %bitcast.core_ref, f32[64,64]{1,0:T(8,128)} %invert.1.own_ref, f32[64,64]{1,0:T(8,128)} %copy-done.2, f32[64,128]{1,0:T(8,128)} %get-tuple-element.10.sketch_ref), custom_call_target="tpu_custom_call" | custom-call | tf_op jit(solution)/shard_map/precond/pallas_call | solution.py:227
  59.3 0.9 %reshape.17 = bf16[2,4096]{1,0:T(2,128)(2,1)S(1)} reshape(bf16[2,64,64]{2,1,0:T(8,128)(2,1)} %precond.1) | data formatting | bytes 32768 | tf_op jit(solution)/shard_map/reshape | solution.py:234
  60.1 7.2 %all-gather.3.cloned.1.call-done = bf16[32,4,4096]{2,1,0:T(4,128)(2,1)} async-done(((bf16[1,4,4096]{2,1,0:T(4,128)(2,1)}), bf16[32,4,4096]{2,1,0:T(4,128)(2,1)}) %all-gather.3.cloned.1.call-update) | async-done | bytes 1048592 | tf_op jit(solution)/shard_map/all_gather | solution.py:181
  67.4 1.3 %reshape.19 = bf16[128,4096]{1,0:T(8,128)(2,1)S(1)} reshape(bf16[32,4,4096]{2,1,0:T(4,128)(2,1)} %all-gather.3.cloned.1.call-done) | data formatting | bytes 2097152
  68.7 0.8 %fusion = f32[2,64]{1,0:T(2,128)} fusion(bf16[2,4096]{1,0:T(2,128)(2,1)S(1)} %reshape.17, bf16[128,4096]{1,0:T(8,128)(2,1)S(1)} %reshape.19, s32[]{:T(128)S(6)} %select_n.11), kind=kOutput, calls=%fused_computation | convolution fusion | flops 1048576 | bytes 541188 | tf_op jit(solution)/shard_map/dot_general | solution.py:19
  (2 shorter events, 0.0 us)
Async XLA Ops:
  6.5 60.8 %all-gather.3.cloned.1.call-start = ((), (), s32[]{:S(2)}) async-start(), calls=%async_computation.2 | async-start | bytes 1081344 | tf_op jit(solution)/shard_map/all_gather | solution.py:181
  30.1 1.9 %copy-start = (bf16[8,128,256]{2,1,0:T(8,128)(2,1)}, bf16[8,128,256]{2,1,0:T(8,128)(2,1)S(1)}, u32[]{:S(2)}) copy-start(bf16[8,128,256]{2,1,0:T(8,128)(2,1)S(1)} %all_to_all.10.own_ref) | copy-start | bytes 1572868
  30.1 1.9 %collective-permute-start = (bf16[8,128,256]{2,1,0:T(8,128)(2,1)S(1)}, bf16[8,128,256]{2,1,0:T(8,128)(2,1)S(1)}, u32[]{:S(2)}, u32[]{:S(2)}) collective-permute-start(bf16[8,128,256]{2,1,0:T(8,128)(2,1)S(1)} %all_to_all.10.own_ref), channel_id=1, source_target_pairs={{0,1},{1,0},{2,3},{3,2},{4,5},{5,4},{6,7},{7,6},{8,9},{9,8},{10,11... | collective-permute-start | bytes 1572872 | tf_op jit(solution)/shard_map/ppermute | solution.py:187
  32.0 0.8 %copy-start.1 = (bf16[8,128,256]{2,1,0:T(8,128)(2,1)}, bf16[8,128,256]{2,1,0:T(8,128)(2,1)S(1)}, u32[]{:S(2)}) copy-start(bf16[8,128,256]{2,1,0:T(8,128)(2,1)S(1)} %collective-permute-done.other_ref) | copy-start | bytes 1572868
  37.4 1.4 %collective-permute-start.1 = (f32[32,128]{1,0:T(8,128)}, f32[32,128]{1,0:T(8,128)S(1)}, u32[]{:S(2)}, u32[]{:S(2)}) collective-permute-start(f32[32,128]{1,0:T(8,128)} %get-tuple-element.9), channel_id=1, source_target_pairs={{0,1},{1,0},{2,3},{3,2},{4,5},{5,4},{6,7},{7,6},{8,9},{9,8},{10,11... | collective-permute-start | bytes 49160 | tf_op jit(solution)/shard_map/ppermute | solution.py:217
  55.5 1.4 %collective-permute-start.2 = (f32[64,64]{1,0:T(8,128)}, f32[64,64]{1,0:T(8,128)S(1)}, u32[]{:S(2)}, u32[]{:S(2)}) collective-permute-start(f32[64,64]{1,0:T(8,128)} %invert.1.own_ref), channel_id=1, source_target_pairs={{0,1},{1,0},{2,3},{3,2},{4,5},{5,4},{6,7},{7,6},{8,9},{9,8},{10,11... | collective-permute-start | bytes 49160 | tf_op jit(solution)/shard_map/ppermute | solution.py:226
  56.9 0.6 copy-start.2
Sparse Core Ops, SparseCore 0:
  10.2 57.1 all-gather.2

commit v2 on v1

--- a/solution.py
+++ b/solution.py
@@ -161,6 +161,10 @@
         precond_ref[p] = right.astype(BF16)
 
 
+def params(mebibytes):
+    return pltpu.CompilerParams(vmem_limit_bytes=mebibytes * 2**20)
+
+
 def whole(space=VMEM):
     return pl.BlockSpec(memory_space=space)
 
@@ -178,9 +182,8 @@
         copies = jnp.broadcast_to(block[None], (chips,) + block.shape)
         return lax.all_to_all(copies, "dp", 0, 0, axis_index_groups=same_core)
 
-    every_eval = lax.all_gather(eval_sketches, ("groups", "dp"), axis=0, tiled=True)
-    evals = every_eval.shape[0] // lax.axis_size("groups")
-    every_eval = lax.dynamic_slice_in_dim(every_eval, lax.axis_index("groups") * evals, evals, 0)
+    own_evals = to_all_chips(eval_sketches)
+    other_evals = lax.ppermute(own_evals, "dp", swap)
 
     mine = jnp.concatenate([proj_in, proj_out], 1).T
     own = to_all_chips(mine)
@@ -205,6 +208,8 @@
         ),
         in_specs=[whole(SMEM), whole(SMEM)] + [whole()] * 4,
         out_specs=(whole(), whole(), whole()),
+        compiler_params=params(24),
+        cost_estimate=pl.CostEstimate(flops=4 * rows * depth * rank, bytes_accessed=6 * rows * depth, transcendentals=0),
         name="project",
     )(
         jnp.concatenate([slot_core, core]),
@@ -221,6 +226,8 @@
         out_shape=jax.ShapeDtypeStruct((rank, rank), F32),
         in_specs=[whole()],
         out_specs=whole(),
+        compiler_params=params(4),
+        cost_estimate=pl.CostEstimate(flops=10**9, bytes_accessed=2**24, transcendentals=0),
         name="invert",
     )(blocks)
     other_inverse = lax.ppermute(inverse, "dp", swap)
@@ -229,9 +236,11 @@
         out_shape=jax.ShapeDtypeStruct((pairs, rank, rank), BF16),
         in_specs=[whole(SMEM)] + [whole()] * 3,
         out_specs=whole(),
+        compiler_params=params(4),
         name="precond",
     )(core, inverse, other_inverse, sketch)
-    return contract_last(precond.reshape(pairs, rank * rank), every_eval)
+    in_order = jnp.where(place % 2 == 0, jnp.stack([own_evals, other_evals], 1), jnp.stack([other_evals, own_evals], 1))
+    return contract_last(precond.reshape(pairs, rank * rank), in_order.reshape(-1, rank * rank))
 
 
 def solution(mesh):

time: 76.9 us -> 55.3 us (0.72)
  between operations: 13.4 us -> 0.08 us
  blocking collectives: 33 us -> 21.6 us
  starting transfers between devices: 0.14 us -> 7.57 us
  Pallas kernels: 11.3 us -> 5.87 us
  waiting for transfers between devices: 11.8 us -> 13.5 us
  other arithmetic: 2.25 us -> 1.38 us
    all_to_all x0 -> x2, waiting for transfers between devices: none -> 12 us  [to_all_chips(): return lax.all_to_all(copies, 'dp', 0, 0, axis_index_groups=same_core)]
    all_to_all x2 -> x1, blocking collectives: 33 us -> 21.6 us  [to_all_chips(): return lax.all_to_all(copies, 'dp', 0, 0, axis_index_groups=same_core)]
    all_gather x1 -> x0, waiting for transfers between devices: 7.23 us -> none  [on_device(): lax.all_gather(eval_sketches, ('groups', 'dp'), axis=0, tiled=True)]
    all_to_all x0 -> x2, starting transfers between devices: none -> 7.14 us  [to_all_chips(): return lax.all_to_all(copies, 'dp', 0, 0, axis_index_groups=same_core)]
    pallas_call x1, Pallas kernels: 4.61 us -> 2.06 us  [on_device(): pl.pallas_call(project_kernel, out_shape=(jax.ShapeDtypeStruct((half, 2 *...]
    broadcast_in_dim x2 -> x3, local copies, waits for them, and re-layouts: 0.05 us -> 2.21 us  [to_all_chips(): copies = jnp.broadcast_to(block[None], (chips,) + block.shape)]
    pallas_call x1, Pallas kernels: 4.93 us -> 3.43 us  [on_device(): pl.pallas_call(invert_kernel, out_shape=jax.ShapeDtypeStruct((rank, rank)...]
    pallas_call x1, Pallas kernels: 1.78 us -> 0.38 us  [on_device(): pl.pallas_call(precond_kernel, out_shape=jax.ShapeDtypeStruct((pairs, ran...]
  transfers between devices with their start and end apart: 4 -> 6, of which waited for: 4 -> 4; matrix products, arithmetic and copies ran while one was open for 4% -> 4% of each run, Pallas kernels for 15% -> 10%
where the time goes in v2:
time: 55.3 us; the launch traced here: 54.8 us
  blocking collectives  21.6 us (39%)
  waiting for transfers between devices  13.5 us (24%)
  starting transfers between devices  7.57 us (14%)
  Pallas kernels  5.87 us (11%)
  local copies, waits for them, and re-layouts  4.04 us (7%)
  other arithmetic  1.38 us (2%)
  matrix products  0.82 us (1%)
    all_to_all x1, blocking collectives, to_all_chips(): return lax.all_to_all(copies, 'dp', 0, 0, axis_index_groups=same_core)  21.6 us
    all_to_all x2, waiting for transfers between devices, to_all_chips(): return lax.all_to_all(copies, 'dp', 0, 0, axis_index_groups=same_core)  12 us
    all_to_all x2, starting transfers between devices, to_all_chips(): return lax.all_to_all(copies, 'dp', 0, 0, axis_index_groups=same_core)  7.14 us
    pallas_call x1, Pallas kernels, on_device(): pl.pallas_call(invert_kernel, out_shape=jax.ShapeDtypeStruct((rank, rank)...  3.43 us
    broadcast_in_dim x3, local copies, waits for them, and re-layouts, to_all_chips(): copies = jnp.broadcast_to(block[None], (chips,) + block.shape)  2.21 us
    pallas_call x1, Pallas kernels, on_device(): pl.pallas_call(project_kernel, out_shape=(jax.ShapeDtypeStruct((half, 2 *...  2.06 us
    unnamed x6, local copies, waits for them, and re-layouts  1.59 us
  transfers between devices with their start and end apart: 6, of which 4 were waited for; matrix products, arithmetic and copies ran while one was open for 4% of the time, Pallas kernels for 10%

profile of v2, /device:TPU:0, one launch (start us, length us, event | category | flops | bytes accessed | tf_op | source)
XLA Modules:
  0.0 54.8 jit_solution(5764609397925354816)
XLA Ops:
  0.0 0.0 copy-start.2
  0.0 0.0 copy-start
  0.0 0.9 %maximum_bitcast_fusion = bf16[128,256]{1,0:T(8,128)(2,1)S(1)} fusion(bf16[256,64]{0,1:T(8,128)(2,1)} %param.10, bf16[256,64]{0,1:T(8,128)(2,1)} %param.9), kind=kLoop, calls=%fused_computation.1 | loop fusion | flops 131072 | bytes 131072 | tf_op jit(solution)/shard_map/transpose | solution.py:188
  1.0 21.6 %all_to_all.15.own_ref = bf16[8,128,256]{2,1,0:T(8,128)(2,1)S(1)} all-to-all(bf16[8,128,256]{2,1,0:T(8,128)(2,1)S(1)} %broadcast_in_dim.6), channel_id=1, replica_groups={{0,2,4,6,8,10,12,14},{1,3,5,7,9,11,13,15},{16,18,20,22,24,26,28,30},{17..., dimensions={0} | all-to-all | bytes 1048576 | tf_op jit(solution)/shard_map/all_to_all | solution.py:183
  22.6 0.0 collective-permute-start
  22.6 1.5 %broadcast_in_dim.8 = bf16[8,4,4096]{2,1,0:T(4,128)(2,1)} broadcast(bf16[4,4096]{1,0:T(4,128)(2,1)} %param.11), dimensions={1,2} | broadcast | bytes 294912 | tf_op jit(solution)/shard_map/broadcast_in_dim | solution.py:182
  24.1 3.6 %all-to-all-start.2 = ((bf16[8,4,4096]{2,1,0:T(4,128)(2,1)}), bf16[8,4,4096]{2,1,0:T(4,128)(2,1)S(1)}, u32[]{:S(2)}, u32[]{:S(2)}) async-start(bf16[8,4,4096]{2,1,0:T(4,128)(2,1)} %broadcast_in_dim.8), calls=%async_computation.2 | async-start | bytes 524288 | tf_op jit(solution)/shard_map/all_to_all | solution.py:183
  27.7 0.1 pad_add_fusion.core_ref
  27.8 0.0 collective-permute-done.other_ref
  27.8 0.0 copy-done.2
  27.8 0.0 copy-done
  27.8 0.0 copy-start.1
  27.8 1.6 %copy-done.1 = bf16[2,2,64,4096]{3,2,1,0:T(8,128)(2,1)S(1)} copy-done((bf16[2,2,64,4096]{3,2,1,0:T(8,128)(2,1)S(1)}, bf16[2,2,64,4096]{3,2,1,0:T(8,128)(2,1)}, u32[]{:S(2)}) %copy-start.1) | copy-done | bytes 2097176
  29.4 2.1 %project.1 = (f32[32,128]{1,0:T(8,128)S(1)}, f32[32,128]{1,0:T(8,128)S(1)}, f32[64,128]{1,0:T(8,128)S(1)}) custom-call(s32[2]{0:T(128)S(1)} %pad_add_fusion.core_ref, s32[2,2]{1,0:T(2,128)S(1)} %copy-done.2, bf16[256,4096]{1,0:T(8,128)(2,1)S(1)} %bitcast.9, bf16[256,4096]{1,0:T(8,128)(2,1)S(1)} %bitcast.10, bf16[8,128,256]{2,1,0:T(8,128)(2,1)S(1)} %all_to_all.15.own_ref, ...), custom_call_target="tpu_custom_call" | custom-call | flops 268435456 | bytes 6291456 | tf_op jit(solution)/shard_map/project/pallas_call | solution.py:202
  31.4 0.4 collective-permute-start.1
  31.9 0.8 %collective-permute-done.1 = f32[32,128]{1,0:T(8,128)S(1)} collective-permute-done((f32[32,128]{1,0:T(8,128)S(1)}, f32[32,128]{1,0:T(8,128)S(1)}, u32[]{:S(2)}, u32[]{:S(2)}) %collective-permute-start.1) | collective-permute-done | bytes 16416 | tf_op jit(solution)/shard_map/ppermute | solution.py:222
  32.7 4.6 %all-to-all-done.2 = bf16[8,4,4096]{2,1,0:T(4,128)(2,1)S(1)} async-done(((bf16[8,4,4096]{2,1,0:T(4,128)(2,1)}), bf16[8,4,4096]{2,1,0:T(4,128)(2,1)S(1)}, u32[]{:S(2)}, u32[]{:S(2)}) %all-to-all-start.2) | async-done | bytes 262176 | tf_op jit(solution)/shard_map/all_to_all | solution.py:183
  37.3 0.6 %broadcast_in_dim.7 = f32[8,32,128]{2,1,0:T(8,128)} broadcast(f32[32,128]{1,0:T(8,128)S(1)} %add.9), dimensions={1,2} | broadcast | bytes 147456 | tf_op jit(solution)/shard_map/broadcast_in_dim | solution.py:182
  38.0 3.6 %all-to-all-start.1 = ((f32[8,32,128]{2,1,0:T(8,128)}), f32[8,32,128]{2,1,0:T(8,128)S(1)}, u32[]{:S(2)}, u32[]{:S(2)}) async-start(f32[8,32,128]{2,1,0:T(8,128)} %broadcast_in_dim.7), calls=%async_computation.1 | async-start | bytes 262144 | tf_op jit(solution)/shard_map/all_to_all | solution.py:183
  41.5 0.0 collective-permute-start.3
  41.5 7.3 %all-to-all-done.1.blocks_ref = f32[8,32,128]{2,1,0:T(8,128)S(1)} async-done(((f32[8,32,128]{2,1,0:T(8,128)}), f32[8,32,128]{2,1,0:T(8,128)S(1)}, u32[]{:S(2)}, u32[]{:S(2)}) %all-to-all-start.1) | async-done | bytes 131104 | tf_op jit(solution)/shard_map/all_to_all | solution.py:183
  48.9 3.4 %invert.1.own_ref = f32[64,64]{1,0:T(8,128)S(1)} custom-call(f32[8,32,128]{2,1,0:T(8,128)S(1)} %all-to-all-done.1.blocks_ref), custom_call_target="tpu_custom_call" | custom-call | flops 1000000000 | bytes 16777216 | tf_op jit(solution)/shard_map/invert/pallas_call | solution.py:224
  52.3 0.0 collective-permute-start.2
  52.3 0.0 collective-permute-done.3
  52.3 0.4 maximum_select_fusion
  52.7 0.1 select_n.30
  52.8 0.7 %collective-permute-done.2.other_ref = f32[64,64]{1,0:T(8,128)S(1)} collective-permute-done((f32[64,64]{1,0:T(8,128)S(1)}, f32[64,64]{1,0:T(8,128)S(1)}, u32[]{:S(2)}, u32[]{:S(2)}) %collective-permute-start.2) | collective-permute-done | bytes 16416 | tf_op jit(solution)/shard_map/ppermute | solution.py:233
  53.5 0.4 precond.1
  53.9 0.1 reshape.31
  54.0 0.8 %fusion = f32[2,64]{1,0:T(2,128)} fusion(bf16[2,4096]{1,0:T(2,128)(2,1)S(1)} %reshape.31, bf16[64,4096]{1,0:T(8,128)(2,1)S(1)} %select_n.30), kind=kOutput, calls=%fused_computation.3 | convolution fusion | flops 1048576 | bytes 541184 | tf_op jit(solution)/shard_map/dot_general | solution.py:19
  (2 shorter events, 0.0 us)
Async XLA Ops:
  0.0 27.8 %copy-start.2 = (s32[2,2]{1,0:T(2,128)S(1)}, s32[2,2]{1,0:T(2,128)}, u32[]{:S(2)}) copy-start(s32[2,2]{1,0:T(2,128)} %lengths_ref.1) | copy-start | bytes 52
  0.0 27.8 %copy-start = (bf16[2,2,64,4096]{3,2,1,0:T(8,128)(2,1)S(1)}, bf16[2,2,64,4096]{3,2,1,0:T(8,128)(2,1)}, u32[]{:S(2)}) copy-start(bf16[2,2,64,4096]{3,2,1,0:T(8,128)(2,1)} %param.6) | copy-start | bytes 6291460
  22.6 5.2 %collective-permute-start = (bf16[8,128,256]{2,1,0:T(8,128)(2,1)S(1)}, bf16[8,128,256]{2,1,0:T(8,128)(2,1)S(1)}, u32[]{:S(2)}, u32[]{:S(2)}) collective-permute-start(bf16[8,128,256]{2,1,0:T(8,128)(2,1)S(1)} %all_to_all.15.own_ref), channel_id=1, source_target_pairs={{0,1},{1,0},{2,3},{3,2},{4,5},{5,4},{6,7},{7,6},{8,9},{9,8},{10,11... | collective-permute-start | bytes 1572872 | tf_op jit(solution)/shard_map/ppermute | solution.py:190
  24.1 13.2 %all-to-all-start.2 = ((bf16[8,4,4096]{2,1,0:T(4,128)(2,1)}), bf16[8,4,4096]{2,1,0:T(4,128)(2,1)S(1)}, u32[]{:S(2)}, u32[]{:S(2)}) async-start(bf16[8,4,4096]{2,1,0:T(4,128)(2,1)} %broadcast_in_dim.8), calls=%async_computation.2 | async-start | bytes 524288 | tf_op jit(solution)/shard_map/all_to_all | solution.py:183
  27.8 1.6 %copy-start.1 = (bf16[2,2,64,4096]{3,2,1,0:T(8,128)(2,1)S(1)}, bf16[2,2,64,4096]{3,2,1,0:T(8,128)(2,1)}, u32[]{:S(2)}) copy-start(bf16[2,2,64,4096]{3,2,1,0:T(8,128)(2,1)} %param.7) | copy-start | bytes 6291460
  31.4 1.3 %collective-permute-start.1 = (f32[32,128]{1,0:T(8,128)S(1)}, f32[32,128]{1,0:T(8,128)S(1)}, u32[]{:S(2)}, u32[]{:S(2)}) collective-permute-start(f32[32,128]{1,0:T(8,128)S(1)} %get-tuple-element.9), channel_id=1, source_target_pairs={{0,1},{1,0},{2,3},{3,2},{4,5},{5,4},{6,7},{7,6},{8,9},{9,8},{10,11... | collective-permute-start | bytes 49160 | tf_op jit(solution)/shard_map/ppermute | solution.py:222
  38.0 10.9 %all-to-all-start.1 = ((f32[8,32,128]{2,1,0:T(8,128)}), f32[8,32,128]{2,1,0:T(8,128)S(1)}, u32[]{:S(2)}, u32[]{:S(2)}) async-start(f32[8,32,128]{2,1,0:T(8,128)} %broadcast_in_dim.7), calls=%async_computation.1 | async-start | bytes 262144 | tf_op jit(solution)/shard_map/all_to_all | solution.py:183
  41.5 10.8 %collective-permute-start.3 = (bf16[8,4,4096]{2,1,0:T(4,128)(2,1)S(1)}, bf16[8,4,4096]{2,1,0:T(4,128)(2,1)S(1)}, u32[]{:S(2)}, u32[]{:S(2)}) collective-permute-start(bf16[8,4,4096]{2,1,0:T(4,128)(2,1)S(1)} %all-to-all-done.2), channel_id=1, source_target_pairs={{0,1},{1,0},{2,3},{3,2},{4,5},{5,4},{6,7},{7,6},{8,9},{9,8},{10,11... | collective-permute-start | bytes 786440 | tf_op jit(solution)/shard_map/ppermute | solution.py:186
  52.3 1.2 %collective-permute-start.2 = (f32[64,64]{1,0:T(8,128)S(1)}, f32[64,64]{1,0:T(8,128)S(1)}, u32[]{:S(2)}, u32[]{:S(2)}) collective-permute-start(f32[64,64]{1,0:T(8,128)S(1)} %invert.1.own_ref), channel_id=1, source_target_pairs={{0,1},{1,0},{2,3},{3,2},{4,5},{5,4},{6,7},{7,6},{8,9},{9,8},{10,11... | collective-permute-start | bytes 49160 | tf_op jit(solution)/shard_map/ppermute | solution.py:233

commit v3 on v2

v3 whole, which is shorter than its diff:
```python
import functools

import jax
import jax.numpy as jnp
from jax import lax
from jax.experimental import pallas as pl
from jax.experimental.pallas import tpu as pltpu
from jax.sharding import PartitionSpec as P

F32 = jnp.float32
BF16 = jnp.bfloat16
LANES = 128
SUB = 8
VMEM = pltpu.VMEM
SMEM = pltpu.SMEM


def contract_last(a, b):
    return lax.dot_general(a, b, (((1,), (1,)), ((), ())), preferred_element_type=F32)


def contract_first(a, b):
    return lax.dot_general(a, b, (((0,), (0,)), ((), ())), preferred_element_type=F32)


def packed_symmetric(matrix):
    half = matrix.shape[0] // 2
    quarter = half // 4
    corners = (matrix[:half, :half], matrix[:half, half:], matrix[half:, half:])
    return jnp.concatenate(
        [
            jnp.concatenate([c[quarter * j : quarter * (j + 1)] for j in range(4)], 1)
            for c in corners
        ],
        0,
    )


def unpacked_symmetric(packed):
    quarter, wide = packed.shape[0] // 3, packed.shape[1]
    half = wide // 4
    corners = []
    for c in range(3):
        rows = packed[c * quarter : (c + 1) * quarter]
        corners.append(
            jnp.concatenate([rows[:, half * j : half * (j + 1)] for j in range(4)], 0)
        )
    first, cross, last = corners
    return jnp.concatenate(
        [jnp.concatenate([first, cross], 1), jnp.concatenate([cross.T, last], 1)], 0
    )


def packed_places(shape):
    quarter = shape[0] // 3
    half = shape[1] // 4
    row = lax.broadcasted_iota(jnp.int32, shape, 0)
    lane = lax.broadcasted_iota(jnp.int32, shape, 1)
    slot = (row == 0) & (lane == half)
    mirror = (row == 0) & (lane == quarter)
    diagonal = (lane % half == (lane // half) * quarter + row % quarter) & (
        (row < quarter) | (row >= 2 * quarter)
    )
    return slot, mirror, diagonal


def stage_kernel(*refs):
    count = len(refs) // 2
    arrived = refs[-1]
    copies = [
        pltpu.make_async_copy(refs[i], refs[count + i], arrived.at[i]) for i in range(count)
    ]
    for copy in copies:
        copy.start()
    for copy in copies:
        copy.wait()


def staged(*arrays):
    count = len(arrays)
    return pl.pallas_call(
        stage_kernel,
        out_shape=tuple(jax.ShapeDtypeStruct(a.shape, a.dtype) for a in arrays),
        in_specs=[whole(pl.ANY)] * count,
        out_specs=(whole(pl.ANY),) * count,
        scratch_shapes=[pltpu.SemaphoreType.DMA((count,))],
        compiler_params=params(1),
        cost_estimate=pl.CostEstimate(flops=0, bytes_accessed=2**22, transcendentals=0),
        name="stage",
    )(*arrays)


def project_kernel(
    numbers_ref,
    lengths_ref,
    act_ref,
    grad_ref,
    own_ref,
    other_ref,
    evals_ref,
    keep_ref,
    send_ref,
    sketch_ref,
    same_evals_ref,
):
    same_evals_ref[...] = evals_ref[...]
    place, core = numbers_ref[0], numbers_ref[1]
    sequences = 2 * lengths_ref.shape[0]
    length_of = [lengths_ref[s // 2, s % 2] for s in range(sequences)]
    blocks, both_ranks, chunk = own_ref.shape
    rank = both_ranks // 2
    pairs = sequences // 2
    rows, depth = act_ref.shape
    seq = rows // sequences
    def project(x_ref, first):
        total = jnp.zeros((rows, rank), F32)
        for g in range(blocks):
            for ref, at in ((own_ref, place), (other_ref, 1 - place)):
                start = pl.multiple_of((2 * g + at) * chunk, chunk)
                total += contract_last(
                    x_ref[:, pl.ds(start, chunk)], ref[g, first : first + rank, :]
                )
        return total

    token = lax.broadcasted_iota(jnp.int32, (seq, rank), 0)

    def masked(total):
        kept = []
        for s in range(sequences):
            live = token < length_of[s]
            kept.append(jnp.where(live, total[s * seq : (s + 1) * seq], 0.0))
        return kept

    count = functools.reduce(lambda a, b: a + b, length_of)
    slot, _, _ = packed_places(keep_ref.shape)

    def factor(rows_of):
        packed = packed_symmetric(contract_first(rows_of, rows_of))
        return jnp.where(slot, count.astype(F32), packed)

    inner = jnp.concatenate(masked(project(act_ref, 0)), 0).astype(BF16)
    outer_parts = masked(project(grad_ref, rank))
    factor_out = factor(jnp.concatenate(outer_parts, 0).astype(BF16))
    factor_in = factor(inner)
    first_core = core == 0
    keep_ref[...] = jnp.where(first_core, factor_in, factor_out)
    send_ref[...] = jnp.where(first_core, factor_out, factor_in)
    signed = jnp.concatenate(
        [-part if s % 2 else part for s, part in enumerate(outer_parts)], 0
    ).astype(BF16)
    sketches = []
    for p in range(pairs):
        own_rows = slice(2 * p * seq, 2 * (p + 1) * seq)
        sketches.append(contract_first(signed[own_rows], inner[own_rows]))
    sketch_ref[...] = jnp.concatenate(sketches, 1)


def gauss_jordan(tiles, width, group):
    count = len(tiles)
    sub = lax.broadcasted_iota(jnp.int32, tiles[0].shape, 0)
    shape = tiles[0].shape

    def spread_row(tile, j):
        return jnp.broadcast_to(tile[j : j + 1, :], shape)

    for start in range(0, width, group):
        columns = [
            [jnp.broadcast_to(tile[:, k : k + 1], shape) for tile in tiles]
            for k in range(start, start + group)
        ]
        for step in range(group):
            home, j = divmod(start + step, SUB)
            column = columns[step]
            inverse = 1.0 / spread_row(column[home], j)

            def eliminate(block):
                scaled = spread_row(block[home], j) * inverse
                result = [block[g] - column[g] * scaled for g in range(count)]
                result[home] = jnp.where(sub == j, scaled, result[home])
                return result

            for later in range(step + 1, group):
                columns[later] = eliminate(columns[later])
            tiles = eliminate(tiles)
    return tiles


def invert_kernel(blocks_ref, inverse_ref):
    rank = inverse_ref.shape[0]
    total = jnp.sum(blocks_ref[...], axis=0)
    slot, mirror, diagonal = packed_places(total.shape)

    def pick(mask):
        return jnp.sum(jnp.where(mask, total, 0.0), axis=(0, 1), keepdims=True)

    count = pick(slot)
    damp = 0.1 * (pick(diagonal) / count) / rank + 1e-06
    total = jnp.where(slot, pick(mirror), total)
    matrix = unpacked_symmetric(total / count + jnp.where(diagonal, damp, 0.0))
    row = lax.broadcasted_iota(jnp.int32, (rank, rank), 0)
    lane = lax.broadcasted_iota(jnp.int32, (rank, rank), 1)
    both = jnp.concatenate([matrix, jnp.where(row == lane, 1.0, 0.0)], 1)
    tiles = [both[g * SUB : (g + 1) * SUB] for g in range(rank // SUB)]
    tiles = gauss_jordan(tiles, rank, SUB)
    inverse_ref[...] = jnp.concatenate([tile[:, rank:] for tile in tiles], 0)


def exact_dot(a, b):
    return jnp.dot(a, b, precision=lax.Precision.HIGHEST, preferred_element_type=F32)


def score_kernel(
    bits, place_ref, own_ref, other_ref, sketch_ref, near_ref, far_ref, scores_ref, rows_ref
):
    place = place_ref[0]
    first_core = place % 2 == 0
    own = own_ref[...]
    other = other_ref[...]
    inverse_in = jnp.where(first_core, own, other)
    inverse_out = jnp.where(first_core, other, own)
    rank = own.shape[0]
    pairs, evals = scores_ref.shape
    left = exact_dot(inverse_out, sketch_ref[...])
    for p in range(pairs):
        rows_ref[p * rank : (p + 1) * rank, :] = exact_dot(
            left[:, p * rank : (p + 1) * rank], inverse_in
        )
    fold = 2 * LANES // rank
    steps = rank // fold
    precond = jnp.concatenate(
        [rows_ref[pl.ds(j, pairs * steps, stride=fold), :] for j in range(fold)], 1
    ).astype(BF16)
    row = lax.broadcasted_iota(jnp.int32, (pairs * steps, evals), 0) % steps
    total = jnp.zeros((pairs * steps, evals), F32)
    for g in range(steps):
        lanes = slice(g * fold * rank, (g + 1) * fold * rank)
        sketches = jnp.concatenate([near_ref[:, lanes], far_ref[:, lanes]], 0)
        total += jnp.where(row == g, contract_last(precond, sketches), 0.0)
    scores = jnp.concatenate(
        [jnp.sum(total[p * steps : (p + 1) * steps], 0, keepdims=True) for p in range(pairs)], 0
    )
    held = evals >> len(bits)
    column = lax.broadcasted_iota(jnp.int32, (evals, evals), 0)
    block = column // held
    source = jnp.full((evals, evals), place, jnp.int32)
    for i, bit in enumerate(bits):
        source = source ^ (((block >> i) & 1) * bit)
    target = source * held + column % held
    order = jnp.where(target == lax.broadcasted_iota(jnp.int32, (evals, evals), 1), 1.0, 0.0)
    scores_ref[...] = exact_dot(scores, order)


def params(mebibytes):
    return pltpu.CompilerParams(vmem_limit_bytes=mebibytes * 2**20)


def whole(space=VMEM):
    return pl.BlockSpec(memory_space=space)


def on_device(devices, activations, out_grads, lengths, proj_in, proj_out, eval_sketches):
    pairs, _, seq, depth = activations.shape
    rank = proj_in.shape[1]
    chips = devices // 2
    same_core = [[2 * chip + core for chip in range(chips)] for core in range(2)]
    place = lax.axis_index("dp").astype(jnp.int32).reshape(1)
    core = place % 2
    bits = [2**i for i in range(2, devices.bit_length() - 1)] + [2, 1]
    mid, late = bits[:-2], bits[-2]

    def swap(block, bit):
        return lax.ppermute(block, "dp", [(d, d ^ bit) for d in range(devices)])

    def copies_of(block):
        return jnp.broadcast_to(block[None], (chips,) + block.shape)

    def to_all_chips(copies):
        return lax.all_to_all(copies, "dp", 0, 0, axis_index_groups=same_core)

    def doubled(block, bit):
        return jnp.concatenate([block, swap(block, bit)], 0)

    rows = 2 * pairs * seq
    flat_in, flat_out, near = staged(
        activations.reshape(rows, depth), out_grads.reshape(rows, depth), eval_sketches
    )
    near = doubled(near, mid[0])
    mine = jnp.concatenate([proj_in, proj_out], 1).T
    own = to_all_chips(copies_of(mine))
    own, near = lax.optimization_barrier((own, near))
    other = swap(own, 1)
    for bit in mid[1:-1]:
        near = doubled(near, bit)
    arriving = swap(near, mid[-1])
    slot_core = core
    local = mine.shape[1]
    if local % LANES:
        stacked = jnp.where(
            core[0] == 0, jnp.stack([own, other], 1), jnp.stack([other, own], 1)
        )
        full = stacked.transpose(2, 0, 1, 3).reshape(2 * rank, depth)
        split = full.reshape(2 * rank, -1, 2, 2 * LANES).transpose(1, 2, 0, 3)
        own, other = split[:, 0], split[:, 1]
        slot_core = jnp.zeros((1,), jnp.int32)

    packed = jax.ShapeDtypeStruct((3 * rank // 8, 2 * rank), F32)
    keep, send, sketch, near = pl.pallas_call(
        project_kernel,
        out_shape=(
            packed,
            packed,
            jax.ShapeDtypeStruct((rank, pairs * rank), F32),
            jax.ShapeDtypeStruct(near.shape, near.dtype),
        ),
        in_specs=[whole(SMEM)] * 2 + [whole()] * 5,
        out_specs=(whole(),) * 4,
        compiler_params=params(24),
        cost_estimate=pl.CostEstimate(
            flops=4 * rows * depth * rank, bytes_accessed=6 * rows * depth, transcendentals=0
        ),
        name="project",
    )(
        jnp.concatenate([slot_core, core]),
        lengths,
        flat_in,
        flat_out,
        own,
        other,
        near,
    )
    sums = copies_of(keep + swap(send, 1))
    blocks = to_all_chips(sums)
    near = doubled(jnp.concatenate([near, arriving], 0), late)
    far = swap(near, 1)
    inverse = pl.pallas_call(
        invert_kernel,
        out_shape=jax.ShapeDtypeStruct((rank, rank), F32),
        in_specs=[whole()],
        out_specs=whole(),
        compiler_params=params(4),
        cost_estimate=pl.CostEstimate(flops=10**9, bytes_accessed=2**24, transcendentals=0),
        name="invert",
    )(blocks)
    other_inverse = swap(inverse, 1)
    evals = 2 * near.shape[0]
    return pl.pallas_call(
        functools.partial(score_kernel, bits),
        out_shape=jax.ShapeDtypeStruct((pairs, evals), F32),
        in_specs=[whole(SMEM)] + [whole()] * 5,
        out_specs=whole(),
        scratch_shapes=[pltpu.VMEM((pairs * rank, rank), F32)],
        compiler_params=params(4 + 6 * evals * rank * rank // 2**20),
        name="score",
    )(place, inverse, other_inverse, sketch, near, far)


def solution(mesh):
    in_specs = (
        P(("groups", "dp"), None, None, None),
        P(("groups", "dp"), None, None, None),
        P(("groups", "dp"), None),
        P(("groups", "dp"), None),
        P(("groups", "dp"), None),
        P(("groups", "dp"), None),
    )
    out_specs = P(("groups", "dp"), None)
    return jax.shard_map(
        functools.partial(on_device, mesh.shape["dp"]),
        mesh=mesh,
        in_specs=in_specs,
        out_specs=out_specs,
        check_vma=False,
    )
```

time: 55.3 us -> 48.6 us (0.88)
  blocking collectives: 21.6 us -> 0 us
  starting transfers between devices: 7.57 us -> 13.5 us
  waiting for transfers between devices: 13.5 us -> 19.2 us
  local copies, waits for them, and re-layouts: 4.04 us -> 8.38 us
  matrix products: 0.82 us -> 0 us
    all_to_all x1 -> x0, blocking collectives: 21.6 us -> none  [to_all_chips(): return lax.all_to_all(copies, 'dp', 0, 0, axis_index_groups=same_core)]
    ppermute x4 -> x7, waiting for transfers between devices: 1.52 us -> 7.36 us  [swap(): return lax.ppermute(block, 'dp', [(d, d ^ bit) for d in range(devices)])]
    unnamed x6 -> x14, local copies, waits for them, and re-layouts: 1.59 us -> 6.87 us
    all_to_all x2, starting transfers between devices: 7.14 us -> 10.9 us  [to_all_chips(): return lax.all_to_all(copies, 'dp', 0, 0, axis_index_groups=same_core)]
    ppermute x4 -> x7, starting transfers between devices: 0.43 us -> 2.63 us  [swap(): return lax.ppermute(block, 'dp', [(d, d ^ bit) for d in range(devices)])]
    pallas_call x2 -> x3, Pallas kernels: 2.45 us -> 3.87 us  [the longest x1 2.05 us: on_device(): pl.pallas_call(project_kernel, out_shape=(packed, packed, jax.ShapeDtypeS...]
    pallas_call x1, Pallas kernels: 3.43 us -> 2.2 us  [on_device(): pl.pallas_call(invert_kernel, out_shape=jax.ShapeDtypeStruct((rank, rank)...]
    dot_general x1 -> x0, matrix products: 0.82 us -> none  [contract_last(): lax.dot_general(a, b, (((1,), (1,)), ((), ())), preferred_element_type=F32)]
  transfers between devices with their start and end apart: 6 -> 9, of which waited for: 4 -> 7; matrix products, arithmetic and copies ran while one was open for 4% -> 2% of each run, Pallas kernels for 10% -> 10%
where the time goes in v3:
time: 48.6 us; the launch traced here: 48.1 us
  waiting for transfers between devices  19.2 us (40%)
  starting transfers between devices  13.5 us (28%)
  local copies, waits for them, and re-layouts  8.38 us (17%)
  Pallas kernels  6.07 us (12%)
  other arithmetic  0.91 us (2%)
    all_to_all x2, waiting for transfers between devices, to_all_chips(): return lax.all_to_all(copies, 'dp', 0, 0, axis_index_groups=same_core)  11.8 us
    all_to_all x2, starting transfers between devices, to_all_chips(): return lax.all_to_all(copies, 'dp', 0, 0, axis_index_groups=same_core)  10.9 us
    ppermute x7, waiting for transfers between devices, swap(): return lax.ppermute(block, 'dp', [(d, d ^ bit) for d in range(devices)])  7.36 us
    unnamed x14, local copies, waits for them, and re-layouts  6.87 us
    ppermute x7, starting transfers between devices, swap(): return lax.ppermute(block, 'dp', [(d, d ^ bit) for d in range(devices)])  2.63 us
    pallas_call x1, Pallas kernels, on_device(): pl.pallas_call(invert_kernel, out_shape=jax.ShapeDtypeStruct((rank, rank)...  2.2 us
    pallas_call x1, Pallas kernels, on_device(): pl.pallas_call(project_kernel, out_shape=(packed, packed, jax.ShapeDtypeS...  2.05 us
    broadcast_in_dim x2, local copies, waits for them, and re-layouts, copies_of(): return jnp.broadcast_to(block[None], (chips,) + block.shape)  1.49 us
  transfers between devices with their start and end apart: 9, of which 7 were waited for; matrix products, arithmetic and copies ran while one was open for 2% of the time, Pallas kernels for 10%

profile of v3, /device:TPU:0, one launch (start us, length us, event | category | flops | bytes accessed | tf_op | source)
XLA Modules:
  0.0 48.1 jit_solution(141926042262527147)
XLA Ops:
  0.0 0.8 %maximum_bitcast_fusion = bf16[128,256]{1,0:T(8,128)(2,1)S(1)} fusion(bf16[256,64]{0,1:T(8,128)(2,1)} %param.10, bf16[256,64]{0,1:T(8,128)(2,1)} %param.9), kind=kLoop, calls=%fused_computation.1 | loop fusion | flops 131072 | bytes 131072 | tf_op jit(solution)/shard_map/transpose | solution.py:288
  0.8 0.8 %broadcast_in_dim.4 = bf16[8,128,256]{2,1,0:T(8,128)(2,1)} broadcast(bf16[128,256]{1,0:T(8,128)(2,1)S(1)} %maximum_bitcast_fusion), dimensions={1,2} | broadcast | bytes 589824 | tf_op jit(solution)/shard_map/broadcast_in_dim | solution.py:275
  1.6 7.3 %all-to-all-start = ((bf16[8,128,256]{2,1,0:T(8,128)(2,1)}), bf16[8,128,256]{2,1,0:T(8,128)(2,1)S(1)}, u32[]{:S(2)}, u32[]{:S(2)}) async-start(bf16[8,128,256]{2,1,0:T(8,128)(2,1)} %broadcast_in_dim.4), calls=%async_computation | async-start | bytes 1048576 | tf_op jit(solution)/shard_map/all_to_all | solution.py:278
  8.9 0.0 copy-start
  8.9 1.6 %copy-done = bf16[2,2,64,4096]{3,2,1,0:T(8,128)(2,1)S(1)} copy-done((bf16[2,2,64,4096]{3,2,1,0:T(8,128)(2,1)S(1)}, bf16[2,2,64,4096]{3,2,1,0:T(8,128)(2,1)}, u32[]{:S(2)}) %copy-start) | copy-done | bytes 2097176
  10.5 0.0 copy-start.1
  10.5 1.6 %copy-done.1 = bf16[2,2,64,4096]{3,2,1,0:T(8,128)(2,1)S(1)} copy-done((bf16[2,2,64,4096]{3,2,1,0:T(8,128)(2,1)S(1)}, bf16[2,2,64,4096]{3,2,1,0:T(8,128)(2,1)}, u32[]{:S(2)}) %copy-start.1) | copy-done | bytes 2097176
  12.1 0.0 copy-start.4
  12.1 0.8 %copy-done.4 = bf16[4,4096]{1,0:T(4,128)(2,1)S(1)} copy-done((bf16[4,4096]{1,0:T(4,128)(2,1)S(1)}, bf16[4,4096]{1,0:T(4,128)(2,1)}, u32[]{:S(2)}) %copy-start.4) | copy-done | bytes 32792
  12.8 0.0 copy-start.5
  12.8 0.3 stage.1
  13.2 0.0 copy-start.2
  13.2 1.3 %copy-done.2 = bf16[256,4096]{1,0:T(8,128)(2,1)} copy-done((bf16[256,4096]{1,0:T(8,128)(2,1)}, bf16[256,4096]{1,0:T(8,128)(2,1)S(1)}, u32[]{:S(2)}) %copy-start.2) | copy-done | bytes 2097176
  14.5 2.0 %collective-permute-start = (bf16[4,4096]{1,0:T(4,128)(2,1)S(1)}, bf16[4,4096]{1,0:T(4,128)(2,1)S(1)}, u32[]{:S(2)}, u32[]{:S(2)}) collective-permute-start(bf16[4,4096]{1,0:T(4,128)(2,1)S(1)} %get-tuple-element.16), channel_id=1, source_target_pairs={{0,4},{1,5},{2,6},{3,7},{4,0},{5,1},{6,2},{7,3},{8,12},{9,13},{10,... | collective-permute-start | bytes 98312 | tf_op jit(solution)/shard_map/ppermute | solution.py:272
  16.5 2.0 %collective-permute-done = bf16[4,4096]{1,0:T(4,128)(2,1)S(1)} collective-permute-done((bf16[4,4096]{1,0:T(4,128)(2,1)S(1)}, bf16[4,4096]{1,0:T(4,128)(2,1)S(1)}, u32[]{:S(2)}, u32[]{:S(2)}) %collective-permute-start) | collective-permute-done | bytes 32800 | tf_op jit(solution)/shard_map/ppermute | solution.py:272
  18.6 4.8 %all-to-all-done.own_ref = bf16[8,128,256]{2,1,0:T(8,128)(2,1)S(1)} async-done(((bf16[8,128,256]{2,1,0:T(8,128)(2,1)}), bf16[8,128,256]{2,1,0:T(8,128)(2,1)S(1)}, u32[]{:S(2)}, u32[]{:S(2)}) %all-to-all-start) | async-done | bytes 524320 | tf_op jit(solution)/shard_map/all_to_all | solution.py:278
  23.4 0.0 collective-permute-start.1
  23.4 0.1 pad_add_fusion.numbers_ref
  23.4 0.2 collective-permute-start.4
  23.6 1.7 %collective-permute-done.1.other_ref = bf16[8,128,256]{2,1,0:T(8,128)(2,1)S(1)} collective-permute-done((bf16[8,128,256]{2,1,0:T(8,128)(2,1)S(1)}, bf16[8,128,256]{2,1,0:T(8,128)(2,1)S(1)}, u32[]{:S(2)}, u32[]{:S(2)}) %collective-permute-start.1) | collective-permute-done | bytes 524320 | tf_op jit(solution)/shard_map/ppermute | solution.py:272
  25.3 0.0 copy-done.5
  25.3 0.0 copy-start.3
  25.3 1.6 %copy-done.3 = bf16[256,4096]{1,0:T(8,128)(2,1)S(1)} copy-done((bf16[256,4096]{1,0:T(8,128)(2,1)S(1)}, bf16[256,4096]{1,0:T(8,128)(2,1)}, u32[]{:S(2)}) %copy-start.3) | copy-done | bytes 2097176
  26.9 2.1 %project.1 = (f32[24,128]{1,0:T(8,128)S(1)}, f32[24,128]{1,0:T(8,128)S(1)}, f32[64,128]{1,0:T(8,128)S(1)}, bf16[8,4096]{1,0:T(8,128)(2,1)S(1)}) custom-call(s32[2]{0:T(128)S(1)} %pad_add_fusion.numbers_ref, s32[2,2]{1,0:T(2,128)S(1)} %copy-done.5, bf16[256,4096]{1,0:T(8,128)(2,1)S(1)} %get-tuple-element.14.act_ref, bf16[256,4096]{1,0:T(8,128)(2,1)S(1)} %copy-done.3, ...), custom_call_target="tpu_custom_call" | custom-call | flops 268435456 | bytes 6291456 | tf_op jit(solution)/shard_map/project/pallas_call | solution.py:307
  28.9 1.3 %collective-permute-done.4 = bf16[8,4096]{1,0:T(8,128)(2,1)S(1)} collective-permute-done((bf16[8,4096]{1,0:T(8,128)(2,1)S(1)}, bf16[8,4096]{1,0:T(8,128)(2,1)S(1)}, u32[]{:S(2)}, u32[]{:S(2)}) %collective-permute-start.4) | collective-permute-done | bytes 65568 | tf_op jit(solution)/shard_map/ppermute | solution.py:272
  30.3 0.3 collective-permute-start.5
  30.6 0.0 collective-permute-start.2
  30.6 1.2 %collective-permute-done.2 = f32[24,128]{1,0:T(8,128)S(1)} collective-permute-done((f32[24,128]{1,0:T(8,128)S(1)}, f32[24,128]{1,0:T(8,128)S(1)}, u32[]{:S(2)}, u32[]{:S(2)}) %collective-permute-start.2) | collective-permute-done | bytes 12320 | tf_op jit(solution)/shard_map/ppermute | solution.py:272
  31.8 0.7 %broadcast_in_dim.5 = f32[8,24,128]{2,1,0:T(8,128)} broadcast(f32[24,128]{1,0:T(8,128)S(1)} %add.10), dimensions={1,2} | broadcast | bytes 110592 | tf_op jit(solution)/shard_map/broadcast_in_dim | solution.py:275
  32.4 3.6 %all-to-all-start.1 = ((f32[8,24,128]{2,1,0:T(8,128)}), f32[8,24,128]{2,1,0:T(8,128)S(1)}, u32[]{:S(2)}, u32[]{:S(2)}) async-start(f32[8,24,128]{2,1,0:T(8,128)} %broadcast_in_dim.5), calls=%async_computation.1 | async-start | bytes 196608 | tf_op jit(solution)/shard_map/all_to_all | solution.py:278
  36.1 0.0 collective-permute-done.5
  36.1 0.1 collective-permute-start.6
  36.2 7.0 %all-to-all-done.1.blocks_ref = f32[8,24,128]{2,1,0:T(8,128)S(1)} async-done(((f32[8,24,128]{2,1,0:T(8,128)}), f32[8,24,128]{2,1,0:T(8,128)S(1)}, u32[]{:S(2)}, u32[]{:S(2)}) %all-to-all-start.1) | async-done | bytes 98336 | tf_op jit(solution)/shard_map/all_to_all | solution.py:278
  43.2 2.2 %invert.1.own_ref = f32[64,64]{1,0:T(8,128)S(1)} custom-call(f32[8,24,128]{2,1,0:T(8,128)S(1)} %all-to-all-done.1.blocks_ref), custom_call_target="tpu_custom_call" | custom-call | flops 1000000000 | bytes 16777216 | tf_op jit(solution)/shard_map/invert/pallas_call | solution.py:335
  45.4 0.0 collective-permute-start.3
  45.5 1.2 %collective-permute-done.3.other_ref = f32[64,64]{1,0:T(8,128)S(1)} collective-permute-done((f32[64,64]{1,0:T(8,128)S(1)}, f32[64,64]{1,0:T(8,128)S(1)}, u32[]{:S(2)}, u32[]{:S(2)}) %collective-permute-start.3) | collective-permute-done | bytes 16416 | tf_op jit(solution)/shard_map/ppermute | solution.py:272
  46.6 0.0 collective-permute-done.6.far_ref
  46.6 1.5 %score.1 = f32[2,64]{1,0:T(2,128)} custom-call(s32[1]{0:T(128)} %bitcast.place_ref, f32[64,64]{1,0:T(8,128)S(1)} %invert.1.own_ref, f32[64,64]{1,0:T(8,128)S(1)} %collective-permute-done.3.other_ref, f32[64,128]{1,0:T(8,128)S(1)} %get-tuple-element.21.sketch_ref, bf16[32,4096]{1,0:T(8,128)(2,1)S(1)} %constant_dynamic-update-slice_fusion.near_ref, ...), custom_call_target="tpu_custom_call" | custom-call | tf_op jit(solution)/shard_map/score/pallas_call | solution.py:346
  (6 shorter events, 0.1 us)
Async XLA Ops:
  1.6 21.7 %all-to-all-start = ((bf16[8,128,256]{2,1,0:T(8,128)(2,1)}), bf16[8,128,256]{2,1,0:T(8,128)(2,1)S(1)}, u32[]{:S(2)}, u32[]{:S(2)}) async-start(bf16[8,128,256]{2,1,0:T(8,128)(2,1)} %broadcast_in_dim.4), calls=%async_computation | async-start | bytes 1048576 | tf_op jit(solution)/shard_map/all_to_all | solution.py:278
  8.9 1.6 %copy-start = (bf16[2,2,64,4096]{3,2,1,0:T(8,128)(2,1)S(1)}, bf16[2,2,64,4096]{3,2,1,0:T(8,128)(2,1)}, u32[]{:S(2)}) copy-start(bf16[2,2,64,4096]{3,2,1,0:T(8,128)(2,1)} %param.6) | copy-start | bytes 6291460
  10.5 1.6 %copy-start.1 = (bf16[2,2,64,4096]{3,2,1,0:T(8,128)(2,1)S(1)}, bf16[2,2,64,4096]{3,2,1,0:T(8,128)(2,1)}, u32[]{:S(2)}) copy-start(bf16[2,2,64,4096]{3,2,1,0:T(8,128)(2,1)} %param.7) | copy-start | bytes 6291460
  12.1 0.8 %copy-start.4 = (bf16[4,4096]{1,0:T(4,128)(2,1)S(1)}, bf16[4,4096]{1,0:T(4,128)(2,1)}, u32[]{:S(2)}) copy-start(bf16[4,4096]{1,0:T(4,128)(2,1)} %refs_2_.1) | copy-start | bytes 98308
  12.8 12.5 %copy-start.5 = (s32[2,2]{1,0:T(2,128)S(1)}, s32[2,2]{1,0:T(2,128)}, u32[]{:S(2)}) copy-start(s32[2,2]{1,0:T(2,128)} %lengths_ref.1) | copy-start | bytes 52
  13.2 1.3 %copy-start.2 = (bf16[256,4096]{1,0:T(8,128)(2,1)}, bf16[256,4096]{1,0:T(8,128)(2,1)S(1)}, u32[]{:S(2)}) copy-start(bf16[256,4096]{1,0:T(8,128)(2,1)S(1)} %get-tuple-element.15.grad_ref) | copy-start | bytes 6291460
  14.5 4.0 %collective-permute-start = (bf16[4,4096]{1,0:T(4,128)(2,1)S(1)}, bf16[4,4096]{1,0:T(4,128)(2,1)S(1)}, u32[]{:S(2)}, u32[]{:S(2)}) collective-permute-start(bf16[4,4096]{1,0:T(4,128)(2,1)S(1)} %get-tuple-element.16), channel_id=1, source_target_pairs={{0,4},{1,5},{2,6},{3,7},{4,0},{5,1},{6,2},{7,3},{8,12},{9,13},{10,... | collective-permute-start | bytes 98312 | tf_op jit(solution)/shard_map/ppermute | solution.py:272
  23.4 1.9 %collective-permute-start.1 = (bf16[8,128,256]{2,1,0:T(8,128)(2,1)S(1)}, bf16[8,128,256]{2,1,0:T(8,128)(2,1)S(1)}, u32[]{:S(2)}, u32[]{:S(2)}) collective-permute-start(bf16[8,128,256]{2,1,0:T(8,128)(2,1)S(1)} %all-to-all-done.own_ref), channel_id=1, source_target_pairs={{0,1},{1,0},{2,3},{3,2},{4,5},{5,4},{6,7},{7,6},{8,9},{9,8},{10,11... | collective-permute-start | bytes 1572872 | tf_op jit(solution)/shard_map/ppermute | solution.py:272
  23.4 6.8 %collective-permute-start.4 = (bf16[8,4096]{1,0:T(8,128)(2,1)S(1)}, bf16[8,4096]{1,0:T(8,128)(2,1)S(1)}, u32[]{:S(2)}, u32[]{:S(2)}) collective-permute-start(bf16[8,4096]{1,0:T(8,128)(2,1)S(1)} %pad_maximum_fusion.1.evals_ref), channel_id=1, source_target_pairs={{0,8},{1,9},{2,10},{3,11},{4,12},{5,13},{6,14},{7,15},{8,0},{9,1},... | collective-permute-start | bytes 196616 | tf_op jit(solution)/shard_map/ppermute | solution.py:272
  25.3 1.6 %copy-start.3 = (bf16[256,4096]{1,0:T(8,128)(2,1)S(1)}, bf16[256,4096]{1,0:T(8,128)(2,1)}, u32[]{:S(2)}) copy-start(bf16[256,4096]{1,0:T(8,128)(2,1)} %copy-done.2) | copy-start | bytes 6291460
  30.3 5.8 %collective-permute-start.5 = (bf16[16,4096]{1,0:T(8,128)(2,1)S(1)}, bf16[16,4096]{1,0:T(8,128)(2,1)S(1)}, u32[]{:S(2)}, u32[]{:S(2)}) collective-permute-start(bf16[16,4096]{1,0:T(8,128)(2,1)S(1)} %pad_maximum_fusion), channel_id=1, source_target_pairs={{0,2},{1,3},{2,0},{3,1},{4,6},{5,7},{6,4},{7,5},{8,10},{9,11},{10,... | collective-permute-start | bytes 393224 | tf_op jit(solution)/shard_map/ppermute | solution.py:272
  30.6 1.2 %collective-permute-start.2 = (f32[24,128]{1,0:T(8,128)S(1)}, f32[24,128]{1,0:T(8,128)S(1)}, u32[]{:S(2)}, u32[]{:S(2)}) collective-permute-start(f32[24,128]{1,0:T(8,128)S(1)} %get-tuple-element.20), channel_id=1, source_target_pairs={{0,1},{1,0},{2,3},{3,2},{4,5},{5,4},{6,7},{7,6},{8,9},{9,8},{10,11... | collective-permute-start | bytes 36872 | tf_op jit(solution)/shard_map/ppermute | solution.py:272
  32.4 10.8 %all-to-all-start.1 = ((f32[8,24,128]{2,1,0:T(8,128)}), f32[8,24,128]{2,1,0:T(8,128)S(1)}, u32[]{:S(2)}, u32[]{:S(2)}) async-start(f32[8,24,128]{2,1,0:T(8,128)} %broadcast_in_dim.5), calls=%async_computation.1 | async-start | bytes 196608 | tf_op jit(solution)/shard_map/all_to_all | solution.py:278
  36.1 10.5 %collective-permute-start.6 = (bf16[32,4096]{1,0:T(8,128)(2,1)S(1)}, bf16[32,4096]{1,0:T(8,128)(2,1)S(1)}, u32[]{:S(2)}, u32[]{:S(2)}) collective-permute-start(bf16[32,4096]{1,0:T(8,128)(2,1)S(1)} %constant_dynamic-update-slice_fusion.near_ref), channel_id=1, source_target_pairs={{0,1},{1,0},{2,3},{3,2},{4,5},{5,4},{6,7},{7,6},{8,9},{9,8},{10,11... | collective-permute-start | bytes 786440 | tf_op jit(solution)/shard_map/ppermute | solution.py:272
  45.4 1.2 %collective-permute-start.3 = (f32[64,64]{1,0:T(8,128)S(1)}, f32[64,64]{1,0:T(8,128)S(1)}, u32[]{:S(2)}, u32[]{:S(2)}) collective-permute-start(f32[64,64]{1,0:T(8,128)S(1)} %invert.1.own_ref), channel_id=1, source_target_pairs={{0,1},{1,0},{2,3},{3,2},{4,5},{5,4},{6,7},{7,6},{8,9},{9,8},{10,11... | collective-permute-start | bytes 49160 | tf_op jit(solution)/shard_map/ppermute | solution.py:272

commit v4 on v3

--- a/solution.py
+++ b/solution.py
@@ -64,6 +64,84 @@
     return slot, mirror, diagonal
 
 
+def projected(x_ref, blocks_ref, first, rank, place, total):
+    blocks, _, chunk = blocks_ref.shape
+    for g in range(blocks):
+        start = pl.multiple_of((2 * g + place) * chunk, chunk)
+        total += contract_last(
+            x_ref[:, pl.ds(start, chunk)], blocks_ref[g, first : first + rank, :]
+        )
+    return total
+
+
+def own_place(split_cores):
+    return lax.axis_index("dp") % 2 if split_cores else 0
+
+
+def first_half_kernel(split_cores, first, x_ref, own_ref, total_ref):
+    total_ref[...] = projected(
+        x_ref,
+        own_ref,
+        first,
+        total_ref.shape[1],
+        own_place(split_cores),
+        jnp.zeros(total_ref.shape, F32),
+    )
+
+
+def second_half_kernel(
+    split_cores,
+    lengths_ref,
+    act_ref,
+    grad_ref,
+    other_ref,
+    half_in_ref,
+    half_out_ref,
+    keep_ref,
+    send_ref,
+    sketch_ref,
+):
+    place = 1 - own_place(split_cores)
+    sequences = 2 * lengths_ref.shape[0]
+    length_of = [lengths_ref[s // 2, s % 2] for s in range(sequences)]
+    pairs = sequences // 2
+    rows, rank = half_in_ref.shape
+    seq = rows // sequences
+    token = lax.broadcasted_iota(jnp.int32, (seq, rank), 0)
+
+    def masked(total):
+        kept = []
+        for s in range(sequences):
+            live = token < length_of[s]
+            kept.append(jnp.where(live, total[s * seq : (s + 1) * seq], 0.0))
+        return kept
+
+    count = functools.reduce(lambda a, b: a + b, length_of)
+    slot, _, _ = packed_places(keep_ref.shape)
+
+    def factor(rows_of):
+        packed = packed_symmetric(contract_first(rows_of, rows_of))
+        return jnp.where(slot, count.astype(F32), packed)
+
+    total_in = projected(act_ref, other_ref, 0, rank, place, half_in_ref[...])
+    total_out = projected(grad_ref, other_ref, rank, rank, place, half_out_ref[...])
+    inner = jnp.concatenate(masked(total_in), 0).astype(BF16)
+    outer_parts = masked(total_out)
+    factor_in = factor(inner)
+    factor_out = factor(jnp.concatenate(outer_parts, 0).astype(BF16))
+    first_core = lax.axis_index("dp") % 2 == 0
+    keep_ref[...] = jnp.where(first_core, factor_in, factor_out)
+    send_ref[...] = jnp.where(first_core, factor_out, factor_in)
+    signed = jnp.concatenate(
+        [-part if s % 2 else part for s, part in enumerate(outer_parts)], 0
+    ).astype(BF16)
+    sketches = []
+    for p in range(pairs):
+        own_rows = slice(2 * p * seq, 2 * (p + 1) * seq)
+        sketches.append(contract_first(signed[own_rows], inner[own_rows]))
+    sketch_ref[...] = jnp.concatenate(sketches, 1)
+
+
 def stage_kernel(*refs):
     count = len(refs) // 2
     arrived = refs[-1]
@@ -90,71 +168,6 @@
     )(*arrays)
 
 
-def project_kernel(
-    numbers_ref,
-    lengths_ref,
-    act_ref,
-    grad_ref,
-    own_ref,
-    other_ref,
-    evals_ref,
-    keep_ref,
-    send_ref,
-    sketch_ref,
-    same_evals_ref,
-):
-    same_evals_ref[...] = evals_ref[...]
-    place, core = numbers_ref[0], numbers_ref[1]
-    sequences = 2 * lengths_ref.shape[0]
-    length_of = [lengths_ref[s // 2, s % 2] for s in range(sequences)]
-    blocks, both_ranks, chunk = own_ref.shape
-    rank = both_ranks // 2
-    pairs = sequences // 2
-    rows, depth = act_ref.shape
-    seq = rows // sequences
-    def project(x_ref, first):
-        total = jnp.zeros((rows, rank), F32)
-        for g in range(blocks):
-            for ref, at in ((own_ref, place), (other_ref, 1 - place)):
-                start = pl.multiple_of((2 * g + at) * chunk, chunk)
-                total += contract_last(
-                    x_ref[:, pl.ds(start, chunk)], ref[g, first : first + rank, :]
-                )
-        return total
-
-    token = lax.broadcasted_iota(jnp.int32, (seq, rank), 0)
-
-    def masked(total):
-        kept = []
-        for s in range(sequences):
-            live = token < length_of[s]
-            kept.append(jnp.where(live, total[s * seq : (s + 1) * seq], 0.0))
-        return kept
-
-    count = functools.reduce(lambda a, b: a + b, length_of)
-    slot, _, _ = packed_places(keep_ref.shape)
-
-    def factor(rows_of):
-        packed = packed_symmetric(contract_first(rows_of, rows_of))
-        return jnp.where(slot, count.astype(F32), packed)
-
-    inner = jnp.concatenate(masked(project(act_ref, 0)), 0).astype(BF16)
-    outer_parts = masked(project(grad_ref, rank))
-    factor_out = factor(jnp.concatenate(outer_parts, 0).astype(BF16))
-    factor_in = factor(inner)
-    first_core = core == 0
-    keep_ref[...] = jnp.where(first_core, factor_in, factor_out)
-    send_ref[...] = jnp.where(first_core, factor_out, factor_in)
-    signed = jnp.concatenate(
-        [-part if s % 2 else part for s, part in enumerate(outer_parts)], 0
-    ).astype(BF16)
-    sketches = []
-    for p in range(pairs):
-        own_rows = slice(2 * p * seq, 2 * (p + 1) * seq)
-        sketches.append(contract_first(signed[own_rows], inner[own_rows]))
-    sketch_ref[...] = jnp.concatenate(sketches, 1)
-
-
 def gauss_jordan(tiles, width, group):
     count = len(tiles)
     sub = lax.broadcasted_iota(jnp.int32, tiles[0].shape, 0)
@@ -210,9 +223,10 @@
 
 
 def score_kernel(
-    bits, place_ref, own_ref, other_ref, sketch_ref, near_ref, far_ref, scores_ref, rows_ref
+    bits, own_ref, other_ref, sketch_ref, *rest
 ):
-    place = place_ref[0]
+    *evals_refs, scores_ref, rows_ref = rest
+    place = lax.axis_index("dp")
     first_core = place % 2 == 0
     own = own_ref[...]
     other = other_ref[...]
@@ -234,7 +248,7 @@
     total = jnp.zeros((pairs * steps, evals), F32)
     for g in range(steps):
         lanes = slice(g * fold * rank, (g + 1) * fold * rank)
-        sketches = jnp.concatenate([near_ref[:, lanes], far_ref[:, lanes]], 0)
+        sketches = jnp.concatenate([ref[:, lanes] for ref in evals_refs], 0)
         total += jnp.where(row == g, contract_last(precond, sketches), 0.0)
     scores = jnp.concatenate(
         [jnp.sum(total[p * steps : (p + 1) * steps], 0, keepdims=True) for p in range(pairs)], 0
@@ -263,10 +277,8 @@
     rank = proj_in.shape[1]
     chips = devices // 2
     same_core = [[2 * chip + core for chip in range(chips)] for core in range(2)]
-    place = lax.axis_index("dp").astype(jnp.int32).reshape(1)
-    core = place % 2
     bits = [2**i for i in range(2, devices.bit_length() - 1)] + [2, 1]
-    mid, late = bits[:-2], bits[-2]
+    first, *mid, late, _ = bits
 
     def swap(block, bit):
         return lax.ppermute(block, "dp", [(d, d ^ bit) for d in range(devices)])
@@ -284,54 +296,54 @@
     flat_in, flat_out, near = staged(
         activations.reshape(rows, depth), out_grads.reshape(rows, depth), eval_sketches
     )
-    near = doubled(near, mid[0])
+    near = doubled(near, first)
     mine = jnp.concatenate([proj_in, proj_out], 1).T
     own = to_all_chips(copies_of(mine))
     own, near = lax.optimization_barrier((own, near))
     other = swap(own, 1)
-    for bit in mid[1:-1]:
+    for bit in mid:
         near = doubled(near, bit)
-    arriving = swap(near, mid[-1])
-    slot_core = core
-    local = mine.shape[1]
-    if local % LANES:
+    arriving = swap(near, late)
+    evals_pieces = [near, arriving, swap(near, 1), swap(arriving, 1)]
+    split_cores = mine.shape[1] % LANES == 0
+    if not split_cores:
+        first_core = lax.axis_index("dp") % 2 == 0
         stacked = jnp.where(
-            core[0] == 0, jnp.stack([own, other], 1), jnp.stack([other, own], 1)
+            first_core, jnp.stack([own, other], 1), jnp.stack([other, own], 1)
         )
         full = stacked.transpose(2, 0, 1, 3).reshape(2 * rank, depth)
         split = full.reshape(2 * rank, -1, 2, 2 * LANES).transpose(1, 2, 0, 3)
         own, other = split[:, 0], split[:, 1]
-        slot_core = jnp.zeros((1,), jnp.int32)
-
+
+    def first_half(x, first):
+        return pl.pallas_call(
+            functools.partial(first_half_kernel, split_cores, first),
+            out_shape=jax.ShapeDtypeStruct((rows, rank), F32),
+            in_specs=[whole()] * 2,
+            out_specs=whole(),
+            compiler_params=params(8),
+            cost_estimate=pl.CostEstimate(
+                flops=rows * depth * rank, bytes_accessed=2 * rows * depth, transcendentals=0
+            ),
+            name="first_half",
+        )(x, own)
+
+    half_in = first_half(flat_in, 0)
+    half_out = first_half(flat_out, rank)
     packed = jax.ShapeDtypeStruct((3 * rank // 8, 2 * rank), F32)
-    keep, send, sketch, near = pl.pallas_call(
-        project_kernel,
-        out_shape=(
-            packed,
-            packed,
-            jax.ShapeDtypeStruct((rank, pairs * rank), F32),
-            jax.ShapeDtypeStruct(near.shape, near.dtype),
+    keep, send, sketch = pl.pallas_call(
+        functools.partial(second_half_kernel, split_cores),
+        out_shape=(packed, packed, jax.ShapeDtypeStruct((rank, pairs * rank), F32)),
+        in_specs=[whole(SMEM)] + [whole()] * 5,
+        out_specs=(whole(),) * 3,
+        compiler_params=params(8),
+        cost_estimate=pl.CostEstimate(
+            flops=2 * rows * depth * rank, bytes_accessed=4 * rows * depth, transcendentals=0
         ),
-        in_specs=[whole(SMEM)] * 2 + [whole()] * 5,
-        out_specs=(whole(),) * 4,
-        compiler_params=params(24),
-        cost_estimate=pl.CostEstimate(
-            flops=4 * rows * depth * rank, bytes_accessed=6 * rows * depth, transcendentals=0
-        ),
-        name="project",
-    )(
-        jnp.concatenate([slot_core, core]),
-        lengths,
-        flat_in,
-        flat_out,
-        own,
-        other,
-        near,
-    )
+        name="second_half",
+    )(lengths, flat_in, flat_out, other, half_in, half_out)
     sums = copies_of(keep + swap(send, 1))
     blocks = to_all_chips(sums)
-    near = doubled(jnp.concatenate([near, arriving], 0), late)
-    far = swap(near, 1)
     inverse = pl.pallas_call(
         invert_kernel,
         out_shape=jax.ShapeDtypeStruct((rank, rank), F32),
@@ -342,16 +354,16 @@
         name="invert",
     )(blocks)
     other_inverse = swap(inverse, 1)
-    evals = 2 * near.shape[0]
+    evals = 4 * near.shape[0]
     return pl.pallas_call(
         functools.partial(score_kernel, bits),
         out_shape=jax.ShapeDtypeStruct((pairs, evals), F32),
-        in_specs=[whole(SMEM)] + [whole()] * 5,
+        in_specs=[whole()] * 7,
         out_specs=whole(),
         scratch_shapes=[pltpu.VMEM((pairs * rank, rank), F32)],
         compiler_params=params(4 + 6 * evals * rank * rank // 2**20),
         name="score",
-    )(place, inverse, other_inverse, sketch, near, far)
+    )(inverse, other_inverse, sketch, *evals_pieces)
 
 
 def solution(mesh):

time: 48.6 us -> 45.3 us (0.932)
  waiting for transfers between devices: 19.2 us -> 14.1 us
  starting transfers between devices: 13.5 us -> 15.6 us
  local copies, waits for them, and re-layouts: 8.38 us -> 7.78 us
    all_to_all x2, waiting for transfers between devices: 11.8 us -> 5.42 us  [to_all_chips(): return lax.all_to_all(copies, 'dp', 0, 0, axis_index_groups=same_core)]
    ppermute x7 -> x8, starting transfers between devices: 2.63 us -> 4.37 us  [swap(): return lax.ppermute(block, 'dp', [(d, d ^ bit) for d in range(devices)])]
    ppermute x7 -> x8, waiting for transfers between devices: 7.36 us -> 8.72 us  [swap(): return lax.ppermute(block, 'dp', [(d, d ^ bit) for d in range(devices)])]
    unnamed x14 -> x13, local copies, waits for them, and re-layouts: 6.87 us -> 6.29 us
    pallas_call x1 -> x3, Pallas kernels: 2.05 us -> 2.34 us  [the longest x1 1.51 us: on_device(): pl.pallas_call(functools.partial(second_half_kernel, split_cores), out_sh...]
  transfers between devices with their start and end apart: 9 -> 10, of which waited for: 7 -> 6; matrix products, arithmetic and copies ran while one was open for 2% -> 2% of each run, Pallas kernels for 10% -> 11%
where the time goes in v4:
time: 45.3 us; the launch traced here: 44.8 us
  starting transfers between devices  15.6 us (34%)
  waiting for transfers between devices  14.1 us (31%)
  local copies, waits for them, and re-layouts  7.78 us (17%)
  Pallas kernels  6.36 us (14%)
  other arithmetic  0.82 us (2%)
    all_to_all x2, starting transfers between devices, to_all_chips(): return lax.all_to_all(copies, 'dp', 0, 0, axis_index_groups=same_core)  11.2 us
    ppermute x8, waiting for transfers between devices, swap(): return lax.ppermute(block, 'dp', [(d, d ^ bit) for d in range(devices)])  8.72 us
    unnamed x13, local copies, waits for them, and re-layouts  6.29 us
    all_to_all x2, waiting for transfers between devices, to_all_chips(): return lax.all_to_all(copies, 'dp', 0, 0, axis_index_groups=same_core)  5.42 us
    ppermute x8, starting transfers between devices, swap(): return lax.ppermute(block, 'dp', [(d, d ^ bit) for d in range(devices)])  4.37 us
    pallas_call x1, Pallas kernels, on_device(): pl.pallas_call(invert_kernel, out_shape=jax.ShapeDtypeStruct((rank, rank)...  2.2 us
    pallas_call x1, Pallas kernels, on_device(): pl.pallas_call(functools.partial(second_half_kernel, split_cores), out_sh...  1.51 us
    broadcast_in_dim x2, local copies, waits for them, and re-layouts, copies_of(): return jnp.broadcast_to(block[None], (chips,) + block.shape)  1.48 us
  transfers between devices with their start and end apart: 10, of which 6 were waited for; matrix products, arithmetic and copies ran while one was open for 2% of the time, Pallas kernels for 11%

profile of v4, /device:TPU:0, one launch (start us, length us, event | category | flops | bytes accessed | tf_op | source)
XLA Modules:
  0.0 44.8 jit_solution(14105492366755587439)
XLA Ops:
  0.0 0.8 %maximum_bitcast_fusion = bf16[128,256]{1,0:T(8,128)(2,1)S(1)} fusion(bf16[256,64]{0,1:T(8,128)(2,1)} %param.10, bf16[256,64]{0,1:T(8,128)(2,1)} %param.9), kind=kLoop, calls=%fused_computation | loop fusion | flops 131072 | bytes 131072 | tf_op jit(solution)/shard_map/transpose | solution.py:300
  0.8 0.8 %broadcast_in_dim.4 = bf16[8,128,256]{2,1,0:T(8,128)(2,1)} broadcast(bf16[128,256]{1,0:T(8,128)(2,1)S(1)} %maximum_bitcast_fusion), dimensions={1,2} | broadcast | bytes 589824 | tf_op jit(solution)/shard_map/broadcast_in_dim | solution.py:287
  1.6 7.3 %all-to-all-start = ((bf16[8,128,256]{2,1,0:T(8,128)(2,1)}), bf16[8,128,256]{2,1,0:T(8,128)(2,1)S(1)}, u32[]{:S(2)}, u32[]{:S(2)}) async-start(bf16[8,128,256]{2,1,0:T(8,128)(2,1)} %broadcast_in_dim.4), calls=%async_computation | async-start | bytes 1048576 | tf_op jit(solution)/shard_map/all_to_all | solution.py:290
  8.9 0.0 copy-start.2
  8.9 1.6 %copy-done.2 = bf16[2,2,64,4096]{3,2,1,0:T(8,128)(2,1)S(1)} copy-done((bf16[2,2,64,4096]{3,2,1,0:T(8,128)(2,1)S(1)}, bf16[2,2,64,4096]{3,2,1,0:T(8,128)(2,1)}, u32[]{:S(2)}) %copy-start.2) | copy-done | bytes 2097176
  10.5 0.0 copy-start.3
  10.5 1.6 %copy-done.3 = bf16[2,2,64,4096]{3,2,1,0:T(8,128)(2,1)S(1)} copy-done((bf16[2,2,64,4096]{3,2,1,0:T(8,128)(2,1)S(1)}, bf16[2,2,64,4096]{3,2,1,0:T(8,128)(2,1)}, u32[]{:S(2)}) %copy-start.3) | copy-done | bytes 2097176
  12.0 0.0 copy-start.4
  12.1 0.8 %copy-done.4 = bf16[4,4096]{1,0:T(4,128)(2,1)S(1)} copy-done((bf16[4,4096]{1,0:T(4,128)(2,1)S(1)}, bf16[4,4096]{1,0:T(4,128)(2,1)}, u32[]{:S(2)}) %copy-start.4) | copy-done | bytes 32792
  12.8 0.3 stage.1
  13.2 0.0 copy-start
  13.2 1.3 %copy-done = bf16[256,4096]{1,0:T(8,128)(2,1)} copy-done((bf16[256,4096]{1,0:T(8,128)(2,1)}, bf16[256,4096]{1,0:T(8,128)(2,1)S(1)}, u32[]{:S(2)}) %copy-start) | copy-done | bytes 2097176
  14.5 2.0 %collective-permute-start = (bf16[4,4096]{1,0:T(4,128)(2,1)S(1)}, bf16[4,4096]{1,0:T(4,128)(2,1)S(1)}, u32[]{:S(2)}, u32[]{:S(2)}) collective-permute-start(bf16[4,4096]{1,0:T(4,128)(2,1)S(1)} %get-tuple-element.15), channel_id=1, source_target_pairs={{0,4},{1,5},{2,6},{3,7},{4,0},{5,1},{6,2},{7,3},{8,12},{9,13},{10,... | collective-permute-start | bytes 98312 | tf_op jit(solution)/shard_map/ppermute | solution.py:284
  16.5 2.0 %collective-permute-done = bf16[4,4096]{1,0:T(4,128)(2,1)S(1)} collective-permute-done((bf16[4,4096]{1,0:T(4,128)(2,1)S(1)}, bf16[4,4096]{1,0:T(4,128)(2,1)S(1)}, u32[]{:S(2)}, u32[]{:S(2)}) %collective-permute-start) | collective-permute-done | bytes 32800 | tf_op jit(solution)/shard_map/ppermute | solution.py:284
  18.6 4.8 %all-to-all-done.own_ref = bf16[8,128,256]{2,1,0:T(8,128)(2,1)S(1)} async-done(((bf16[8,128,256]{2,1,0:T(8,128)(2,1)}), bf16[8,128,256]{2,1,0:T(8,128)(2,1)S(1)}, u32[]{:S(2)}, u32[]{:S(2)}) %all-to-all-start) | async-done | bytes 524320 | tf_op jit(solution)/shard_map/all_to_all | solution.py:290
  23.4 0.0 copy-start.1
  23.4 0.0 collective-permute-start.1
  23.4 0.2 collective-permute-start.4
  23.5 0.0 copy-start.5
  23.5 0.4 first_half.2.half_in_ref
  23.9 1.0 %copy-done.1 = bf16[256,4096]{1,0:T(8,128)(2,1)S(1)} copy-done((bf16[256,4096]{1,0:T(8,128)(2,1)S(1)}, bf16[256,4096]{1,0:T(8,128)(2,1)}, u32[]{:S(2)}) %copy-start.1) | copy-done | bytes 2097176
  24.9 0.4 first_half.3.half_out_ref
  25.4 0.0 collective-permute-done.1.other_ref
  25.4 0.0 copy-done.5
  25.4 1.5 %second_half.1 = (f32[24,128]{1,0:T(8,128)S(1)}, f32[24,128]{1,0:T(8,128)S(1)}, f32[64,128]{1,0:T(8,128)S(1)}) custom-call(s32[2,2]{1,0:T(2,128)S(1)} %copy-done.5, bf16[256,4096]{1,0:T(8,128)(2,1)S(1)} %get-tuple-element.13.x_ref.act_ref, bf16[256,4096]{1,0:T(8,128)(2,1)S(1)} %copy-done.1, bf16[8,128,256]{2,1,0:T(8,128)(2,1)S(1)} %collective-permute-done.1.other_ref, ...), custom_call_target="tpu_custom_call" | custom-call | flops 134217728 | bytes 4194304 | tf_op jit(solution)/shard_map/second_half/pallas_call | solution.py:334
  26.9 0.1 collective-permute-start.2
  27.0 1.2 %collective-permute-done.2 = f32[24,128]{1,0:T(8,128)S(1)} collective-permute-done((f32[24,128]{1,0:T(8,128)S(1)}, f32[24,128]{1,0:T(8,128)S(1)}, u32[]{:S(2)}, u32[]{:S(2)}) %collective-permute-start.2) | collective-permute-done | bytes 12320 | tf_op jit(solution)/shard_map/ppermute | solution.py:284
  28.2 0.6 %broadcast_in_dim.5 = f32[8,24,128]{2,1,0:T(8,128)} broadcast(f32[24,128]{1,0:T(8,128)S(1)} %add.3), dimensions={1,2} | broadcast | bytes 110592 | tf_op jit(solution)/shard_map/broadcast_in_dim | solution.py:287
  28.8 4.0 %all-to-all-start.1 = ((f32[8,24,128]{2,1,0:T(8,128)}), f32[8,24,128]{2,1,0:T(8,128)S(1)}, u32[]{:S(2)}, u32[]{:S(2)}) async-start(f32[8,24,128]{2,1,0:T(8,128)} %broadcast_in_dim.5), calls=%async_computation.1 | async-start | bytes 196608 | tf_op jit(solution)/shard_map/all_to_all | solution.py:290
  32.8 0.0 collective-permute-done.4
  32.8 2.1 %collective-permute-start.5 = (bf16[16,4096]{1,0:T(8,128)(2,1)S(1)}, bf16[16,4096]{1,0:T(8,128)(2,1)S(1)}, u32[]{:S(2)}, u32[]{:S(2)}) collective-permute-start(bf16[16,4096]{1,0:T(8,128)(2,1)S(1)} %constant_dynamic-update-slice_fusion.rest_0_), channel_id=1, source_target_pairs={{0,2},{1,3},{2,0},{3,1},{4,6},{5,7},{6,4},{7,5},{8,10},{9,11},{10,... | collective-permute-start | bytes 393224 | tf_op jit(solution)/shard_map/ppermute | solution.py:284
  34.9 0.0 collective-permute-start.6
  34.9 4.4 %collective-permute-done.5.rest_1_ = bf16[16,4096]{1,0:T(8,128)(2,1)S(1)} collective-permute-done((bf16[16,4096]{1,0:T(8,128)(2,1)S(1)}, bf16[16,4096]{1,0:T(8,128)(2,1)S(1)}, u32[]{:S(2)}, u32[]{:S(2)}) %collective-permute-start.5) | collective-permute-done | bytes 131104 | tf_op jit(solution)/shard_map/ppermute | solution.py:284
  39.2 0.0 collective-permute-start.7
  39.2 0.6 %all-to-all-done.1.blocks_ref = f32[8,24,128]{2,1,0:T(8,128)S(1)} async-done(((f32[8,24,128]{2,1,0:T(8,128)}), f32[8,24,128]{2,1,0:T(8,128)S(1)}, u32[]{:S(2)}, u32[]{:S(2)}) %all-to-all-start.1) | async-done | bytes 98336 | tf_op jit(solution)/shard_map/all_to_all | solution.py:290
  39.9 2.2 %invert.1.own_ref = f32[64,64]{1,0:T(8,128)S(1)} custom-call(f32[8,24,128]{2,1,0:T(8,128)S(1)} %all-to-all-done.1.blocks_ref), custom_call_target="tpu_custom_call" | custom-call | flops 1000000000 | bytes 16777216 | tf_op jit(solution)/shard_map/invert/pallas_call | solution.py:347
  42.1 0.0 collective-permute-start.3
  42.1 0.0 collective-permute-done.6.rest_2_
  42.1 0.0 collective-permute-done.7.rest_3_
  42.1 1.2 %collective-permute-done.3.other_ref = f32[64,64]{1,0:T(8,128)S(1)} collective-permute-done((f32[64,64]{1,0:T(8,128)S(1)}, f32[64,64]{1,0:T(8,128)S(1)}, u32[]{:S(2)}, u32[]{:S(2)}) %collective-permute-start.3) | collective-permute-done | bytes 16416 | tf_op jit(solution)/shard_map/ppermute | solution.py:284
  43.3 1.5 %score.1 = f32[2,64]{1,0:T(2,128)} custom-call(f32[64,64]{1,0:T(8,128)S(1)} %invert.1.own_ref, f32[64,64]{1,0:T(8,128)S(1)} %collective-permute-done.3.other_ref, f32[64,128]{1,0:T(8,128)S(1)} %get-tuple-element.19.sketch_ref, bf16[16,4096]{1,0:T(8,128)(2,1)S(1)} %constant_dynamic-update-slice_fusion.rest_0_, ...), custom_call_target="tpu_custom_call" | custom-call | tf_op jit(solution)/shard_map/score/pallas_call | solution.py:358
  (4 shorter events, 0.1 us)
Async XLA Ops:
  1.6 21.7 %all-to-all-start = ((bf16[8,128,256]{2,1,0:T(8,128)(2,1)}), bf16[8,128,256]{2,1,0:T(8,128)(2,1)S(1)}, u32[]{:S(2)}, u32[]{:S(2)}) async-start(bf16[8,128,256]{2,1,0:T(8,128)(2,1)} %broadcast_in_dim.4), calls=%async_computation | async-start | bytes 1048576 | tf_op jit(solution)/shard_map/all_to_all | solution.py:290
  8.9 1.6 %copy-start.2 = (bf16[2,2,64,4096]{3,2,1,0:T(8,128)(2,1)S(1)}, bf16[2,2,64,4096]{3,2,1,0:T(8,128)(2,1)}, u32[]{:S(2)}) copy-start(bf16[2,2,64,4096]{3,2,1,0:T(8,128)(2,1)} %param.6) | copy-start | bytes 6291460
  10.5 1.6 %copy-start.3 = (bf16[2,2,64,4096]{3,2,1,0:T(8,128)(2,1)S(1)}, bf16[2,2,64,4096]{3,2,1,0:T(8,128)(2,1)}, u32[]{:S(2)}) copy-start(bf16[2,2,64,4096]{3,2,1,0:T(8,128)(2,1)} %param.7) | copy-start | bytes 6291460
  12.0 0.8 %copy-start.4 = (bf16[4,4096]{1,0:T(4,128)(2,1)S(1)}, bf16[4,4096]{1,0:T(4,128)(2,1)}, u32[]{:S(2)}) copy-start(bf16[4,4096]{1,0:T(4,128)(2,1)} %refs_2_.1) | copy-start | bytes 98308
  13.2 1.3 %copy-start = (bf16[256,4096]{1,0:T(8,128)(2,1)}, bf16[256,4096]{1,0:T(8,128)(2,1)S(1)}, u32[]{:S(2)}) copy-start(bf16[256,4096]{1,0:T(8,128)(2,1)S(1)} %get-tuple-element.14.x_ref.grad_ref) | copy-start | bytes 6291460
  14.5 4.0 %collective-permute-start = (bf16[4,4096]{1,0:T(4,128)(2,1)S(1)}, bf16[4,4096]{1,0:T(4,128)(2,1)S(1)}, u32[]{:S(2)}, u32[]{:S(2)}) collective-permute-start(bf16[4,4096]{1,0:T(4,128)(2,1)S(1)} %get-tuple-element.15), channel_id=1, source_target_pairs={{0,4},{1,5},{2,6},{3,7},{4,0},{5,1},{6,2},{7,3},{8,12},{9,13},{10,... | collective-permute-start | bytes 98312 | tf_op jit(solution)/shard_map/ppermute | solution.py:284
  23.4 1.6 %copy-start.1 = (bf16[256,4096]{1,0:T(8,128)(2,1)S(1)}, bf16[256,4096]{1,0:T(8,128)(2,1)}, u32[]{:S(2)}) copy-start(bf16[256,4096]{1,0:T(8,128)(2,1)} %copy-done) | copy-start | bytes 6291460
  23.4 2.0 %collective-permute-start.1 = (bf16[8,128,256]{2,1,0:T(8,128)(2,1)S(1)}, bf16[8,128,256]{2,1,0:T(8,128)(2,1)S(1)}, u32[]{:S(2)}, u32[]{:S(2)}) collective-permute-start(bf16[8,128,256]{2,1,0:T(8,128)(2,1)S(1)} %all-to-all-done.own_ref), channel_id=1, source_target_pairs={{0,1},{1,0},{2,3},{3,2},{4,5},{5,4},{6,7},{7,6},{8,9},{9,8},{10,11... | collective-permute-start | bytes 1572872 | tf_op jit(solution)/shard_map/ppermute | solution.py:284
  23.4 9.4 %collective-permute-start.4 = (bf16[8,4096]{1,0:T(8,128)(2,1)S(1)}, bf16[8,4096]{1,0:T(8,128)(2,1)S(1)}, u32[]{:S(2)}, u32[]{:S(2)}) collective-permute-start(bf16[8,4096]{1,0:T(8,128)(2,1)S(1)} %pad_maximum_fusion), channel_id=1, source_target_pairs={{0,8},{1,9},{2,10},{3,11},{4,12},{5,13},{6,14},{7,15},{8,0},{9,1},... | collective-permute-start | bytes 196616 | tf_op jit(solution)/shard_map/ppermute | solution.py:284
  23.5 1.9 %copy-start.5 = (s32[2,2]{1,0:T(2,128)S(1)}, s32[2,2]{1,0:T(2,128)}, u32[]{:S(2)}) copy-start(s32[2,2]{1,0:T(2,128)} %lengths_ref.1) | copy-start | bytes 52
  26.9 1.2 %collective-permute-start.2 = (f32[24,128]{1,0:T(8,128)S(1)}, f32[24,128]{1,0:T(8,128)S(1)}, u32[]{:S(2)}, u32[]{:S(2)}) collective-permute-start(f32[24,128]{1,0:T(8,128)S(1)} %get-tuple-element.18), channel_id=1, source_target_pairs={{0,1},{1,0},{2,3},{3,2},{4,5},{5,4},{6,7},{7,6},{8,9},{9,8},{10,11... | collective-permute-start | bytes 36872 | tf_op jit(solution)/shard_map/ppermute | solution.py:284
  28.8 11.1 %all-to-all-start.1 = ((f32[8,24,128]{2,1,0:T(8,128)}), f32[8,24,128]{2,1,0:T(8,128)S(1)}, u32[]{:S(2)}, u32[]{:S(2)}) async-start(f32[8,24,128]{2,1,0:T(8,128)} %broadcast_in_dim.5), calls=%async_computation.1 | async-start | bytes 196608 | tf_op jit(solution)/shard_map/all_to_all | solution.py:290
  32.8 6.5 %collective-permute-start.5 = (bf16[16,4096]{1,0:T(8,128)(2,1)S(1)}, bf16[16,4096]{1,0:T(8,128)(2,1)S(1)}, u32[]{:S(2)}, u32[]{:S(2)}) collective-permute-start(bf16[16,4096]{1,0:T(8,128)(2,1)S(1)} %constant_dynamic-update-slice_fusion.rest_0_), channel_id=1, source_target_pairs={{0,2},{1,3},{2,0},{3,1},{4,6},{5,7},{6,4},{7,5},{8,10},{9,11},{10,... | collective-permute-start | bytes 393224 | tf_op jit(solution)/shard_map/ppermute | solution.py:284
  34.9 7.3 %collective-permute-start.6 = (bf16[16,4096]{1,0:T(8,128)(2,1)S(1)}, bf16[16,4096]{1,0:T(8,128)(2,1)S(1)}, u32[]{:S(2)}, u32[]{:S(2)}) collective-permute-start(bf16[16,4096]{1,0:T(8,128)(2,1)S(1)} %constant_dynamic-update-slice_fusion.rest_0_), channel_id=1, source_target_pairs={{0,1},{1,0},{2,3},{3,2},{4,5},{5,4},{6,7},{7,6},{8,9},{9,8},{10,11... | collective-permute-start | bytes 393224 | tf_op jit(solution)/shard_map/ppermute | solution.py:284
  39.2 2.9 %collective-permute-start.7 = (bf16[16,4096]{1,0:T(8,128)(2,1)S(1)}, bf16[16,4096]{1,0:T(8,128)(2,1)S(1)}, u32[]{:S(2)}, u32[]{:S(2)}) collective-permute-start(bf16[16,4096]{1,0:T(8,128)(2,1)S(1)} %collective-permute-done.5.rest_1_), channel_id=1, source_target_pairs={{0,1},{1,0},{2,3},{3,2},{4,5},{5,4},{6,7},{7,6},{8,9},{9,8},{10,11... | collective-permute-start | bytes 393224 | tf_op jit(solution)/shard_map/ppermute | solution.py:284
  42.1 1.2 %collective-permute-start.3 = (f32[64,64]{1,0:T(8,128)S(1)}, f32[64,64]{1,0:T(8,128)S(1)}, u32[]{:S(2)}, u32[]{:S(2)}) collective-permute-start(f32[64,64]{1,0:T(8,128)S(1)} %invert.1.own_ref), channel_id=1, source_target_pairs={{0,1},{1,0},{2,3},{3,2},{4,5},{5,4},{6,7},{7,6},{8,9},{9,8},{10,11... | collective-permute-start | bytes 49160 | tf_op jit(solution)/shard_map/ppermute | solution.py:284

commit v5 on v4

--- a/solution.py
+++ b/solution.py
@@ -91,7 +91,8 @@
 
 def second_half_kernel(
     split_cores,
-    lengths_ref,
+    live_ref,
+    count_ref,
     act_ref,
     grad_ref,
     other_ref,
@@ -102,38 +103,31 @@
     sketch_ref,
 ):
     place = 1 - own_place(split_cores)
-    sequences = 2 * lengths_ref.shape[0]
-    length_of = [lengths_ref[s // 2, s % 2] for s in range(sequences)]
-    pairs = sequences // 2
     rows, rank = half_in_ref.shape
-    seq = rows // sequences
-    token = lax.broadcasted_iota(jnp.int32, (seq, rank), 0)
-
-    def masked(total):
-        kept = []
-        for s in range(sequences):
-            live = token < length_of[s]
-            kept.append(jnp.where(live, total[s * seq : (s + 1) * seq], 0.0))
-        return kept
-
-    count = functools.reduce(lambda a, b: a + b, length_of)
+    pairs = sketch_ref.shape[1] // rank
+    seq = rows // (2 * pairs)
+    live = live_ref[...] > 0.0
     slot, _, _ = packed_places(keep_ref.shape)
 
     def factor(rows_of):
         packed = packed_symmetric(contract_first(rows_of, rows_of))
-        return jnp.where(slot, count.astype(F32), packed)
+        return jnp.where(slot, count_ref[...], packed)
 
     total_in = projected(act_ref, other_ref, 0, rank, place, half_in_ref[...])
     total_out = projected(grad_ref, other_ref, rank, rank, place, half_out_ref[...])
-    inner = jnp.concatenate(masked(total_in), 0).astype(BF16)
-    outer_parts = masked(total_out)
+    inner = jnp.where(live, total_in, 0.0).astype(BF16)
+    outer = jnp.where(live, total_out, 0.0)
     factor_in = factor(inner)
-    factor_out = factor(jnp.concatenate(outer_parts, 0).astype(BF16))
+    factor_out = factor(outer.astype(BF16))
     first_core = lax.axis_index("dp") % 2 == 0
     keep_ref[...] = jnp.where(first_core, factor_in, factor_out)
     send_ref[...] = jnp.where(first_core, factor_out, factor_in)
     signed = jnp.concatenate(
-        [-part if s % 2 else part for s, part in enumerate(outer_parts)], 0
+        [
+            -outer[s * seq : (s + 1) * seq] if s % 2 else outer[s * seq : (s + 1) * seq]
+            for s in range(2 * pairs)
+        ],
+        0,
     ).astype(BF16)
     sketches = []
     for p in range(pairs):
@@ -142,30 +136,39 @@
     sketch_ref[...] = jnp.concatenate(sketches, 1)
 
 
-def stage_kernel(*refs):
+def stage_kernel(lengths_ref, *refs):
+    *refs, live_ref, count_ref, arrived = refs
     count = len(refs) // 2
-    arrived = refs[-1]
     copies = [
         pltpu.make_async_copy(refs[i], refs[count + i], arrived.at[i]) for i in range(count)
     ]
     for copy in copies:
         copy.start()
+    pairs, responses = lengths_ref.shape
+    seq = live_ref.shape[0] // (pairs * responses)
+    token = lax.broadcasted_iota(jnp.int32, (seq, live_ref.shape[1]), 0)
+    tokens = 0
+    for s in range(pairs * responses):
+        length = lengths_ref[s // responses, s % responses]
+        live_ref[s * seq : (s + 1) * seq, :] = jnp.where(token < length, 1.0, 0.0)
+        tokens += length
+    count_ref[...] = jnp.full(count_ref.shape, tokens, jnp.int32).astype(F32)
     for copy in copies:
         copy.wait()
 
 
-def staged(*arrays):
-    count = len(arrays)
+def staged(lengths, live, count, *arrays):
     return pl.pallas_call(
         stage_kernel,
-        out_shape=tuple(jax.ShapeDtypeStruct(a.shape, a.dtype) for a in arrays),
-        in_specs=[whole(pl.ANY)] * count,
-        out_specs=(whole(pl.ANY),) * count,
-        scratch_shapes=[pltpu.SemaphoreType.DMA((count,))],
+        out_shape=tuple(jax.ShapeDtypeStruct(a.shape, a.dtype) for a in arrays)
+        + (jax.ShapeDtypeStruct(live, F32), jax.ShapeDtypeStruct(count, F32)),
+        in_specs=[whole(SMEM)] + [whole(pl.ANY)] * len(arrays),
+        out_specs=(whole(pl.ANY),) * len(arrays) + (whole(), whole()),
+        scratch_shapes=[pltpu.SemaphoreType.DMA((len(arrays),))],
         compiler_params=params(1),
         cost_estimate=pl.CostEstimate(flops=0, bytes_accessed=2**22, transcendentals=0),
         name="stage",
-    )(*arrays)
+    )(lengths, *arrays)
 
 
 def gauss_jordan(tiles, width, group):
@@ -293,8 +296,14 @@
         return jnp.concatenate([block, swap(block, bit)], 0)
 
     rows = 2 * pairs * seq
-    flat_in, flat_out, near = staged(
-        activations.reshape(rows, depth), out_grads.reshape(rows, depth), eval_sketches
+    packed = jax.ShapeDtypeStruct((3 * rank // 8, 2 * rank), F32)
+    flat_in, flat_out, near, live, count = staged(
+        lengths,
+        (rows, rank),
+        packed.shape,
+        activations.reshape(rows, depth),
+        out_grads.reshape(rows, depth),
+        eval_sketches,
     )
     near = doubled(near, first)
     mine = jnp.concatenate([proj_in, proj_out], 1).T
@@ -330,18 +339,17 @@
 
     half_in = first_half(flat_in, 0)
     half_out = first_half(flat_out, rank)
-    packed = jax.ShapeDtypeStruct((3 * rank // 8, 2 * rank), F32)
     keep, send, sketch = pl.pallas_call(
         functools.partial(second_half_kernel, split_cores),
         out_shape=(packed, packed, jax.ShapeDtypeStruct((rank, pairs * rank), F32)),
-        in_specs=[whole(SMEM)] + [whole()] * 5,
+        in_specs=[whole()] * 7,
         out_specs=(whole(),) * 3,
         compiler_params=params(8),
         cost_estimate=pl.CostEstimate(
             flops=2 * rows * depth * rank, bytes_accessed=4 * rows * depth, transcendentals=0
         ),
         name="second_half",
-    )(lengths, flat_in, flat_out, other, half_in, half_out)
+    )(live, count, flat_in, flat_out, other, half_in, half_out)
     sums = copies_of(keep + swap(send, 1))
     blocks = to_all_chips(sums)
     inverse = pl.pallas_call(

time: 45.3 us -> 44.8 us (0.989)
  waiting for transfers between devices: 14.1 us -> 12.9 us
  local copies, waits for them, and re-layouts: 7.78 us -> 8.45 us
    all_to_all x2, waiting for transfers between devices: 5.42 us -> 3.95 us  [to_all_chips(): return lax.all_to_all(copies, 'dp', 0, 0, axis_index_groups=same_core)]
    unnamed x13, local copies, waits for them, and re-layouts: 6.29 us -> 6.97 us
    pallas_call x1, Pallas kernels: 0.35 us -> 0.92 us  [staged(): pl.pallas_call(stage_kernel, out_shape=tuple((jax.ShapeDtypeStruct(a.shap...]
    pallas_call x1, Pallas kernels: 1.51 us -> 0.97 us  [on_device(): pl.pallas_call(functools.partial(second_half_kernel, split_cores), out_sh...]
where the time goes in v5:
time: 44.8 us; the launch traced here: 44.2 us
  starting transfers between devices  15.6 us (35%)
  waiting for transfers between devices  12.9 us (29%)
  local copies, waits for them, and re-layouts  8.45 us (19%)
  Pallas kernels  6.38 us (14%)
  other arithmetic  0.82 us (2%)
    all_to_all x2, starting transfers between devices, to_all_chips(): return lax.all_to_all(copies, 'dp', 0, 0, axis_index_groups=same_core)  11.2 us
    ppermute x8, waiting for transfers between devices, swap(): return lax.ppermute(block, 'dp', [(d, d ^ bit) for d in range(devices)])  8.94 us
    unnamed x13, local copies, waits for them, and re-layouts  6.97 us
    ppermute x8, starting transfers between devices, swap(): return lax.ppermute(block, 'dp', [(d, d ^ bit) for d in range(devices)])  4.38 us
    all_to_all x2, waiting for transfers between devices, to_all_chips(): return lax.all_to_all(copies, 'dp', 0, 0, axis_index_groups=same_core)  3.95 us
    pallas_call x1, Pallas kernels, on_device(): pl.pallas_call(invert_kernel, out_shape=jax.ShapeDtypeStruct((rank, rank)...  2.2 us
    broadcast_in_dim x2, local copies, waits for them, and re-layouts, copies_of(): return jnp.broadcast_to(block[None], (chips,) + block.shape)  1.48 us
    pallas_call x1, Pallas kernels, on_device(): pl.pallas_call(functools.partial(score_kernel, bits), out_shape=jax.Shape...  1.47 us
  transfers between devices with their start and end apart: 10, of which 6 were waited for; matrix products, arithmetic and copies ran while one was open for 2% of the time, Pallas kernels for 11%

profile of v5, /device:TPU:0, one launch (start us, length us, event | category | flops | bytes accessed | tf_op | source)
XLA Modules:
  0.0 44.2 jit_solution(6992544610657283289)
XLA Ops:
  0.0 0.8 %maximum_bitcast_fusion = bf16[128,256]{1,0:T(8,128)(2,1)S(1)} fusion(bf16[256,64]{0,1:T(8,128)(2,1)} %param.10, bf16[256,64]{0,1:T(8,128)(2,1)} %param.9), kind=kLoop, calls=%fused_computation | loop fusion | flops 131072 | bytes 131072 | tf_op jit(solution)/shard_map/transpose | solution.py:309
  0.8 0.8 %broadcast_in_dim.4 = bf16[8,128,256]{2,1,0:T(8,128)(2,1)} broadcast(bf16[128,256]{1,0:T(8,128)(2,1)S(1)} %maximum_bitcast_fusion), dimensions={1,2} | broadcast | bytes 589824 | tf_op jit(solution)/shard_map/broadcast_in_dim | solution.py:290
  1.6 7.3 %all-to-all-start = ((bf16[8,128,256]{2,1,0:T(8,128)(2,1)}), bf16[8,128,256]{2,1,0:T(8,128)(2,1)S(1)}, u32[]{:S(2)}, u32[]{:S(2)}) async-start(bf16[8,128,256]{2,1,0:T(8,128)(2,1)} %broadcast_in_dim.4), calls=%async_computation | async-start | bytes 1048576 | tf_op jit(solution)/shard_map/all_to_all | solution.py:293
  8.9 0.0 copy-start.2
  8.9 1.6 %copy-done.2 = bf16[2,2,64,4096]{3,2,1,0:T(8,128)(2,1)S(1)} copy-done((bf16[2,2,64,4096]{3,2,1,0:T(8,128)(2,1)S(1)}, bf16[2,2,64,4096]{3,2,1,0:T(8,128)(2,1)}, u32[]{:S(2)}) %copy-start.2) | copy-done | bytes 2097176
  10.5 0.0 copy-start.3
  10.5 1.6 %copy-done.3 = bf16[2,2,64,4096]{3,2,1,0:T(8,128)(2,1)S(1)} copy-done((bf16[2,2,64,4096]{3,2,1,0:T(8,128)(2,1)S(1)}, bf16[2,2,64,4096]{3,2,1,0:T(8,128)(2,1)}, u32[]{:S(2)}) %copy-start.3) | copy-done | bytes 2097176
  12.0 0.0 copy-start.4
  12.1 0.8 %copy-done.4 = bf16[4,4096]{1,0:T(4,128)(2,1)S(1)} copy-done((bf16[4,4096]{1,0:T(4,128)(2,1)S(1)}, bf16[4,4096]{1,0:T(4,128)(2,1)}, u32[]{:S(2)}) %copy-start.4) | copy-done | bytes 32792
  12.8 0.0 copy-start.5
  12.8 0.7 %copy-done.5 = s32[2,2]{1,0:T(2,128)S(1)} copy-done((s32[2,2]{1,0:T(2,128)S(1)}, s32[2,2]{1,0:T(2,128)}, u32[]{:S(2)}) %copy-start.5) | copy-done | bytes 40
  13.5 0.9 %stage.1 = (bf16[256,4096]{1,0:T(8,128)(2,1)S(1)}, bf16[256,4096]{1,0:T(8,128)(2,1)S(1)}, bf16[4,4096]{1,0:T(4,128)(2,1)S(1)}, f32[256,64]{1,0:T(8,128)S(1)}, f32[24,128]{1,0:T(8,128)S(1)}) custom-call(s32[2,2]{1,0:T(2,128)S(1)} %copy-done.5, bf16[256,4096]{1,0:T(8,128)(2,1)S(1)} %bitcast.4, bf16[256,4096]{1,0:T(8,128)(2,1)S(1)} %bitcast.5, ...), custom_call_target="tpu_custom_call" | custom-call | bytes 4194304 | tf_op jit(solution)/shard_map/stage/pallas_call | solution.py:161
  14.4 0.0 copy-start
  14.4 1.3 %copy-done = bf16[256,4096]{1,0:T(8,128)(2,1)} copy-done((bf16[256,4096]{1,0:T(8,128)(2,1)}, bf16[256,4096]{1,0:T(8,128)(2,1)S(1)}, u32[]{:S(2)}) %copy-start) | copy-done | bytes 2097176
  15.8 2.0 %collective-permute-start = (bf16[4,4096]{1,0:T(4,128)(2,1)S(1)}, bf16[4,4096]{1,0:T(4,128)(2,1)S(1)}, u32[]{:S(2)}, u32[]{:S(2)}) collective-permute-start(bf16[4,4096]{1,0:T(4,128)(2,1)S(1)} %get-tuple-element.19), channel_id=1, source_target_pairs={{0,4},{1,5},{2,6},{3,7},{4,0},{5,1},{6,2},{7,3},{8,12},{9,13},{10,... | collective-permute-start | bytes 98312 | tf_op jit(solution)/shard_map/ppermute | solution.py:287
  17.8 2.2 %collective-permute-done = bf16[4,4096]{1,0:T(4,128)(2,1)S(1)} collective-permute-done((bf16[4,4096]{1,0:T(4,128)(2,1)S(1)}, bf16[4,4096]{1,0:T(4,128)(2,1)S(1)}, u32[]{:S(2)}, u32[]{:S(2)}) %collective-permute-start) | collective-permute-done | bytes 32800 | tf_op jit(solution)/shard_map/ppermute | solution.py:287
  20.1 3.3 %all-to-all-done.own_ref = bf16[8,128,256]{2,1,0:T(8,128)(2,1)S(1)} async-done(((bf16[8,128,256]{2,1,0:T(8,128)(2,1)}), bf16[8,128,256]{2,1,0:T(8,128)(2,1)S(1)}, u32[]{:S(2)}, u32[]{:S(2)}) %all-to-all-start) | async-done | bytes 524320 | tf_op jit(solution)/shard_map/all_to_all | solution.py:293
  23.4 0.0 copy-start.1
  23.4 0.0 collective-permute-start.1
  23.4 0.2 collective-permute-start.4
  23.5 0.4 first_half.2.half_in_ref
  23.9 1.0 %copy-done.1 = bf16[256,4096]{1,0:T(8,128)(2,1)S(1)} copy-done((bf16[256,4096]{1,0:T(8,128)(2,1)S(1)}, bf16[256,4096]{1,0:T(8,128)(2,1)}, u32[]{:S(2)}) %copy-start.1) | copy-done | bytes 2097176
  24.9 0.4 first_half.3.half_out_ref
  25.4 0.0 collective-permute-done.1.other_ref
  25.4 1.0 %second_half.1 = (f32[24,128]{1,0:T(8,128)S(1)}, f32[24,128]{1,0:T(8,128)S(1)}, f32[64,128]{1,0:T(8,128)S(1)}) custom-call(f32[256,64]{1,0:T(8,128)S(1)} %get-tuple-element.15.live_ref, f32[24,128]{1,0:T(8,128)S(1)} %get-tuple-element.16.count_ref, bf16[256,4096]{1,0:T(8,128)(2,1)S(1)} %get-tuple-element.17.x_ref.act_ref, bf16[256,4096]{1,0:T(8,128)(2,1)S(1)} %copy-done.1, ...), custom_call_target="tpu_custom_call" | custom-call | flops 134217728 | bytes 4194304 | tf_op jit(solution)/shard_map/second_half/pallas_call | solution.py:342
  26.4 0.1 collective-permute-start.2
  26.4 1.2 %collective-permute-done.2 = f32[24,128]{1,0:T(8,128)S(1)} collective-permute-done((f32[24,128]{1,0:T(8,128)S(1)}, f32[24,128]{1,0:T(8,128)S(1)}, u32[]{:S(2)}, u32[]{:S(2)}) %collective-permute-start.2) | collective-permute-done | bytes 12320 | tf_op jit(solution)/shard_map/ppermute | solution.py:287
  27.6 0.6 %broadcast_in_dim.5 = f32[8,24,128]{2,1,0:T(8,128)} broadcast(f32[24,128]{1,0:T(8,128)S(1)} %add.3), dimensions={1,2} | broadcast | bytes 110592 | tf_op jit(solution)/shard_map/broadcast_in_dim | solution.py:290
  28.2 3.9 %all-to-all-start.1 = ((f32[8,24,128]{2,1,0:T(8,128)}), f32[8,24,128]{2,1,0:T(8,128)S(1)}, u32[]{:S(2)}, u32[]{:S(2)}) async-start(f32[8,24,128]{2,1,0:T(8,128)} %broadcast_in_dim.5), calls=%async_computation.1 | async-start | bytes 196608 | tf_op jit(solution)/shard_map/all_to_all | solution.py:293
  32.2 0.0 collective-permute-done.4
  32.2 2.1 %collective-permute-start.5 = (bf16[16,4096]{1,0:T(8,128)(2,1)S(1)}, bf16[16,4096]{1,0:T(8,128)(2,1)S(1)}, u32[]{:S(2)}, u32[]{:S(2)}) collective-permute-start(bf16[16,4096]{1,0:T(8,128)(2,1)S(1)} %constant_dynamic-update-slice_fusion.rest_0_), channel_id=1, source_target_pairs={{0,2},{1,3},{2,0},{3,1},{4,6},{5,7},{6,4},{7,5},{8,10},{9,11},{10,... | collective-permute-start | bytes 393224 | tf_op jit(solution)/shard_map/ppermute | solution.py:287
  34.3 0.0 collective-permute-start.6
  34.3 4.4 %collective-permute-done.5.rest_1_ = bf16[16,4096]{1,0:T(8,128)(2,1)S(1)} collective-permute-done((bf16[16,4096]{1,0:T(8,128)(2,1)S(1)}, bf16[16,4096]{1,0:T(8,128)(2,1)S(1)}, u32[]{:S(2)}, u32[]{:S(2)}) %collective-permute-start.5) | collective-permute-done | bytes 131104 | tf_op jit(solution)/shard_map/ppermute | solution.py:287
  38.7 0.0 collective-permute-start.7
  38.7 0.6 %all-to-all-done.1.blocks_ref = f32[8,24,128]{2,1,0:T(8,128)S(1)} async-done(((f32[8,24,128]{2,1,0:T(8,128)}), f32[8,24,128]{2,1,0:T(8,128)S(1)}, u32[]{:S(2)}, u32[]{:S(2)}) %all-to-all-start.1) | async-done | bytes 98336 | tf_op jit(solution)/shard_map/all_to_all | solution.py:293
  39.3 2.2 %invert.1.own_ref = f32[64,64]{1,0:T(8,128)S(1)} custom-call(f32[8,24,128]{2,1,0:T(8,128)S(1)} %all-to-all-done.1.blocks_ref), custom_call_target="tpu_custom_call" | custom-call | flops 1000000000 | bytes 16777216 | tf_op jit(solution)/shard_map/invert/pallas_call | solution.py:355
  41.5 0.0 collective-permute-start.3
  41.6 0.0 collective-permute-done.6.rest_2_
  41.6 0.0 collective-permute-done.7.rest_3_
  41.6 1.2 %collective-permute-done.3.other_ref = f32[64,64]{1,0:T(8,128)S(1)} collective-permute-done((f32[64,64]{1,0:T(8,128)S(1)}, f32[64,64]{1,0:T(8,128)S(1)}, u32[]{:S(2)}, u32[]{:S(2)}) %collective-permute-start.3) | collective-permute-done | bytes 16416 | tf_op jit(solution)/shard_map/ppermute | solution.py:287
  42.8 1.5 %score.1 = f32[2,64]{1,0:T(2,128)} custom-call(f32[64,64]{1,0:T(8,128)S(1)} %invert.1.own_ref, f32[64,64]{1,0:T(8,128)S(1)} %collective-permute-done.3.other_ref, f32[64,128]{1,0:T(8,128)S(1)} %get-tuple-element.23.sketch_ref, bf16[16,4096]{1,0:T(8,128)(2,1)S(1)} %constant_dynamic-update-slice_fusion.rest_0_, ...), custom_call_target="tpu_custom_call" | custom-call | tf_op jit(solution)/shard_map/score/pallas_call | solution.py:366
  (4 shorter events, 0.1 us)
Async XLA Ops:
  1.6 21.7 %all-to-all-start = ((bf16[8,128,256]{2,1,0:T(8,128)(2,1)}), bf16[8,128,256]{2,1,0:T(8,128)(2,1)S(1)}, u32[]{:S(2)}, u32[]{:S(2)}) async-start(bf16[8,128,256]{2,1,0:T(8,128)(2,1)} %broadcast_in_dim.4), calls=%async_computation | async-start | bytes 1048576 | tf_op jit(solution)/shard_map/all_to_all | solution.py:293
  8.9 1.6 %copy-start.2 = (bf16[2,2,64,4096]{3,2,1,0:T(8,128)(2,1)S(1)}, bf16[2,2,64,4096]{3,2,1,0:T(8,128)(2,1)}, u32[]{:S(2)}) copy-start(bf16[2,2,64,4096]{3,2,1,0:T(8,128)(2,1)} %param.6) | copy-start | bytes 6291460
  10.5 1.6 %copy-start.3 = (bf16[2,2,64,4096]{3,2,1,0:T(8,128)(2,1)S(1)}, bf16[2,2,64,4096]{3,2,1,0:T(8,128)(2,1)}, u32[]{:S(2)}) copy-start(bf16[2,2,64,4096]{3,2,1,0:T(8,128)(2,1)} %param.7) | copy-start | bytes 6291460
  12.0 0.8 %copy-start.4 = (bf16[4,4096]{1,0:T(4,128)(2,1)S(1)}, bf16[4,4096]{1,0:T(4,128)(2,1)}, u32[]{:S(2)}) copy-start(bf16[4,4096]{1,0:T(4,128)(2,1)} %refs_2_.1) | copy-start | bytes 98308
  12.8 0.7 %copy-start.5 = (s32[2,2]{1,0:T(2,128)S(1)}, s32[2,2]{1,0:T(2,128)}, u32[]{:S(2)}) copy-start(s32[2,2]{1,0:T(2,128)} %lengths_ref.1) | copy-start | bytes 52
  14.4 1.3 %copy-start = (bf16[256,4096]{1,0:T(8,128)(2,1)}, bf16[256,4096]{1,0:T(8,128)(2,1)S(1)}, u32[]{:S(2)}) copy-start(bf16[256,4096]{1,0:T(8,128)(2,1)S(1)} %get-tuple-element.18.x_ref.grad_ref) | copy-start | bytes 6291460
  15.8 4.3 %collective-permute-start = (bf16[4,4096]{1,0:T(4,128)(2,1)S(1)}, bf16[4,4096]{1,0:T(4,128)(2,1)S(1)}, u32[]{:S(2)}, u32[]{:S(2)}) collective-permute-start(bf16[4,4096]{1,0:T(4,128)(2,1)S(1)} %get-tuple-element.19), channel_id=1, source_target_pairs={{0,4},{1,5},{2,6},{3,7},{4,0},{5,1},{6,2},{7,3},{8,12},{9,13},{10,... | collective-permute-start | bytes 98312 | tf_op jit(solution)/shard_map/ppermute | solution.py:287
  23.4 1.6 %copy-start.1 = (bf16[256,4096]{1,0:T(8,128)(2,1)S(1)}, bf16[256,4096]{1,0:T(8,128)(2,1)}, u32[]{:S(2)}) copy-start(bf16[256,4096]{1,0:T(8,128)(2,1)} %copy-done) | copy-start | bytes 6291460
  23.4 2.0 %collective-permute-start.1 = (bf16[8,128,256]{2,1,0:T(8,128)(2,1)S(1)}, bf16[8,128,256]{2,1,0:T(8,128)(2,1)S(1)}, u32[]{:S(2)}, u32[]{:S(2)}) collective-permute-start(bf16[8,128,256]{2,1,0:T(8,128)(2,1)S(1)} %all-to-all-done.own_ref), channel_id=1, source_target_pairs={{0,1},{1,0},{2,3},{3,2},{4,5},{5,4},{6,7},{7,6},{8,9},{9,8},{10,11... | collective-permute-start | bytes 1572872 | tf_op jit(solution)/shard_map/ppermute | solution.py:287
  23.4 8.8 %collective-permute-start.4 = (bf16[8,4096]{1,0:T(8,128)(2,1)S(1)}, bf16[8,4096]{1,0:T(8,128)(2,1)S(1)}, u32[]{:S(2)}, u32[]{:S(2)}) collective-permute-start(bf16[8,4096]{1,0:T(8,128)(2,1)S(1)} %pad_maximum_fusion), channel_id=1, source_target_pairs={{0,8},{1,9},{2,10},{3,11},{4,12},{5,13},{6,14},{7,15},{8,0},{9,1},... | collective-permute-start | bytes 196616 | tf_op jit(solution)/shard_map/ppermute | solution.py:287
  26.4 1.2 %collective-permute-start.2 = (f32[24,128]{1,0:T(8,128)S(1)}, f32[24,128]{1,0:T(8,128)S(1)}, u32[]{:S(2)}, u32[]{:S(2)}) collective-permute-start(f32[24,128]{1,0:T(8,128)S(1)} %get-tuple-element.22), channel_id=1, source_target_pairs={{0,1},{1,0},{2,3},{3,2},{4,5},{5,4},{6,7},{7,6},{8,9},{9,8},{10,11... | collective-permute-start | bytes 36872 | tf_op jit(solution)/shard_map/ppermute | solution.py:287
  28.2 11.1 %all-to-all-start.1 = ((f32[8,24,128]{2,1,0:T(8,128)}), f32[8,24,128]{2,1,0:T(8,128)S(1)}, u32[]{:S(2)}, u32[]{:S(2)}) async-start(f32[8,24,128]{2,1,0:T(8,128)} %broadcast_in_dim.5), calls=%async_computation.1 | async-start | bytes 196608 | tf_op jit(solution)/shard_map/all_to_all | solution.py:293
  32.2 6.5 %collective-permute-start.5 = (bf16[16,4096]{1,0:T(8,128)(2,1)S(1)}, bf16[16,4096]{1,0:T(8,128)(2,1)S(1)}, u32[]{:S(2)}, u32[]{:S(2)}) collective-permute-start(bf16[16,4096]{1,0:T(8,128)(2,1)S(1)} %constant_dynamic-update-slice_fusion.rest_0_), channel_id=1, source_target_pairs={{0,2},{1,3},{2,0},{3,1},{4,6},{5,7},{6,4},{7,5},{8,10},{9,11},{10,... | collective-permute-start | bytes 393224 | tf_op jit(solution)/shard_map/ppermute | solution.py:287
  34.3 7.3 %collective-permute-start.6 = (bf16[16,4096]{1,0:T(8,128)(2,1)S(1)}, bf16[16,4096]{1,0:T(8,128)(2,1)S(1)}, u32[]{:S(2)}, u32[]{:S(2)}) collective-permute-start(bf16[16,4096]{1,0:T(8,128)(2,1)S(1)} %constant_dynamic-update-slice_fusion.rest_0_), channel_id=1, source_target_pairs={{0,1},{1,0},{2,3},{3,2},{4,5},{5,4},{6,7},{7,6},{8,9},{9,8},{10,11... | collective-permute-start | bytes 393224 | tf_op jit(solution)/shard_map/ppermute | solution.py:287
  38.7 2.9 %collective-permute-start.7 = (bf16[16,4096]{1,0:T(8,128)(2,1)S(1)}, bf16[16,4096]{1,0:T(8,128)(2,1)S(1)}, u32[]{:S(2)}, u32[]{:S(2)}) collective-permute-start(bf16[16,4096]{1,0:T(8,128)(2,1)S(1)} %collective-permute-done.5.rest_1_), channel_id=1, source_target_pairs={{0,1},{1,0},{2,3},{3,2},{4,5},{5,4},{6,7},{7,6},{8,9},{9,8},{10,11... | collective-permute-start | bytes 393224 | tf_op jit(solution)/shard_map/ppermute | solution.py:287
  41.5 1.2 %collective-permute-start.3 = (f32[64,64]{1,0:T(8,128)S(1)}, f32[64,64]{1,0:T(8,128)S(1)}, u32[]{:S(2)}, u32[]{:S(2)}) collective-permute-start(f32[64,64]{1,0:T(8,128)S(1)} %invert.1.own_ref), channel_id=1, source_target_pairs={{0,1},{1,0},{2,3},{3,2},{4,5},{5,4},{6,7},{7,6},{8,9},{9,8},{10,11... | collective-permute-start | bytes 49160 | tf_op jit(solution)/shard_map/ppermute | solution.py:287

commit v6 on v5

--- a/solution.py
+++ b/solution.py
@@ -136,8 +136,8 @@
     sketch_ref[...] = jnp.concatenate(sketches, 1)
 
 
-def stage_kernel(lengths_ref, *refs):
-    *refs, live_ref, count_ref, arrived = refs
+def stage_kernel(lengths_ref, evals_ref, *refs):
+    *refs, live_ref, count_ref, same_evals_ref, arrived = refs
     count = len(refs) // 2
     copies = [
         pltpu.make_async_copy(refs[i], refs[count + i], arrived.at[i]) for i in range(count)
@@ -152,52 +152,70 @@
         length = lengths_ref[s // responses, s % responses]
         live_ref[s * seq : (s + 1) * seq, :] = jnp.where(token < length, 1.0, 0.0)
         tokens += length
+    same_evals_ref[...] = evals_ref[...]
     count_ref[...] = jnp.full(count_ref.shape, tokens, jnp.int32).astype(F32)
     for copy in copies:
         copy.wait()
 
 
-def staged(lengths, live, count, *arrays):
+def staged(lengths, evals, live, count, *arrays):
     return pl.pallas_call(
         stage_kernel,
         out_shape=tuple(jax.ShapeDtypeStruct(a.shape, a.dtype) for a in arrays)
-        + (jax.ShapeDtypeStruct(live, F32), jax.ShapeDtypeStruct(count, F32)),
-        in_specs=[whole(SMEM)] + [whole(pl.ANY)] * len(arrays),
-        out_specs=(whole(pl.ANY),) * len(arrays) + (whole(), whole()),
+        + (
+            jax.ShapeDtypeStruct(live, F32),
+            jax.ShapeDtypeStruct(count, F32),
+            jax.ShapeDtypeStruct(evals.shape, evals.dtype),
+        ),
+        in_specs=[whole(SMEM), whole()] + [whole(pl.ANY)] * len(arrays),
+        out_specs=(whole(pl.ANY),) * len(arrays) + (whole(),) * 3,
         scratch_shapes=[pltpu.SemaphoreType.DMA((len(arrays),))],
         compiler_params=params(1),
         cost_estimate=pl.CostEstimate(flops=0, bytes_accessed=2**22, transcendentals=0),
         name="stage",
-    )(lengths, *arrays)
+    )(lengths, evals, *arrays)
 
 
 def gauss_jordan(tiles, width, group):
-    count = len(tiles)
-    sub = lax.broadcasted_iota(jnp.int32, tiles[0].shape, 0)
     shape = tiles[0].shape
+    sub = lax.broadcasted_iota(jnp.int32, shape, 0)
 
     def spread_row(tile, j):
         return jnp.broadcast_to(tile[j : j + 1, :], shape)
 
+    def spread_column(tile, k):
+        return jnp.broadcast_to(tile[:, k : k + 1], shape)
+
     for start in range(0, width, group):
-        columns = [
-            [jnp.broadcast_to(tile[:, k : k + 1], shape) for tile in tiles]
+        first, last = start // SUB, (start + group) // SUB
+        pivots = [
+            [spread_column(tile, k) for tile in tiles[first:last]]
             for k in range(start, start + group)
         ]
+        rows = tiles[first:last]
         for step in range(group):
-            home, j = divmod(start + step, SUB)
-            column = columns[step]
+            home, j = divmod(step, SUB)
+            column = pivots[step]
             inverse = 1.0 / spread_row(column[home], j)
 
             def eliminate(block):
                 scaled = spread_row(block[home], j) * inverse
-                result = [block[g] - column[g] * scaled for g in range(count)]
+                result = [tile - c * scaled for tile, c in zip(block, column)]
                 result[home] = jnp.where(sub == j, scaled, result[home])
                 return result
 
-            for later in range(step + 1, group):
-                columns[later] = eliminate(columns[later])
-            tiles = eliminate(tiles)
+            pivots[step + 1 :] = [eliminate(pivot) for pivot in pivots[step + 1 :]]
+            rows = eliminate(rows)
+        solved = [spread_row(rows[step // SUB], step % SUB) for step in range(group)]
+        tiles = [
+            rows[g - first]
+            if first <= g < last
+            else tile
+            - functools.reduce(
+                jnp.add, [spread_column(tile, start + t) * s for t, s in enumerate(solved)]
+            )
+            for g, tile in enumerate(tiles)
+        ]
     return tiles
 
 
@@ -217,7 +235,7 @@
     lane = lax.broadcasted_iota(jnp.int32, (rank, rank), 1)
     both = jnp.concatenate([matrix, jnp.where(row == lane, 1.0, 0.0)], 1)
     tiles = [both[g * SUB : (g + 1) * SUB] for g in range(rank // SUB)]
-    tiles = gauss_jordan(tiles, rank, SUB)
+    tiles = gauss_jordan(tiles, rank, 2 * SUB)
     inverse_ref[...] = jnp.concatenate([tile[:, rank:] for tile in tiles], 0)
 
 
@@ -225,23 +243,40 @@
     return jnp.dot(a, b, precision=lax.Precision.HIGHEST, preferred_element_type=F32)
 
 
-def score_kernel(
-    bits, own_ref, other_ref, sketch_ref, *rest
-):
+def solve_kernel(inverse_ref, sketch_ref, left_ref):
+    rank = inverse_ref.shape[0]
+    first_core = lax.axis_index("dp") % 2 == 0
+
+    @pl.when(first_core)
+    def _():
+        for p in range(0, sketch_ref.shape[1], rank):
+            left_ref[:, p : p + rank] = exact_dot(sketch_ref[:, p : p + rank], inverse_ref[...])
+
+    @pl.when(jnp.logical_not(first_core))
+    def _():
+        left_ref[...] = exact_dot(inverse_ref[...], sketch_ref[...])
+
+
+def score_kernel(bits, other_ref, left_ref, *rest):
     *evals_refs, scores_ref, rows_ref = rest
     place = lax.axis_index("dp")
     first_core = place % 2 == 0
-    own = own_ref[...]
-    other = other_ref[...]
-    inverse_in = jnp.where(first_core, own, other)
-    inverse_out = jnp.where(first_core, other, own)
-    rank = own.shape[0]
+    rank = other_ref.shape[0]
     pairs, evals = scores_ref.shape
-    left = exact_dot(inverse_out, sketch_ref[...])
-    for p in range(pairs):
-        rows_ref[p * rank : (p + 1) * rank, :] = exact_dot(
-            left[:, p * rank : (p + 1) * rank], inverse_in
-        )
+
+    @pl.when(first_core)
+    def _():
+        solved = exact_dot(other_ref[...], left_ref[...])
+        for p in range(pairs):
+            rows_ref[p * rank : (p + 1) * rank, :] = solved[:, p * rank : (p + 1) * rank]
+
+    @pl.when(jnp.logical_not(first_core))
+    def _():
+        for p in range(pairs):
+            rows_ref[p * rank : (p + 1) * rank, :] = exact_dot(
+                left_ref[:, p * rank : (p + 1) * rank], other_ref[...]
+            )
+
     fold = 2 * LANES // rank
     steps = rank // fold
     precond = jnp.concatenate(
@@ -297,13 +332,13 @@
 
     rows = 2 * pairs * seq
     packed = jax.ShapeDtypeStruct((3 * rank // 8, 2 * rank), F32)
-    flat_in, flat_out, near, live, count = staged(
+    flat_in, flat_out, live, count, near = staged(
         lengths,
+        eval_sketches,
         (rows, rank),
         packed.shape,
         activations.reshape(rows, depth),
         out_grads.reshape(rows, depth),
-        eval_sketches,
     )
     near = doubled(near, first)
     mine = jnp.concatenate([proj_in, proj_out], 1).T
@@ -362,16 +397,25 @@
         name="invert",
     )(blocks)
     other_inverse = swap(inverse, 1)
+    left = pl.pallas_call(
+        solve_kernel,
+        out_shape=jax.ShapeDtypeStruct((rank, pairs * rank), F32),
+        in_specs=[whole()] * 2,
+        out_specs=whole(),
+        compiler_params=params(4),
+        cost_estimate=pl.CostEstimate(flops=10**8, bytes_accessed=2**21, transcendentals=0),
+        name="solve",
+    )(inverse, sketch)
     evals = 4 * near.shape[0]
     return pl.pallas_call(
         functools.partial(score_kernel, bits),
         out_shape=jax.ShapeDtypeStruct((pairs, evals), F32),
-        in_specs=[whole()] * 7,
+        in_specs=[whole()] * 6,
         out_specs=whole(),
         scratch_shapes=[pltpu.VMEM((pairs * rank, rank), F32)],
         compiler_params=params(4 + 6 * evals * rank * rank // 2**20),
         name="score",
-    )(inverse, other_inverse, sketch, *evals_pieces)
+    )(other_inverse, left, *evals_pieces)
 
 
 def solution(mesh):

time: 44.8 us -> 44.1 us (0.984)
  no operation moved by 1% of the time
where the time goes in v6:
time: 44.1 us; the launch traced here: 43.6 us
  starting transfers between devices  15.6 us (35%)
  waiting for transfers between devices  12.6 us (29%)
  local copies, waits for them, and re-layouts  8.45 us (19%)
  Pallas kernels  6.01 us (14%)
  other arithmetic  0.82 us (2%)
    all_to_all x2, starting transfers between devices, to_all_chips(): return lax.all_to_all(copies, 'dp', 0, 0, axis_index_groups=same_core)  11.2 us
    ppermute x8, waiting for transfers between devices, swap(): return lax.ppermute(block, 'dp', [(d, d ^ bit) for d in range(devices)])  8.64 us
    unnamed x13, local copies, waits for them, and re-layouts  6.97 us
    ppermute x8, starting transfers between devices, swap(): return lax.ppermute(block, 'dp', [(d, d ^ bit) for d in range(devices)])  4.37 us
    all_to_all x2, waiting for transfers between devices, to_all_chips(): return lax.all_to_all(copies, 'dp', 0, 0, axis_index_groups=same_core)  3.99 us
    pallas_call x1, Pallas kernels, on_device(): pl.pallas_call(invert_kernel, out_shape=jax.ShapeDtypeStruct((rank, rank)...  1.75 us
    broadcast_in_dim x2, local copies, waits for them, and re-layouts, copies_of(): return jnp.broadcast_to(block[None], (chips,) + block.shape)  1.48 us
    pallas_call x1, Pallas kernels, on_device(): pl.pallas_call(functools.partial(score_kernel, bits), out_shape=jax.Shape...  1.29 us
  transfers between devices with their start and end apart: 10, of which 6 were waited for; matrix products, arithmetic and copies ran while one was open for 2% of the time, Pallas kernels for 11%

profile of v6, /device:TPU:0, one launch (start us, length us, event | category | flops | bytes accessed | tf_op | source)
XLA Modules:
  0.0 43.6 jit_solution(3775295370742742276)
XLA Ops:
  0.0 0.8 %maximum_bitcast_fusion = bf16[128,256]{1,0:T(8,128)(2,1)S(1)} fusion(bf16[256,64]{0,1:T(8,128)(2,1)} %param.10, bf16[256,64]{0,1:T(8,128)(2,1)} %param.9), kind=kLoop, calls=%fused_computation | loop fusion | flops 131072 | bytes 131072 | tf_op jit(solution)/shard_map/transpose | solution.py:344
  0.8 0.8 %broadcast_in_dim.4 = bf16[8,128,256]{2,1,0:T(8,128)(2,1)} broadcast(bf16[128,256]{1,0:T(8,128)(2,1)S(1)} %maximum_bitcast_fusion), dimensions={1,2} | broadcast | bytes 589824 | tf_op jit(solution)/shard_map/broadcast_in_dim | solution.py:325
  1.6 7.3 %all-to-all-start = ((bf16[8,128,256]{2,1,0:T(8,128)(2,1)}), bf16[8,128,256]{2,1,0:T(8,128)(2,1)S(1)}, u32[]{:S(2)}, u32[]{:S(2)}) async-start(bf16[8,128,256]{2,1,0:T(8,128)(2,1)} %broadcast_in_dim.4), calls=%async_computation | async-start | bytes 1048576 | tf_op jit(solution)/shard_map/all_to_all | solution.py:328
  8.9 0.0 copy-start.2
  8.9 1.6 %copy-done.2 = bf16[2,2,64,4096]{3,2,1,0:T(8,128)(2,1)S(1)} copy-done((bf16[2,2,64,4096]{3,2,1,0:T(8,128)(2,1)S(1)}, bf16[2,2,64,4096]{3,2,1,0:T(8,128)(2,1)}, u32[]{:S(2)}) %copy-start.2) | copy-done | bytes 2097176
  10.5 0.0 copy-start.3
  10.5 1.6 %copy-done.3 = bf16[2,2,64,4096]{3,2,1,0:T(8,128)(2,1)S(1)} copy-done((bf16[2,2,64,4096]{3,2,1,0:T(8,128)(2,1)S(1)}, bf16[2,2,64,4096]{3,2,1,0:T(8,128)(2,1)}, u32[]{:S(2)}) %copy-start.3) | copy-done | bytes 2097176
  12.0 0.0 copy-start.4
  12.1 0.8 %copy-done.4 = bf16[4,4096]{1,0:T(4,128)(2,1)S(1)} copy-done((bf16[4,4096]{1,0:T(4,128)(2,1)S(1)}, bf16[4,4096]{1,0:T(4,128)(2,1)}, u32[]{:S(2)}) %copy-start.4) | copy-done | bytes 32792
  12.8 0.0 copy-start.5
  12.8 0.7 %copy-done.5 = s32[2,2]{1,0:T(2,128)S(1)} copy-done((s32[2,2]{1,0:T(2,128)S(1)}, s32[2,2]{1,0:T(2,128)}, u32[]{:S(2)}) %copy-start.5) | copy-done | bytes 40
  13.5 0.9 %stage.1 = (bf16[256,4096]{1,0:T(8,128)(2,1)S(1)}, bf16[256,4096]{1,0:T(8,128)(2,1)S(1)}, f32[256,64]{1,0:T(8,128)S(1)}, f32[24,128]{1,0:T(8,128)S(1)}, bf16[4,4096]{1,0:T(4,128)(2,1)S(1)}) custom-call(s32[2,2]{1,0:T(2,128)S(1)} %copy-done.5, bf16[4,4096]{1,0:T(4,128)(2,1)S(1)} %copy-done.4, bf16[256,4096]{1,0:T(8,128)(2,1)S(1)} %bitcast.4, ...), custom_call_target="tpu_custom_call" | custom-call | bytes 4194304 | tf_op jit(solution)/shard_map/stage/pallas_call | solution.py:162
  14.4 0.0 copy-start
  14.4 1.3 %copy-done = bf16[256,4096]{1,0:T(8,128)(2,1)} copy-done((bf16[256,4096]{1,0:T(8,128)(2,1)}, bf16[256,4096]{1,0:T(8,128)(2,1)S(1)}, u32[]{:S(2)}) %copy-start) | copy-done | bytes 2097176
  15.7 2.0 %collective-permute-start = (bf16[4,4096]{1,0:T(4,128)(2,1)S(1)}, bf16[4,4096]{1,0:T(4,128)(2,1)S(1)}, u32[]{:S(2)}, u32[]{:S(2)}) collective-permute-start(bf16[4,4096]{1,0:T(4,128)(2,1)S(1)} %get-tuple-element.19), channel_id=1, source_target_pairs={{0,4},{1,5},{2,6},{3,7},{4,0},{5,1},{6,2},{7,3},{8,12},{9,13},{10,... | collective-permute-start | bytes 98312 | tf_op jit(solution)/shard_map/ppermute | solution.py:322
  17.7 2.2 %collective-permute-done = bf16[4,4096]{1,0:T(4,128)(2,1)S(1)} collective-permute-done((bf16[4,4096]{1,0:T(4,128)(2,1)S(1)}, bf16[4,4096]{1,0:T(4,128)(2,1)S(1)}, u32[]{:S(2)}, u32[]{:S(2)}) %collective-permute-start) | collective-permute-done | bytes 32800 | tf_op jit(solution)/shard_map/ppermute | solution.py:322
  20.0 3.3 %all-to-all-done.own_ref = bf16[8,128,256]{2,1,0:T(8,128)(2,1)S(1)} async-done(((bf16[8,128,256]{2,1,0:T(8,128)(2,1)}), bf16[8,128,256]{2,1,0:T(8,128)(2,1)S(1)}, u32[]{:S(2)}, u32[]{:S(2)}) %all-to-all-start) | async-done | bytes 524320 | tf_op jit(solution)/shard_map/all_to_all | solution.py:328
  23.4 0.0 copy-start.1
  23.4 0.0 collective-permute-start.1
  23.4 0.2 collective-permute-start.4
  23.5 0.4 first_half.2.half_in_ref
  23.9 1.0 %copy-done.1 = bf16[256,4096]{1,0:T(8,128)(2,1)S(1)} copy-done((bf16[256,4096]{1,0:T(8,128)(2,1)S(1)}, bf16[256,4096]{1,0:T(8,128)(2,1)}, u32[]{:S(2)}) %copy-start.1) | copy-done | bytes 2097176
  24.9 0.4 first_half.3.half_out_ref
  25.4 0.0 collective-permute-done.1.other_ref
  25.4 1.0 %second_half.1 = (f32[24,128]{1,0:T(8,128)S(1)}, f32[24,128]{1,0:T(8,128)S(1)}, f32[64,128]{1,0:T(8,128)S(1)}) custom-call(f32[256,64]{1,0:T(8,128)S(1)} %get-tuple-element.15.live_ref, f32[24,128]{1,0:T(8,128)S(1)} %get-tuple-element.16.count_ref, bf16[256,4096]{1,0:T(8,128)(2,1)S(1)} %get-tuple-element.17.x_ref.act_ref, bf16[256,4096]{1,0:T(8,128)(2,1)S(1)} %copy-done.1, ...), custom_call_target="tpu_custom_call" | custom-call | flops 134217728 | bytes 4194304 | tf_op jit(solution)/shard_map/second_half/pallas_call | solution.py:377
  26.4 0.1 collective-permute-start.2
  26.4 1.2 %collective-permute-done.2 = f32[24,128]{1,0:T(8,128)S(1)} collective-permute-done((f32[24,128]{1,0:T(8,128)S(1)}, f32[24,128]{1,0:T(8,128)S(1)}, u32[]{:S(2)}, u32[]{:S(2)}) %collective-permute-start.2) | collective-permute-done | bytes 12320 | tf_op jit(solution)/shard_map/ppermute | solution.py:322
  27.6 0.6 %broadcast_in_dim.5 = f32[8,24,128]{2,1,0:T(8,128)} broadcast(f32[24,128]{1,0:T(8,128)S(1)} %add.3), dimensions={1,2} | broadcast | bytes 110592 | tf_op jit(solution)/shard_map/broadcast_in_dim | solution.py:325
  28.2 3.9 %all-to-all-start.1 = ((f32[8,24,128]{2,1,0:T(8,128)}), f32[8,24,128]{2,1,0:T(8,128)S(1)}, u32[]{:S(2)}, u32[]{:S(2)}) async-start(f32[8,24,128]{2,1,0:T(8,128)} %broadcast_in_dim.5), calls=%async_computation.1 | async-start | bytes 196608 | tf_op jit(solution)/shard_map/all_to_all | solution.py:328
  32.2 0.0 collective-permute-done.4
  32.2 2.1 %collective-permute-start.5 = (bf16[16,4096]{1,0:T(8,128)(2,1)S(1)}, bf16[16,4096]{1,0:T(8,128)(2,1)S(1)}, u32[]{:S(2)}, u32[]{:S(2)}) collective-permute-start(bf16[16,4096]{1,0:T(8,128)(2,1)S(1)} %constant_dynamic-update-slice_fusion.rest_0_), channel_id=1, source_target_pairs={{0,2},{1,3},{2,0},{3,1},{4,6},{5,7},{6,4},{7,5},{8,10},{9,11},{10,... | collective-permute-start | bytes 393224 | tf_op jit(solution)/shard_map/ppermute | solution.py:322
  34.3 0.0 collective-permute-start.6
  34.3 4.4 %collective-permute-done.5.rest_1_ = bf16[16,4096]{1,0:T(8,128)(2,1)S(1)} collective-permute-done((bf16[16,4096]{1,0:T(8,128)(2,1)S(1)}, bf16[16,4096]{1,0:T(8,128)(2,1)S(1)}, u32[]{:S(2)}, u32[]{:S(2)}) %collective-permute-start.5) | collective-permute-done | bytes 131104 | tf_op jit(solution)/shard_map/ppermute | solution.py:322
  38.7 0.0 collective-permute-start.7
  38.7 0.6 %all-to-all-done.1.blocks_ref = f32[8,24,128]{2,1,0:T(8,128)S(1)} async-done(((f32[8,24,128]{2,1,0:T(8,128)}), f32[8,24,128]{2,1,0:T(8,128)S(1)}, u32[]{:S(2)}, u32[]{:S(2)}) %all-to-all-start.1) | async-done | bytes 98336 | tf_op jit(solution)/shard_map/all_to_all | solution.py:328
  39.3 1.8 %invert.1.inverse_ref = f32[64,64]{1,0:T(8,128)S(1)} custom-call(f32[8,24,128]{2,1,0:T(8,128)S(1)} %all-to-all-done.1.blocks_ref), custom_call_target="tpu_custom_call" | custom-call | flops 1000000000 | bytes 16777216 | tf_op jit(solution)/shard_map/invert/pallas_call | solution.py:390
  41.1 0.0 collective-permute-start.3
  41.1 0.3 solve.1.left_ref
  41.4 0.0 collective-permute-done.6.rest_2_
  41.4 0.0 collective-permute-done.7.rest_3_
  41.4 0.9 %collective-permute-done.3.other_ref = f32[64,64]{1,0:T(8,128)S(1)} collective-permute-done((f32[64,64]{1,0:T(8,128)S(1)}, f32[64,64]{1,0:T(8,128)S(1)}, u32[]{:S(2)}, u32[]{:S(2)}) %collective-permute-start.3) | collective-permute-done | bytes 16416 | tf_op jit(solution)/shard_map/ppermute | solution.py:322
  42.3 1.3 %score.1 = f32[2,64]{1,0:T(2,128)} custom-call(f32[64,64]{1,0:T(8,128)S(1)} %collective-permute-done.3.other_ref, f32[64,128]{1,0:T(8,128)S(1)} %solve.1.left_ref, bf16[16,4096]{1,0:T(8,128)(2,1)S(1)} %constant_dynamic-update-slice_fusion.rest_0_, bf16[16,4096]{1,0:T(8,128)(2,1)S(1)} %collective-permute-done.5.rest_1_, ...), custom_call_target="tpu_custom_call" | custom-call | tf_op jit(solution)/shard_map/score/pallas_call | solution.py:410
  (4 shorter events, 0.1 us)
Async XLA Ops:
  1.6 21.7 %all-to-all-start = ((bf16[8,128,256]{2,1,0:T(8,128)(2,1)}), bf16[8,128,256]{2,1,0:T(8,128)(2,1)S(1)}, u32[]{:S(2)}, u32[]{:S(2)}) async-start(bf16[8,128,256]{2,1,0:T(8,128)(2,1)} %broadcast_in_dim.4), calls=%async_computation | async-start | bytes 1048576 | tf_op jit(solution)/shard_map/all_to_all | solution.py:328
  8.9 1.6 %copy-start.2 = (bf16[2,2,64,4096]{3,2,1,0:T(8,128)(2,1)S(1)}, bf16[2,2,64,4096]{3,2,1,0:T(8,128)(2,1)}, u32[]{:S(2)}) copy-start(bf16[2,2,64,4096]{3,2,1,0:T(8,128)(2,1)} %param.6) | copy-start | bytes 6291460
  10.5 1.6 %copy-start.3 = (bf16[2,2,64,4096]{3,2,1,0:T(8,128)(2,1)S(1)}, bf16[2,2,64,4096]{3,2,1,0:T(8,128)(2,1)}, u32[]{:S(2)}) copy-start(bf16[2,2,64,4096]{3,2,1,0:T(8,128)(2,1)} %param.7) | copy-start | bytes 6291460
  12.0 0.8 %copy-start.4 = (bf16[4,4096]{1,0:T(4,128)(2,1)S(1)}, bf16[4,4096]{1,0:T(4,128)(2,1)}, u32[]{:S(2)}) copy-start(bf16[4,4096]{1,0:T(4,128)(2,1)} %evals_ref.1) | copy-start | bytes 98308
  12.8 0.7 %copy-start.5 = (s32[2,2]{1,0:T(2,128)S(1)}, s32[2,2]{1,0:T(2,128)}, u32[]{:S(2)}) copy-start(s32[2,2]{1,0:T(2,128)} %lengths_ref.1) | copy-start | bytes 52
  14.4 1.3 %copy-start = (bf16[256,4096]{1,0:T(8,128)(2,1)}, bf16[256,4096]{1,0:T(8,128)(2,1)S(1)}, u32[]{:S(2)}) copy-start(bf16[256,4096]{1,0:T(8,128)(2,1)S(1)} %get-tuple-element.18.x_ref.grad_ref) | copy-start | bytes 6291460
  15.7 4.3 %collective-permute-start = (bf16[4,4096]{1,0:T(4,128)(2,1)S(1)}, bf16[4,4096]{1,0:T(4,128)(2,1)S(1)}, u32[]{:S(2)}, u32[]{:S(2)}) collective-permute-start(bf16[4,4096]{1,0:T(4,128)(2,1)S(1)} %get-tuple-element.19), channel_id=1, source_target_pairs={{0,4},{1,5},{2,6},{3,7},{4,0},{5,1},{6,2},{7,3},{8,12},{9,13},{10,... | collective-permute-start | bytes 98312 | tf_op jit(solution)/shard_map/ppermute | solution.py:322
  23.4 1.6 %copy-start.1 = (bf16[256,4096]{1,0:T(8,128)(2,1)S(1)}, bf16[256,4096]{1,0:T(8,128)(2,1)}, u32[]{:S(2)}) copy-start(bf16[256,4096]{1,0:T(8,128)(2,1)} %copy-done) | copy-start | bytes 6291460
  23.4 2.0 %collective-permute-start.1 = (bf16[8,128,256]{2,1,0:T(8,128)(2,1)S(1)}, bf16[8,128,256]{2,1,0:T(8,128)(2,1)S(1)}, u32[]{:S(2)}, u32[]{:S(2)}) collective-permute-start(bf16[8,128,256]{2,1,0:T(8,128)(2,1)S(1)} %all-to-all-done.own_ref), channel_id=1, source_target_pairs={{0,1},{1,0},{2,3},{3,2},{4,5},{5,4},{6,7},{7,6},{8,9},{9,8},{10,11... | collective-permute-start | bytes 1572872 | tf_op jit(solution)/shard_map/ppermute | solution.py:322
  23.4 8.8 %collective-permute-start.4 = (bf16[8,4096]{1,0:T(8,128)(2,1)S(1)}, bf16[8,4096]{1,0:T(8,128)(2,1)S(1)}, u32[]{:S(2)}, u32[]{:S(2)}) collective-permute-start(bf16[8,4096]{1,0:T(8,128)(2,1)S(1)} %pad_maximum_fusion), channel_id=1, source_target_pairs={{0,8},{1,9},{2,10},{3,11},{4,12},{5,13},{6,14},{7,15},{8,0},{9,1},... | collective-permute-start | bytes 196616 | tf_op jit(solution)/shard_map/ppermute | solution.py:322
  26.4 1.2 %collective-permute-start.2 = (f32[24,128]{1,0:T(8,128)S(1)}, f32[24,128]{1,0:T(8,128)S(1)}, u32[]{:S(2)}, u32[]{:S(2)}) collective-permute-start(f32[24,128]{1,0:T(8,128)S(1)} %get-tuple-element.22), channel_id=1, source_target_pairs={{0,1},{1,0},{2,3},{3,2},{4,5},{5,4},{6,7},{7,6},{8,9},{9,8},{10,11... | collective-permute-start | bytes 36872 | tf_op jit(solution)/shard_map/ppermute | solution.py:322
  28.2 11.1 %all-to-all-start.1 = ((f32[8,24,128]{2,1,0:T(8,128)}), f32[8,24,128]{2,1,0:T(8,128)S(1)}, u32[]{:S(2)}, u32[]{:S(2)}) async-start(f32[8,24,128]{2,1,0:T(8,128)} %broadcast_in_dim.5), calls=%async_computation.1 | async-start | bytes 196608 | tf_op jit(solution)/shard_map/all_to_all | solution.py:328
  32.2 6.5 %collective-permute-start.5 = (bf16[16,4096]{1,0:T(8,128)(2,1)S(1)}, bf16[16,4096]{1,0:T(8,128)(2,1)S(1)}, u32[]{:S(2)}, u32[]{:S(2)}) collective-permute-start(bf16[16,4096]{1,0:T(8,128)(2,1)S(1)} %constant_dynamic-update-slice_fusion.rest_0_), channel_id=1, source_target_pairs={{0,2},{1,3},{2,0},{3,1},{4,6},{5,7},{6,4},{7,5},{8,10},{9,11},{10,... | collective-permute-start | bytes 393224 | tf_op jit(solution)/shard_map/ppermute | solution.py:322
  34.3 7.1 %collective-permute-start.6 = (bf16[16,4096]{1,0:T(8,128)(2,1)S(1)}, bf16[16,4096]{1,0:T(8,128)(2,1)S(1)}, u32[]{:S(2)}, u32[]{:S(2)}) collective-permute-start(bf16[16,4096]{1,0:T(8,128)(2,1)S(1)} %constant_dynamic-update-slice_fusion.rest_0_), channel_id=1, source_target_pairs={{0,1},{1,0},{2,3},{3,2},{4,5},{5,4},{6,7},{7,6},{8,9},{9,8},{10,11... | collective-permute-start | bytes 393224 | tf_op jit(solution)/shard_map/ppermute | solution.py:322
  38.7 2.8 %collective-permute-start.7 = (bf16[16,4096]{1,0:T(8,128)(2,1)S(1)}, bf16[16,4096]{1,0:T(8,128)(2,1)S(1)}, u32[]{:S(2)}, u32[]{:S(2)}) collective-permute-start(bf16[16,4096]{1,0:T(8,128)(2,1)S(1)} %collective-permute-done.5.rest_1_), channel_id=1, source_target_pairs={{0,1},{1,0},{2,3},{3,2},{4,5},{5,4},{6,7},{7,6},{8,9},{9,8},{10,11... | collective-permute-start | bytes 393224 | tf_op jit(solution)/shard_map/ppermute | solution.py:322
  41.1 1.2 %collective-permute-start.3 = (f32[64,64]{1,0:T(8,128)S(1)}, f32[64,64]{1,0:T(8,128)S(1)}, u32[]{:S(2)}, u32[]{:S(2)}) collective-permute-start(f32[64,64]{1,0:T(8,128)S(1)} %invert.1.inverse_ref), channel_id=1, source_target_pairs={{0,1},{1,0},{2,3},{3,2},{4,5},{5,4},{6,7},{7,6},{8,9},{9,8},{10,11... | collective-permute-start | bytes 49160 | tf_op jit(solution)/shard_map/ppermute | solution.py:322

commit v7 on v6

--- a/solution.py
+++ b/solution.py
@@ -91,6 +91,7 @@
 
 def second_half_kernel(
     split_cores,
+    outer_core,
     live_ref,
     count_ref,
     act_ref,
@@ -98,42 +99,55 @@
     other_ref,
     half_in_ref,
     half_out_ref,
-    keep_ref,
-    send_ref,
-    sketch_ref,
+    factor_ref,
+    tokens_ref,
 ):
     place = 1 - own_place(split_cores)
-    rows, rank = half_in_ref.shape
+    rank = half_in_ref.shape[1]
+    slot, _, _ = packed_places(factor_ref.shape)
+
+    def side(x_ref, first, half_ref):
+        total = projected(x_ref, other_ref, first, rank, place, half_ref[...])
+        tokens = jnp.where(live_ref[...] > 0.0, total, 0.0).astype(BF16)
+        packed = packed_symmetric(contract_first(tokens, tokens))
+        factor_ref[...] = jnp.where(slot, count_ref[...], packed)
+        tokens_ref[...] = tokens
+
+    outer_here = lax.axis_index("dp") % 2 == outer_core
+
+    @pl.when(outer_here)
+    def _():
+        side(grad_ref, rank, half_out_ref)
+
+    @pl.when(jnp.logical_not(outer_here))
+    def _():
+        side(act_ref, 0, half_in_ref)
+
+
+def sketch_kernel(sent_ref, kept_ref, sketch_ref):
+    rank = sent_ref.shape[1]
     pairs = sketch_ref.shape[1] // rank
-    seq = rows // (2 * pairs)
-    live = live_ref[...] > 0.0
-    slot, _, _ = packed_places(keep_ref.shape)
-
-    def factor(rows_of):
-        packed = packed_symmetric(contract_first(rows_of, rows_of))
-        return jnp.where(slot, count_ref[...], packed)
-
-    total_in = projected(act_ref, other_ref, 0, rank, place, half_in_ref[...])
-    total_out = projected(grad_ref, other_ref, rank, rank, place, half_out_ref[...])
-    inner = jnp.where(live, total_in, 0.0).astype(BF16)
-    outer = jnp.where(live, total_out, 0.0)
-    factor_in = factor(inner)
-    factor_out = factor(outer.astype(BF16))
+    seq = sent_ref.shape[0] // (2 * pairs)
+
+    def sketch(outer_ref, inner_ref):
+        for p in range(pairs):
+            start = 2 * p * seq
+            chosen = slice(start, start + seq)
+            rejected = slice(start + seq, start + 2 * seq)
+            signed = jnp.concatenate([outer_ref[chosen, :], -outer_ref[rejected, :]], 0)
+            sketch_ref[:, p * rank : (p + 1) * rank] = contract_first(
+                signed, inner_ref[start : start + 2 * seq, :]
+            )
+
     first_core = lax.axis_index("dp") % 2 == 0
-    keep_ref[...] = jnp.where(first_core, factor_in, factor_out)
-    send_ref[...] = jnp.where(first_core, factor_out, factor_in)
-    signed = jnp.concatenate(
-        [
-            -outer[s * seq : (s + 1) * seq] if s % 2 else outer[s * seq : (s + 1) * seq]
-            for s in range(2 * pairs)
-        ],
-        0,
-    ).astype(BF16)
-    sketches = []
-    for p in range(pairs):
-        own_rows = slice(2 * p * seq, 2 * (p + 1) * seq)
-        sketches.append(contract_first(signed[own_rows], inner[own_rows]))
-    sketch_ref[...] = jnp.concatenate(sketches, 1)
+
+    @pl.when(first_core)
+    def _():
+        sketch(sent_ref, kept_ref)
+
+    @pl.when(jnp.logical_not(first_core))
+    def _():
+        sketch(kept_ref, sent_ref)
 
 
 def stage_kernel(lengths_ref, evals_ref, *refs):
@@ -374,18 +388,32 @@
 
     half_in = first_half(flat_in, 0)
     half_out = first_half(flat_out, rank)
-    keep, send, sketch = pl.pallas_call(
-        functools.partial(second_half_kernel, split_cores),
-        out_shape=(packed, packed, jax.ShapeDtypeStruct((rank, pairs * rank), F32)),
-        in_specs=[whole()] * 7,
-        out_specs=(whole(),) * 3,
-        compiler_params=params(8),
-        cost_estimate=pl.CostEstimate(
-            flops=2 * rows * depth * rank, bytes_accessed=4 * rows * depth, transcendentals=0
-        ),
-        name="second_half",
-    )(live, count, flat_in, flat_out, other, half_in, half_out)
-    sums = copies_of(keep + swap(send, 1))
+    def second_half(outer_core):
+        return pl.pallas_call(
+            functools.partial(second_half_kernel, split_cores, outer_core),
+            out_shape=(packed, jax.ShapeDtypeStruct((rows, rank), BF16)),
+            in_specs=[whole()] * 7,
+            out_specs=(whole(),) * 2,
+            compiler_params=params(8),
+            cost_estimate=pl.CostEstimate(
+                flops=rows * depth * rank, bytes_accessed=2 * rows * depth, transcendentals=0
+            ),
+            name="second_half",
+        )(live, count, flat_in, flat_out, other, half_in, half_out)
+
+    send, sent = second_half(0)
+    arrived = swap(send, 1)
+    keep, kept = second_half(1)
+    sketch = pl.pallas_call(
+        sketch_kernel,
+        out_shape=jax.ShapeDtypeStruct((rank, pairs * rank), F32),
+        in_specs=[whole()] * 2,
+        out_specs=whole(),
+        compiler_params=params(4),
+        cost_estimate=pl.CostEstimate(flops=10**8, bytes_accessed=2**21, transcendentals=0),
+        name="sketch",
+    )(sent, kept)
+    sums = copies_of(keep + arrived)
     blocks = to_all_chips(sums)
     inverse = pl.pallas_call(
         invert_kernel,

time: 44.1 us -> 43.9 us (level)
  waiting for transfers between devices: 12.6 us -> 11.7 us
  Pallas kernels: 6.01 us -> 6.68 us
    ppermute x8, waiting for transfers between devices: 8.64 us -> 7.69 us  [swap(): return lax.ppermute(block, 'dp', [(d, d ^ bit) for d in range(devices)])]
    pallas_call x1 -> x3, Pallas kernels: 0.97 us -> 1.64 us  [the longest x2 1.39 us: second_half(): pl.pallas_call(functools.partial(second_half_kernel, split_cores, outer_c...]
  transfers between devices with their start and end apart: 10 -> 10, of which waited for: 6 -> 6; matrix products, arithmetic and copies ran while one was open for 2% -> 2% of each run, Pallas kernels for 11% -> 12%
where the time goes in v7:
time: 43.9 us; the launch traced here: 43.3 us
  starting transfers between devices  15.6 us (36%)
  waiting for transfers between devices  11.7 us (27%)
  local copies, waits for them, and re-layouts  8.45 us (19%)
  Pallas kernels  6.68 us (15%)
  other arithmetic  0.82 us (2%)
    all_to_all x2, starting transfers between devices, to_all_chips(): return lax.all_to_all(copies, 'dp', 0, 0, axis_index_groups=same_core)  11.2 us
    ppermute x8, waiting for transfers between devices, swap(): return lax.ppermute(block, 'dp', [(d, d ^ bit) for d in range(devices)])  7.69 us
    unnamed x13, local copies, waits for them, and re-layouts  6.96 us
    ppermute x8, starting transfers between devices, swap(): return lax.ppermute(block, 'dp', [(d, d ^ bit) for d in range(devices)])  4.36 us
    all_to_all x2, waiting for transfers between devices, to_all_chips(): return lax.all_to_all(copies, 'dp', 0, 0, axis_index_groups=same_core)  4 us
    pallas_call x1, Pallas kernels, on_device(): pl.pallas_call(invert_kernel, out_shape=jax.ShapeDtypeStruct((rank, rank)...  1.75 us
    broadcast_in_dim x2, local copies, waits for them, and re-layouts, copies_of(): return jnp.broadcast_to(block[None], (chips,) + block.shape)  1.48 us
    pallas_call x2, Pallas kernels, second_half(): pl.pallas_call(functools.partial(second_half_kernel, split_cores, outer_c...  1.39 us
  transfers between devices with their start and end apart: 10, of which 6 were waited for; matrix products, arithmetic and copies ran while one was open for 2% of the time, Pallas kernels for 12%

profile of v7, /device:TPU:0, one launch (start us, length us, event | category | flops | bytes accessed | tf_op | source)
XLA Modules:
  0.0 43.3 jit_solution(8027485517893909720)
XLA Ops:
  0.0 0.8 %maximum_bitcast_fusion = bf16[128,256]{1,0:T(8,128)(2,1)S(1)} fusion(bf16[256,64]{0,1:T(8,128)(2,1)} %param.10, bf16[256,64]{0,1:T(8,128)(2,1)} %param.9), kind=kLoop, calls=%fused_computation | loop fusion | flops 131072 | bytes 131072 | tf_op jit(solution)/shard_map/transpose | solution.py:358
  0.8 0.8 %broadcast_in_dim.4 = bf16[8,128,256]{2,1,0:T(8,128)(2,1)} broadcast(bf16[128,256]{1,0:T(8,128)(2,1)S(1)} %maximum_bitcast_fusion), dimensions={1,2} | broadcast | bytes 589824 | tf_op jit(solution)/shard_map/broadcast_in_dim | solution.py:339
  1.6 7.3 %all-to-all-start = ((bf16[8,128,256]{2,1,0:T(8,128)(2,1)}), bf16[8,128,256]{2,1,0:T(8,128)(2,1)S(1)}, u32[]{:S(2)}, u32[]{:S(2)}) async-start(bf16[8,128,256]{2,1,0:T(8,128)(2,1)} %broadcast_in_dim.4), calls=%async_computation | async-start | bytes 1048576 | tf_op jit(solution)/shard_map/all_to_all | solution.py:342
  8.9 0.0 copy-start.2
  8.9 1.6 %copy-done.2 = bf16[2,2,64,4096]{3,2,1,0:T(8,128)(2,1)S(1)} copy-done((bf16[2,2,64,4096]{3,2,1,0:T(8,128)(2,1)S(1)}, bf16[2,2,64,4096]{3,2,1,0:T(8,128)(2,1)}, u32[]{:S(2)}) %copy-start.2) | copy-done | bytes 2097176
  10.5 0.0 copy-start.3
  10.5 1.6 %copy-done.3 = bf16[2,2,64,4096]{3,2,1,0:T(8,128)(2,1)S(1)} copy-done((bf16[2,2,64,4096]{3,2,1,0:T(8,128)(2,1)S(1)}, bf16[2,2,64,4096]{3,2,1,0:T(8,128)(2,1)}, u32[]{:S(2)}) %copy-start.3) | copy-done | bytes 2097176
  12.0 0.0 copy-start.4
  12.0 0.8 %copy-done.4 = bf16[4,4096]{1,0:T(4,128)(2,1)S(1)} copy-done((bf16[4,4096]{1,0:T(4,128)(2,1)S(1)}, bf16[4,4096]{1,0:T(4,128)(2,1)}, u32[]{:S(2)}) %copy-start.4) | copy-done | bytes 32792
  12.8 0.0 copy-start.5
  12.8 0.7 %copy-done.5 = s32[2,2]{1,0:T(2,128)S(1)} copy-done((s32[2,2]{1,0:T(2,128)S(1)}, s32[2,2]{1,0:T(2,128)}, u32[]{:S(2)}) %copy-start.5) | copy-done | bytes 40
  13.5 0.9 %stage.1 = (bf16[256,4096]{1,0:T(8,128)(2,1)S(1)}, bf16[256,4096]{1,0:T(8,128)(2,1)S(1)}, f32[256,64]{1,0:T(8,128)S(1)}, f32[24,128]{1,0:T(8,128)S(1)}, bf16[4,4096]{1,0:T(4,128)(2,1)S(1)}) custom-call(s32[2,2]{1,0:T(2,128)S(1)} %copy-done.5, bf16[4,4096]{1,0:T(4,128)(2,1)S(1)} %copy-done.4, bf16[256,4096]{1,0:T(8,128)(2,1)S(1)} %bitcast.4, ...), custom_call_target="tpu_custom_call" | custom-call | bytes 4194304 | tf_op jit(solution)/shard_map/stage/pallas_call | solution.py:176
  14.4 0.0 copy-start
  14.4 1.3 %copy-done = bf16[256,4096]{1,0:T(8,128)(2,1)} copy-done((bf16[256,4096]{1,0:T(8,128)(2,1)}, bf16[256,4096]{1,0:T(8,128)(2,1)S(1)}, u32[]{:S(2)}) %copy-start) | copy-done | bytes 2097176
  15.7 2.0 %collective-permute-start = (bf16[4,4096]{1,0:T(4,128)(2,1)S(1)}, bf16[4,4096]{1,0:T(4,128)(2,1)S(1)}, u32[]{:S(2)}, u32[]{:S(2)}) collective-permute-start(bf16[4,4096]{1,0:T(4,128)(2,1)S(1)} %get-tuple-element.20), channel_id=1, source_target_pairs={{0,4},{1,5},{2,6},{3,7},{4,0},{5,1},{6,2},{7,3},{8,12},{9,13},{10,... | collective-permute-start | bytes 98312 | tf_op jit(solution)/shard_map/ppermute | solution.py:336
  17.7 2.2 %collective-permute-done = bf16[4,4096]{1,0:T(4,128)(2,1)S(1)} collective-permute-done((bf16[4,4096]{1,0:T(4,128)(2,1)S(1)}, bf16[4,4096]{1,0:T(4,128)(2,1)S(1)}, u32[]{:S(2)}, u32[]{:S(2)}) %collective-permute-start) | collective-permute-done | bytes 32800 | tf_op jit(solution)/shard_map/ppermute | solution.py:336
  20.0 3.4 %all-to-all-done.own_ref = bf16[8,128,256]{2,1,0:T(8,128)(2,1)S(1)} async-done(((bf16[8,128,256]{2,1,0:T(8,128)(2,1)}), bf16[8,128,256]{2,1,0:T(8,128)(2,1)S(1)}, u32[]{:S(2)}, u32[]{:S(2)}) %all-to-all-start) | async-done | bytes 524320 | tf_op jit(solution)/shard_map/all_to_all | solution.py:342
  23.4 0.0 copy-start.1
  23.4 0.0 collective-permute-start.1
  23.4 0.2 collective-permute-start.4
  23.5 0.4 first_half.2.half_in_ref
  23.9 1.0 %copy-done.1 = bf16[256,4096]{1,0:T(8,128)(2,1)S(1)} copy-done((bf16[256,4096]{1,0:T(8,128)(2,1)S(1)}, bf16[256,4096]{1,0:T(8,128)(2,1)}, u32[]{:S(2)}) %copy-start.1) | copy-done | bytes 2097176
  24.9 0.4 first_half.3.half_out_ref
  25.4 0.0 collective-permute-done.1.other_ref
  25.4 0.7 %second_half.3 = (f32[24,128]{1,0:T(8,128)S(1)}, bf16[256,64]{1,0:T(8,128)(2,1)S(1)}) custom-call(f32[256,64]{1,0:T(8,128)S(1)} %get-tuple-element.16.live_ref, f32[24,128]{1,0:T(8,128)S(1)} %get-tuple-element.17.count_ref, bf16[256,4096]{1,0:T(8,128)(2,1)S(1)} %get-tuple-element.18.x_ref.act_ref, bf16[256,4096]{1,0:T(8,128)(2,1)S(1)} %copy-done.1, ...), custom_call_target="tpu_custom_call" | custom-call | flops 67108864 | bytes 2097152 | tf_op jit(solution)/shard_map/second_half/pallas_call | solution.py:392
  26.1 0.1 collective-permute-start.2
  26.2 0.7 %second_half.2 = (f32[24,128]{1,0:T(8,128)S(1)}, bf16[256,64]{1,0:T(8,128)(2,1)S(1)}) custom-call(f32[256,64]{1,0:T(8,128)S(1)} %get-tuple-element.16.live_ref, f32[24,128]{1,0:T(8,128)S(1)} %get-tuple-element.17.count_ref, bf16[256,4096]{1,0:T(8,128)(2,1)S(1)} %get-tuple-element.18.x_ref.act_ref, bf16[256,4096]{1,0:T(8,128)(2,1)S(1)} %copy-done.1, ...), custom_call_target="tpu_custom_call" | custom-call | flops 67108864 | bytes 2097152 | tf_op jit(solution)/shard_map/second_half/pallas_call | solution.py:392
  26.9 0.5 %collective-permute-done.2 = f32[24,128]{1,0:T(8,128)S(1)} collective-permute-done((f32[24,128]{1,0:T(8,128)S(1)}, f32[24,128]{1,0:T(8,128)S(1)}, u32[]{:S(2)}, u32[]{:S(2)}) %collective-permute-start.2) | collective-permute-done | bytes 12320 | tf_op jit(solution)/shard_map/ppermute | solution.py:336
  27.3 0.7 %broadcast_in_dim.5 = f32[8,24,128]{2,1,0:T(8,128)} broadcast(f32[24,128]{1,0:T(8,128)S(1)} %add.3), dimensions={1,2} | broadcast | bytes 110592 | tf_op jit(solution)/shard_map/broadcast_in_dim | solution.py:339
  28.0 4.0 %all-to-all-start.1 = ((f32[8,24,128]{2,1,0:T(8,128)}), f32[8,24,128]{2,1,0:T(8,128)S(1)}, u32[]{:S(2)}, u32[]{:S(2)}) async-start(f32[8,24,128]{2,1,0:T(8,128)} %broadcast_in_dim.5), calls=%async_computation.1 | async-start | bytes 196608 | tf_op jit(solution)/shard_map/all_to_all | solution.py:342
  31.9 0.0 collective-permute-done.4
  32.0 2.1 %collective-permute-start.5 = (bf16[16,4096]{1,0:T(8,128)(2,1)S(1)}, bf16[16,4096]{1,0:T(8,128)(2,1)S(1)}, u32[]{:S(2)}, u32[]{:S(2)}) collective-permute-start(bf16[16,4096]{1,0:T(8,128)(2,1)S(1)} %constant_dynamic-update-slice_fusion.rest_0_), channel_id=1, source_target_pairs={{0,2},{1,3},{2,0},{3,1},{4,6},{5,7},{6,4},{7,5},{8,10},{9,11},{10,... | collective-permute-start | bytes 393224 | tf_op jit(solution)/shard_map/ppermute | solution.py:336
  34.0 0.0 collective-permute-start.6
  34.0 4.4 %collective-permute-done.5.rest_1_ = bf16[16,4096]{1,0:T(8,128)(2,1)S(1)} collective-permute-done((bf16[16,4096]{1,0:T(8,128)(2,1)S(1)}, bf16[16,4096]{1,0:T(8,128)(2,1)S(1)}, u32[]{:S(2)}, u32[]{:S(2)}) %collective-permute-start.5) | collective-permute-done | bytes 131104 | tf_op jit(solution)/shard_map/ppermute | solution.py:336
  38.4 0.0 collective-permute-start.7
  38.4 0.6 %all-to-all-done.1.blocks_ref = f32[8,24,128]{2,1,0:T(8,128)S(1)} async-done(((f32[8,24,128]{2,1,0:T(8,128)}), f32[8,24,128]{2,1,0:T(8,128)S(1)}, u32[]{:S(2)}, u32[]{:S(2)}) %all-to-all-start.1) | async-done | bytes 98336 | tf_op jit(solution)/shard_map/all_to_all | solution.py:342
  39.1 1.8 %invert.1.inverse_ref = f32[64,64]{1,0:T(8,128)S(1)} custom-call(f32[8,24,128]{2,1,0:T(8,128)S(1)} %all-to-all-done.1.blocks_ref), custom_call_target="tpu_custom_call" | custom-call | flops 1000000000 | bytes 16777216 | tf_op jit(solution)/shard_map/invert/pallas_call | solution.py:418
  40.8 0.0 collective-permute-start.3
  40.8 0.3 sketch.1.sketch_ref
  41.1 0.3 solve.1.left_ref
  41.4 0.0 collective-permute-done.6.rest_2_
  41.4 0.0 collective-permute-done.7.rest_3_
  41.4 0.6 %collective-permute-done.3.other_ref = f32[64,64]{1,0:T(8,128)S(1)} collective-permute-done((f32[64,64]{1,0:T(8,128)S(1)}, f32[64,64]{1,0:T(8,128)S(1)}, u32[]{:S(2)}, u32[]{:S(2)}) %collective-permute-start.3) | collective-permute-done | bytes 16416 | tf_op jit(solution)/shard_map/ppermute | solution.py:336
  42.0 1.3 %score.1 = f32[2,64]{1,0:T(2,128)} custom-call(f32[64,64]{1,0:T(8,128)S(1)} %collective-permute-done.3.other_ref, f32[64,128]{1,0:T(8,128)S(1)} %solve.1.left_ref, bf16[16,4096]{1,0:T(8,128)(2,1)S(1)} %constant_dynamic-update-slice_fusion.rest_0_, bf16[16,4096]{1,0:T(8,128)(2,1)S(1)} %collective-permute-done.5.rest_1_, ...), custom_call_target="tpu_custom_call" | custom-call | tf_op jit(solution)/shard_map/score/pallas_call | solution.py:438
  (4 shorter events, 0.1 us)
Async XLA Ops:
  1.6 21.7 %all-to-all-start = ((bf16[8,128,256]{2,1,0:T(8,128)(2,1)}), bf16[8,128,256]{2,1,0:T(8,128)(2,1)S(1)}, u32[]{:S(2)}, u32[]{:S(2)}) async-start(bf16[8,128,256]{2,1,0:T(8,128)(2,1)} %broadcast_in_dim.4), calls=%async_computation | async-start | bytes 1048576 | tf_op jit(solution)/shard_map/all_to_all | solution.py:342
  8.9 1.6 %copy-start.2 = (bf16[2,2,64,4096]{3,2,1,0:T(8,128)(2,1)S(1)}, bf16[2,2,64,4096]{3,2,1,0:T(8,128)(2,1)}, u32[]{:S(2)}) copy-start(bf16[2,2,64,4096]{3,2,1,0:T(8,128)(2,1)} %param.6) | copy-start | bytes 6291460
  10.5 1.6 %copy-start.3 = (bf16[2,2,64,4096]{3,2,1,0:T(8,128)(2,1)S(1)}, bf16[2,2,64,4096]{3,2,1,0:T(8,128)(2,1)}, u32[]{:S(2)}) copy-start(bf16[2,2,64,4096]{3,2,1,0:T(8,128)(2,1)} %param.7) | copy-start | bytes 6291460
  12.0 0.8 %copy-start.4 = (bf16[4,4096]{1,0:T(4,128)(2,1)S(1)}, bf16[4,4096]{1,0:T(4,128)(2,1)}, u32[]{:S(2)}) copy-start(bf16[4,4096]{1,0:T(4,128)(2,1)} %evals_ref.1) | copy-start | bytes 98308
  12.8 0.7 %copy-start.5 = (s32[2,2]{1,0:T(2,128)S(1)}, s32[2,2]{1,0:T(2,128)}, u32[]{:S(2)}) copy-start(s32[2,2]{1,0:T(2,128)} %lengths_ref.1) | copy-start | bytes 52
  14.4 1.3 %copy-start = (bf16[256,4096]{1,0:T(8,128)(2,1)}, bf16[256,4096]{1,0:T(8,128)(2,1)S(1)}, u32[]{:S(2)}) copy-start(bf16[256,4096]{1,0:T(8,128)(2,1)S(1)} %get-tuple-element.19.x_ref.grad_ref) | copy-start | bytes 6291460
  15.7 4.3 %collective-permute-start = (bf16[4,4096]{1,0:T(4,128)(2,1)S(1)}, bf16[4,4096]{1,0:T(4,128)(2,1)S(1)}, u32[]{:S(2)}, u32[]{:S(2)}) collective-permute-start(bf16[4,4096]{1,0:T(4,128)(2,1)S(1)} %get-tuple-element.20), channel_id=1, source_target_pairs={{0,4},{1,5},{2,6},{3,7},{4,0},{5,1},{6,2},{7,3},{8,12},{9,13},{10,... | collective-permute-start | bytes 98312 | tf_op jit(solution)/shard_map/ppermute | solution.py:336
  23.4 1.6 %copy-start.1 = (bf16[256,4096]{1,0:T(8,128)(2,1)S(1)}, bf16[256,4096]{1,0:T(8,128)(2,1)}, u32[]{:S(2)}) copy-start(bf16[256,4096]{1,0:T(8,128)(2,1)} %copy-done) | copy-start | bytes 6291460
  23.4 2.0 %collective-permute-start.1 = (bf16[8,128,256]{2,1,0:T(8,128)(2,1)S(1)}, bf16[8,128,256]{2,1,0:T(8,128)(2,1)S(1)}, u32[]{:S(2)}, u32[]{:S(2)}) collective-permute-start(bf16[8,128,256]{2,1,0:T(8,128)(2,1)S(1)} %all-to-all-done.own_ref), channel_id=1, source_target_pairs={{0,1},{1,0},{2,3},{3,2},{4,5},{5,4},{6,7},{7,6},{8,9},{9,8},{10,11... | collective-permute-start | bytes 1572872 | tf_op jit(solution)/shard_map/ppermute | solution.py:336
  23.4 8.6 %collective-permute-start.4 = (bf16[8,4096]{1,0:T(8,128)(2,1)S(1)}, bf16[8,4096]{1,0:T(8,128)(2,1)S(1)}, u32[]{:S(2)}, u32[]{:S(2)}) collective-permute-start(bf16[8,4096]{1,0:T(8,128)(2,1)S(1)} %pad_maximum_fusion), channel_id=1, source_target_pairs={{0,8},{1,9},{2,10},{3,11},{4,12},{5,13},{6,14},{7,15},{8,0},{9,1},... | collective-permute-start | bytes 196616 | tf_op jit(solution)/shard_map/ppermute | solution.py:336
  26.1 1.2 %collective-permute-start.2 = (f32[24,128]{1,0:T(8,128)S(1)}, f32[24,128]{1,0:T(8,128)S(1)}, u32[]{:S(2)}, u32[]{:S(2)}) collective-permute-start(f32[24,128]{1,0:T(8,128)S(1)} %get-tuple-element.23), channel_id=1, source_target_pairs={{0,1},{1,0},{2,3},{3,2},{4,5},{5,4},{6,7},{7,6},{8,9},{9,8},{10,11... | collective-permute-start | bytes 36872 | tf_op jit(solution)/shard_map/ppermute | solution.py:336
  28.0 11.1 %all-to-all-start.1 = ((f32[8,24,128]{2,1,0:T(8,128)}), f32[8,24,128]{2,1,0:T(8,128)S(1)}, u32[]{:S(2)}, u32[]{:S(2)}) async-start(f32[8,24,128]{2,1,0:T(8,128)} %broadcast_in_dim.5), calls=%async_computation.1 | async-start | bytes 196608 | tf_op jit(solution)/shard_map/all_to_all | solution.py:342
  32.0 6.5 %collective-permute-start.5 = (bf16[16,4096]{1,0:T(8,128)(2,1)S(1)}, bf16[16,4096]{1,0:T(8,128)(2,1)S(1)}, u32[]{:S(2)}, u32[]{:S(2)}) collective-permute-start(bf16[16,4096]{1,0:T(8,128)(2,1)S(1)} %constant_dynamic-update-slice_fusion.rest_0_), channel_id=1, source_target_pairs={{0,2},{1,3},{2,0},{3,1},{4,6},{5,7},{6,4},{7,5},{8,10},{9,11},{10,... | collective-permute-start | bytes 393224 | tf_op jit(solution)/shard_map/ppermute | solution.py:336
  34.0 7.4 %collective-permute-start.6 = (bf16[16,4096]{1,0:T(8,128)(2,1)S(1)}, bf16[16,4096]{1,0:T(8,128)(2,1)S(1)}, u32[]{:S(2)}, u32[]{:S(2)}) collective-permute-start(bf16[16,4096]{1,0:T(8,128)(2,1)S(1)} %constant_dynamic-update-slice_fusion.rest_0_), channel_id=1, source_target_pairs={{0,1},{1,0},{2,3},{3,2},{4,5},{5,4},{6,7},{7,6},{8,9},{9,8},{10,11... | collective-permute-start | bytes 393224 | tf_op jit(solution)/shard_map/ppermute | solution.py:336
  38.4 3.0 %collective-permute-start.7 = (bf16[16,4096]{1,0:T(8,128)(2,1)S(1)}, bf16[16,4096]{1,0:T(8,128)(2,1)S(1)}, u32[]{:S(2)}, u32[]{:S(2)}) collective-permute-start(bf16[16,4096]{1,0:T(8,128)(2,1)S(1)} %collective-permute-done.5.rest_1_), channel_id=1, source_target_pairs={{0,1},{1,0},{2,3},{3,2},{4,5},{5,4},{6,7},{7,6},{8,9},{9,8},{10,11... | collective-permute-start | bytes 393224 | tf_op jit(solution)/shard_map/ppermute | solution.py:336
  40.8 1.2 %collective-permute-start.3 = (f32[64,64]{1,0:T(8,128)S(1)}, f32[64,64]{1,0:T(8,128)S(1)}, u32[]{:S(2)}, u32[]{:S(2)}) collective-permute-start(f32[64,64]{1,0:T(8,128)S(1)} %invert.1.inverse_ref), channel_id=1, source_target_pairs={{0,1},{1,0},{2,3},{3,2},{4,5},{5,4},{6,7},{7,6},{8,9},{9,8},{10,11... | collective-permute-start | bytes 49160 | tf_op jit(solution)/shard_map/ppermute | solution.py:336
